TPU v7x, 128 devices: a whole 4x4x4 slice. The times are simulated.
128 devices in a mesh: site: 8 (over y, core), op: 16 (over x, z).
Axes of the slice: x: 4, y: 4, z: 4, core: 2. Of those that a mesh axis runs over, the one named last changes fastest.
Arguments:
- psi: bfloat16 [8, 16, 256, 256], P('site'), may hold values from -16 to 16
- diagonal: float32 [8, 16, 256, 256], P('site'), may hold values from 1 to 32
- left_step: float32 [8, 256, 256], P('site'), may hold values from -0.375 to 0.375
- right_step: float32 [8, 256, 256], P('site'), may hold values from -0.375 to 0.375
- left_env: bfloat16 [64, 256, 256], P('op'), may hold values from -1.125 to 1.125
- right_env: bfloat16 [64, 256, 256], P('op'), may hold values from -1.125 to 1.125
- src_block: int32 [64], P('op'), may hold values from 0 to 15
- dst_block: int32 [64], P('op'), may hold values from 0 to 15
Outputs:
- ground: float32 [8, 16, 256, 256], P('site', 'op')
All inputs are finite; a program needn't handle non-finite values.
Results may differ from a plain program's by a relative error of at most 0.0078.
Values may be sent and summed in bfloat16 or wider, within the bound.
No kernel may reach another device: no remote copies, remote signals or barrier semaphores. Data moves between devices by JAX's collectives and lax.ppermute only.
A program may use at most 128 MiB of HBM per device.

v0:
```python
import jax
import jax.numpy as jnp
from jax import lax
from jax.sharding import PartitionSpec as P

ITERS = 2


HIGH = lax.Precision.HIGHEST


def carried_in(value, axis, join, neutral, backward):
    count, mine = (lax.axis_size(axis), lax.axis_index(axis))
    pieces = lax.all_gather(value, axis)
    if backward:
        pieces = pieces[::-1]
        mine = count - 1 - mine
    subtotal = jnp.full_like(value, 0) + jnp.asarray(neutral, value.dtype)

    def lap(position, subtotal):
        longer = join(subtotal, pieces[position])
        return jnp.where(position < mine, longer, subtotal)

    return lax.fori_loop(0, count - 1, lap, subtotal)


def term_parts(full_b, lenv, renv, src_block, dst_block):
    forward = jnp.einsum(
        "tij,tjk->tik", full_b[src_block], renv, preferred_element_type=jnp.float32
    ).astype(jnp.bfloat16)
    backward = jnp.einsum(
        "tij,tkj->tik", full_b[dst_block], renv, preferred_element_type=jnp.float32
    ).astype(jnp.bfloat16)
    first = jnp.einsum("tij,tjk->tik", lenv, forward, preferred_element_type=jnp.float32)
    second = jnp.einsum("tji,tjk->tik", lenv, backward, preferred_element_type=jnp.float32)
    return (first, second)


def collect(first, second, src_block, dst_block, begin, count):
    dst_local = dst_block - begin
    src_local = src_block - begin
    dst_ids = jnp.where((dst_local >= 0) & (dst_local < count), dst_local, count)
    src_ids = jnp.where((src_local >= 0) & (src_local < count), src_local, count)
    total = jax.ops.segment_sum(first, dst_ids, count + 1)[:count]
    return total + jax.ops.segment_sum(second, src_ids, count + 1)[:count]


def body(psi, diagonal, left_step, right_step, left_env, right_env, src_block, dst_block):
    blk = psi.shape[-1]
    nblocks = psi.shape[1]
    eye = jnp.eye(blk, dtype=jnp.float32)
    step_l = eye + 0.3 * left_step[0]
    step_r = eye + 0.3 * right_step[0]
    left_prod = carried_in(
        step_l, "site", lambda early, late: jnp.dot(early, late, precision=HIGH), eye, False
    )
    right_prod = carried_in(
        step_r, "site", lambda early, late: jnp.dot(late, early, precision=HIGH), eye, True
    )
    left_q = left_prod.astype(jnp.bfloat16)
    right_q = right_prod.astype(jnp.bfloat16)
    ltemp = jnp.einsum("tij,jk->tik", left_env, left_q, preferred_element_type=jnp.float32).astype(
        jnp.bfloat16
    )
    lenv = jnp.einsum("ji,tjk->tik", left_q, ltemp, preferred_element_type=jnp.float32).astype(
        jnp.bfloat16
    )
    rtemp = jnp.einsum(
        "tij,kj->tik", right_env, right_q, preferred_element_type=jnp.float32
    ).astype(jnp.bfloat16)
    renv = jnp.einsum("ij,tjk->tik", right_q, rtemp, preferred_element_type=jnp.float32).astype(
        jnp.bfloat16
    )
    start_vec = psi[0].astype(jnp.float32)
    x_full = start_vec / jnp.sqrt(jnp.sum(start_vec * start_vec) + 1e-12)
    diag = diagonal[0]
    x = x_full

    def apply_ham(full_b, vec):
        first, second = term_parts(full_b, lenv, renv, src_block, dst_block)
        summed = lax.psum(collect(first, second, src_block, dst_block, 0, nblocks), "op")
        return diag * vec + summed

    def inner_one(left, right):
        return jnp.sum(left * right)

    h = apply_ham(x_full.astype(jnp.bfloat16), x)
    for step in range(ITERS):
        theta = inner_one(x, h)
        t = (h - theta * x) / diag
        t = t - inner_one(x, t) * x
        t = t / jnp.sqrt(inner_one(t, t) + 1e-12)
        g = apply_ham(t.astype(jnp.bfloat16), t)
        cross = jnp.sum(x * g)
        curve = jnp.sum(t * g)
        lowered = (curve - theta) / 2 + jnp.sqrt(((theta - curve) / 2) ** 2 + cross * cross)
        norm_pair = jnp.sqrt(lowered * lowered + cross * cross)
        keep = lowered / norm_pair
        move = cross / norm_pair
        x = keep * x - move * t
        h = keep * h - move * g
    scaled = x * jnp.sqrt(jnp.float32(nblocks * blk * blk))
    owned_rows = nblocks // lax.axis_size("op")
    scaled = lax.dynamic_slice_in_dim(scaled, lax.axis_index("op") * owned_rows, owned_rows, 0)
    return scaled[None]


def solution(mesh):
    placed = (
        P("site", None, None, None),
        P("site", None, None, None),
        P("site", None, None),
        P("site", None, None),
        P("op", None, None),
        P("op", None, None),
        P("op"),
        P("op"),
    )
    return jax.shard_map(
        body, mesh=mesh, in_specs=placed, out_specs=P("site", "op", None, None), check_vma=False
    )
```

profile of v0, /device:TPU:0, one launch (start us, length us, event | category | flops | bytes accessed | tf_op | source)
XLA Modules:
  0.0 541.5 jit_solution(7223183171309892968)
XLA Ops:
  10.4 3.3 fusion.7
  22.3 14.4 %all-gather.5.cloned.1.call-done = f32[8,256,256]{2,1,0:T(8,128)} async-done(((f32[1,256,256]{2,1,0:T(8,128)}), f32[8,256,256]{2,1,0:T(8,128)}) %all-gather.5.cloned.1.call-update) | async-done | bytes 2097168 | tf_op jit(solution)/shard_map/all_gather | solution.py:14
  39.8 9.7 %while.27 = (s32[]{:T(128)}, f32[256,256]{1,0:T(8,128)S(1)}, s32[]{:T(128)}, f32[8,256,256]{2,1,0:T(8,128)}, s32[]{:T(128)}) while((s32[]{:T(128)}, f32[256,256]{1,0:T(8,128)S(1)}, s32[]{:T(128)}, f32[8,256,256]{2,1,0:T(8,128)}, s32[]{:T(128)}) %tuple.67), condition=%wide.region_4.5_spmd, body=%wide.region_3.4_spmd.sunk | while | flops 201392128 | bytes 1573447 | solution.py:24
  49.5 14.4 %all-gather.3.cloned.1.call-done = f32[8,256,256]{2,1,0:T(8,128)} async-done(((f32[1,256,256]{2,1,0:T(8,128)}), f32[8,256,256]{2,1,0:T(8,128)}) %all-gather.3.cloned.1.call-update) | async-done | bytes 2097168 | tf_op jit(solution)/shard_map/all_gather | solution.py:14
  64.0 11.2 %while.26 = (s32[]{:T(128)}, f32[256,256]{0,1:T(8,128)S(1)}, s32[]{:T(128)}, f32[8,256,256]{2,1,0:T(8,128)}, s32[]{:T(128)}) while((s32[]{:T(128)}, f32[256,256]{0,1:T(8,128)S(1)}, s32[]{:T(128)}, f32[8,256,256]{2,1,0:T(8,128)}, s32[]{:T(128)}) %tuple.64), condition=%wide.region_2.3_spmd, body=%wide.region_1.2_spmd.sunk | while | flops 201392128 | bytes 1573447 | solution.py:24
  85.9 3.5 scatter_fusion
  91.9 3.5 scatter_fusion.1
  95.4 6.0 %slice_add_fusion.2 = f32[16,256,256]{2,1,0:T(8,128)} fusion(f32[17,256,256]{2,1,0:T(8,128)} %scatter_fusion.1, f32[17,256,256]{2,1,0:T(8,128)} %scatter_fusion), kind=kLoop, calls=%fused_computation.27 | loop fusion | flops 1048576 | bytes 12582912 | tf_op jit(solution)/shard_map/add | solution.py:45
  101.7 103.7 %all-reduce.4.cloned.1.call-done = f32[16,256,256]{2,1,0:T(8,128)} async-done(((f32[16,256,256]{2,1,0:T(8,128)}), f32[16,256,256]{2,1,0:T(8,128)}) %all-reduce.4.cloned.1.call-update) | async-done | bytes 4194320 | tf_op jit(solution)/shard_map/psum | solution.py:81
  205.4 5.3 multiply_reduce_fusion.9
  214.1 5.0 multiply_reduce_fusion.7
  219.7 4.0 fusion.32
  237.3 3.5 scatter_fusion.2
  243.3 3.5 scatter_fusion.3
  246.9 6.1 %slice_add_fusion.1 = f32[16,256,256]{2,1,0:T(8,128)} fusion(f32[17,256,256]{2,1,0:T(8,128)} %scatter_fusion.3, f32[17,256,256]{2,1,0:T(8,128)} %scatter_fusion.2), kind=kLoop, calls=%fused_computation.26 | loop fusion | flops 1048576 | bytes 12582912 | tf_op jit(solution)/shard_map/add | solution.py:45
  253.2 103.0 %all-reduce.6.cloned.1.call-done = f32[16,256,256]{2,1,0:T(8,128)} async-done(((f32[16,256,256]{2,1,0:T(8,128)}), f32[16,256,256]{2,1,0:T(8,128)}) %all-reduce.6.cloned.1.call-update) | async-done | bytes 4194320 | tf_op jit(solution)/shard_map/psum | solution.py:81
  356.2 7.5 %multiply_reduce_fusion.6 = (f32[]{:T(128)}, f32[]{:T(128)}, f32[16,256,256]{2,1,0:T(8,128)}) fusion(f32[16,256,256]{2,1,0:T(8,128)} %get-tuple-element.201, f32[]{:T(128)S(6)} %sqrt.22, f32[]{:T(128)S(6)} %sqrt.21, bf16[1,16,256,256]{3,2,1,0:T(8,128)(2,1)S(1)} %copy-done.4, f32[16,256,256]{2,1,0:T(8,128)} %all-reduce.6.cloned.1.call-done, ...), kind=kLoop, calls=%fused_computation.45 | loop fusion | flops 9437182 | bytes 18874384 | tf_op jit(solution)/shard_map/reduce_sum | solution.py:95
  368.2 7.5 %multiply_reduce_fusion.4 = (f32[]{:T(128)}, f32[16,256,256]{2,1,0:T(8,128)S(1)}) fusion(f32[16,256,256]{2,1,0:T(8,128)} %get-tuple-element.199, f32[]{:T(128)S(6)} %div.55, f32[]{:T(128)S(6)} %div.54, f32[16,256,256]{2,1,0:T(8,128)} %all-reduce.4.cloned.1.call-done, f32[1,16,256,256]{3,2,1,0:T(8,128)} %param.13, f32[]{:T(128)S(6)} %sqrt.21, ...), kind=kLoop, calls=%fused_computation.41 | loop fusion | flops 13631487 | bytes 23068692 | tf_op jit(solution)/shard_map/reduce_sum | solution.py:85
  379.2 3.3 multiply_reduce_fusion.3
  387.4 6.9 %fusion.34 = (bf16[16,256,256]{2,1,0:T(8,128)(2,1)S(1)}, f32[16,256,256]{2,1,0:T(8,128)}) fusion(f32[]{:T(128)S(6)} %sqrt.25, f32[16,256,256]{2,1,0:T(8,128)} %copy-done.9, f32[16,256,256]{2,1,0:T(8,128)} %copy-done.5, f32[]{:T(128)} %get-tuple-element.195), kind=kLoop, calls=%fused_computation.92 | loop fusion | flops 4194304 | bytes 14680072 | tf_op jit(solution)/shard_map/convert_element_type | solution.py:93
  402.7 3.2 scatter_fusion.4
  411.5 6.1 %slice_add_fusion = f32[16,256,256]{2,1,0:T(8,128)} fusion(f32[17,256,256]{2,1,0:T(8,128)} %scatter_fusion.5, f32[17,256,256]{2,1,0:T(8,128)} %scatter_fusion.4), kind=kLoop, calls=%fused_computation.25 | loop fusion | flops 1048576 | bytes 12582912 | tf_op jit(solution)/shard_map/add | solution.py:45
  417.6 103.3 %all-reduce.8.cloned.1.call-done = f32[16,256,256]{2,1,0:T(8,128)} async-done(((f32[16,256,256]{2,1,0:T(8,128)}), f32[16,256,256]{2,1,0:T(8,128)}) %all-reduce.8.cloned.1.call-update) | async-done | bytes 4194320 | tf_op jit(solution)/shard_map/psum | solution.py:81
  520.9 7.8 %multiply_reduce_fusion.1 = (f32[]{:T(128)}, f32[]{:T(128)}) fusion(f32[16,256,256]{2,1,0:T(8,128)} %get-tuple-element.194, f32[16,256,256]{2,1,0:T(8,128)} %all-reduce.8.cloned.1.call-done, f32[1,16,256,256]{3,2,1,0:T(8,128)} %param.13, f32[16,256,256]{2,1,0:T(8,128)} %copy-done.5), kind=kLoop, calls=%fused_computation.37 | loop fusion | flops 6291454 | bytes 16777224 | tf_op jit(solution)/shard_map/reduce_sum | solution.py:95
  (97 shorter events, 92.0 us)
Async XLA Ops:
  6.5 69.4 %copy-start = (bf16[4,256,256]{2,1,0:T(8,128)(2,1)S(1)}, bf16[4,256,256]{2,1,0:T(8,128)(2,1)}, u32[]{:S(2)}) copy-start(bf16[4,256,256]{2,1,0:T(8,128)(2,1)} %param.17) | copy-start | bytes 1572868
  6.5 8.0 %copy-start.4 = (bf16[1,16,256,256]{3,2,1,0:T(8,128)(2,1)S(1)}, bf16[1,16,256,256]{3,2,1,0:T(8,128)(2,1)}, u32[]{:S(2)}) copy-start(bf16[1,16,256,256]{3,2,1,0:T(8,128)(2,1)} %param.12) | copy-start | bytes 6291460
  6.5 8.0 %copy-start.11 = (s32[4]{0:T(128)S(1)}, s32[4]{0:T(128)}, u32[]{:S(2)}) copy-start(s32[4]{0:T(128)} %param.18) | copy-start | bytes 52
  6.5 8.0 %copy-start.12 = (s32[4]{0:T(128)S(1)}, s32[4]{0:T(128)}, u32[]{:S(2)}) copy-start(s32[4]{0:T(128)} %param.19) | copy-start | bytes 52
  6.5 30.2 %all-gather.5.cloned.1.call-start = ((), (), s32[]{:S(2)}) async-start(), calls=%async_computation.1 | async-start | bytes 2359296 | tf_op jit(solution)/shard_map/all_gather | solution.py:14
  8.4 55.5 %all-gather.3.cloned.1.call-start = ((), (), s32[]{:S(2)}) async-start(), calls=%async_computation | async-start | bytes 2359296 | tf_op jit(solution)/shard_map/all_gather | solution.py:14
  10.2 195.2 %all-reduce.4.cloned.1.call-start = ((), (), s32[]{:S(2)}) async-start(), calls=%async_computation.2 | async-start | bytes 8388608 | tf_op jit(solution)/shard_map/psum | solution.py:81
  75.2 0.7 copy-start.10
  101.5 254.7 %all-reduce.6.cloned.1.call-start = ((), (), s32[]{:S(2)}) async-start(), calls=%async_computation.3 | async-start | bytes 8388608 | tf_op jit(solution)/shard_map/psum | solution.py:81
  205.4 5.3 copy-start.2
  205.4 5.9 %copy-start.6 = (f32[16,256,256]{2,1,0:T(8,128)S(1)}, f32[16,256,256]{2,1,0:T(8,128)}, u32[]{:S(2)}) copy-start(f32[16,256,256]{2,1,0:T(8,128)} %all-reduce.4.cloned.1.call-done) | copy-start | bytes 12582916
  252.9 268.0 %all-reduce.8.cloned.1.call-start = ((), (), s32[]{:S(2)}) async-start(), calls=%async_computation.4 | async-start | bytes 8388608 | tf_op jit(solution)/shard_map/psum | solution.py:81
  368.2 7.6 %copy-start.3 = (f32[1,16,256,256]{3,2,1,0:T(8,128)S(1)}, f32[1,16,256,256]{3,2,1,0:T(8,128)}, u32[]{:S(2)}) copy-start(f32[1,16,256,256]{3,2,1,0:T(8,128)} %param.13) | copy-start | bytes 12582916
  368.2 8.3 %copy-start.7 = (f32[16,256,256]{2,1,0:T(8,128)S(1)}, f32[16,256,256]{2,1,0:T(8,128)}, u32[]{:S(2)}) copy-start(f32[16,256,256]{2,1,0:T(8,128)} %all-reduce.4.cloned.1.call-done) | copy-start | bytes 12582916
  368.2 11.0 %copy-start.8 = (f32[16,256,256]{2,1,0:T(8,128)S(1)}, f32[16,256,256]{2,1,0:T(8,128)}, u32[]{:S(2)}) copy-start(f32[16,256,256]{2,1,0:T(8,128)} %get-tuple-element.199) | copy-start | bytes 12582916
  375.7 6.7 %copy-start.5 = (f32[16,256,256]{2,1,0:T(8,128)}, f32[16,256,256]{2,1,0:T(8,128)S(1)}, u32[]{:S(2)}) copy-start(f32[16,256,256]{2,1,0:T(8,128)S(1)} %get-tuple-element.198) | copy-start | bytes 12582916
  382.5 1.9 copy-start.9
  520.9 14.1 %copy-start.1 = (bf16[4,256,256]{2,1,0:T(8,128)(2,1)S(1)}, bf16[4,256,256]{2,1,0:T(8,128)(2,1)}, u32[]{:S(2)}) copy-start(bf16[4,256,256]{2,1,0:T(8,128)(2,1)} %param.17) | copy-start | bytes 1572868
Sparse Core Ops, SparseCore 0:
  9.1 27.6 all-gather.4
  38.5 25.4 all-gather.2
  101.6 103.7 all-reduce.3
  253.1 103.0 all-reduce.5
  417.7 103.1 all-reduce.7
where the time goes:
time: 544 us; the launch traced here: 542 us
  waiting for transfers between devices  339 us (62%)
  other arithmetic  101 us (19%)
  local copies, waits for them, and re-layouts  40 us (7%)
  matrix products  35.9 us (7%)
  between operations  24.2 us (4%)
    psum x3, waiting for transfers between devices, apply_ham(): lax.psum(collect(first, second, src_block, dst_block, 0, nblocks), 'op')  310 us
    all_gather x2, waiting for transfers between devices, carried_in(): pieces = lax.all_gather(value, axis)  28.8 us
    reduce_sum x6, other arithmetic, inner_one(): return jnp.sum(left * right)  26.3 us
    add x3, other arithmetic, collect(): return total + jax.ops.segment_sum(second, src_ids, count + 1)[:count]  18.1 us
    reduce_sum x2, other arithmetic, body(): curve = jnp.sum(t * g)  15.4 us
    another operation x6, local copies, waits for them, and re-layouts  15.1 us
    dot_general x7, matrix products, body(): jnp.dot(early, late, precision=HIGH)  10.9 us
  transfers between devices with their start and end apart: 5, of which 5 were waited for; matrix products, arithmetic and copies ran while one was open for 5% of the time, Pallas kernels for 0%

commit v1 on v0

v1 whole, which is shorter than its diff:
```python
import jax
import jax.numpy as jnp
from jax import lax
from jax.experimental import pallas as pl
from jax.experimental.pallas import tpu as pltpu
from jax.sharding import PartitionSpec as P

ITERS = 2
BLK = 256
NB = 16
BF16 = jnp.bfloat16
F32 = jnp.float32
HIGH = lax.Precision.HIGHEST
MIB = 1 << 20

XA, XB, ZA, ZB = (1, 0), (3, 0), (0, 1), (0, 3)
ORDERS = ((XA, ZA, XB, ZB), (ZA, XB, ZB, XA), (XB, ZB, XA, ZA), (ZB, XA, ZA, XB))


def swap_op(value, mask):
    mx, mz = mask
    pairs = [
        (x * 4 + z, (x ^ mx) * 4 + (z ^ mz)) for x in range(4) for z in range(4)
    ]
    return lax.ppermute(value, "op", pairs)


def swap_core(value):
    return lax.ppermute(value, "site", [(i, i ^ 1) for i in range(8)])


def dot(a, b):
    return jnp.dot(a, b, preferred_element_type=F32)


def dot_nt(a, b):
    return lax.dot_general(a, b, (((1,), (1,)), ((), ())), preferred_element_type=F32)


def dot_tn(a, b):
    return lax.dot_general(a, b, (((0,), (0,)), ((), ())), preferred_element_type=F32)


def dot_high(a, b):
    return jnp.dot(a, b, precision=HIGH, preferred_element_type=F32)


def identity():
    rows = lax.broadcasted_iota(jnp.int32, (BLK, BLK), 0)
    cols = lax.broadcasted_iota(jnp.int32, (BLK, BLK), 1)
    return jnp.where(rows == cols, 1.0, 0.0).astype(F32)


def pair_kernel(site_ref, own_ref, other_ref, out_ref):
    eye = identity()
    core = site_ref[0] % 2

    @pl.when(core == 0)
    def _():
        out_ref[...] = dot_high(eye + 0.3 * own_ref[0], eye + 0.3 * other_ref[0])

    @pl.when(core == 1)
    def _():
        out_ref[...] = dot_high(eye + 0.3 * other_ref[1], eye + 0.3 * own_ref[1])


def pair_product(site, own, other):
    vmem = pl.BlockSpec(memory_space=pltpu.VMEM)
    return pl.pallas_call(
        pair_kernel,
        out_shape=jax.ShapeDtypeStruct((BLK, BLK), F32),
        in_specs=[pl.BlockSpec(memory_space=pltpu.SMEM), vmem, vmem],
        out_specs=vmem,
        cost_estimate=pl.CostEstimate(flops=12 * BLK**3, bytes_accessed=MIB, transcendentals=0),
    )(site, own, other)


def chain_kernel(site_ref, other_ref, m1, m2, m3, n1, n2, n3, lq_ref, rq_ref):
    eye = identity()
    site = site_ref[0]
    core, y = site % 2, site // 2

    def chain(left, right):
        lefts = [jnp.where(y >= k + 1, left[k][...], eye) for k in range(3)]
        rights = [jnp.where(y + k + 1 <= 3, right[k][...], eye) for k in range(3)]
        s_part = jnp.where(core == 1, eye + 0.3 * other_ref[0], eye)
        t_part = jnp.where(core == 0, eye + 0.3 * other_ref[1], eye)
        a = dot_high(lefts[2], lefts[1])
        b = dot_high(lefts[0], s_part)
        c = dot_high(t_part, rights[0])
        d = dot_high(rights[1], rights[2])
        lq_ref[...] = dot_high(a, b).astype(BF16)
        rq_ref[...] = dot_high(c, d).astype(BF16)

    @pl.when(core == 0)
    def _():
        chain((m1, m2, m3), (n1, n2, n3))

    @pl.when(core == 1)
    def _():
        chain((n1, n2, n3), (m1, m2, m3))


def chain_products(site, other, received, across):
    vmem = pl.BlockSpec(memory_space=pltpu.VMEM)
    out = jax.ShapeDtypeStruct((BLK, BLK), BF16)
    return pl.pallas_call(
        chain_kernel,
        out_shape=(out, out),
        in_specs=[pl.BlockSpec(memory_space=pltpu.SMEM)] + [vmem] * 7,
        out_specs=(vmem, vmem),
        cost_estimate=pl.CostEstimate(flops=72 * BLK**3, bytes_accessed=2 * MIB, transcendentals=0),
    )(site, other, *received, *across)


def transfers(site, left_step, right_step):
    own = jnp.concatenate([left_step, right_step], 0)
    other = swap_core(own)
    mine = pair_product(site, own, other)
    received = []
    for k in (1, 2, 3):
        pairs = [(2 * y, 2 * (y + k)) for y in range(4 - k)]
        pairs += [(2 * y + 1, 2 * (y - k) + 1) for y in range(k, 4)]
        received.append(lax.ppermute(mine, "site", pairs))
    across = [swap_core(r) for r in received]
    return chain_products(site, other, received, across)


def gather_terms(parts):
    held = [p[None] for p in parts]
    for stage in range(3):
        got = [swap_op(h, order[stage]) for h, order in zip(held, ORDERS)]
        held = [jnp.concatenate(pair, 0) for pair in zip(held, got)]
    last = [swap_op(h, order[3]) for h, order in zip(held, ORDERS)]
    return held, last, [swap_core(h) for h in held], [swap_core(h) for h in last]


def term_slots(k, place):
    pick, t, j = k // 32, (k // 16) % 2, k % 16
    b0, b1, b2, b3 = j % 2, (j // 2) % 2, (j // 4) % 2, j // 8
    xa, xb = jnp.where(t == 0, b0, b2), jnp.where(t == 0, b2, b0)
    za, zb = jnp.where(t == 0, b1, b3), jnp.where(t == 0, b3, b1)
    x = jnp.bitwise_xor(place[0], xa + xb * 3 - 2 * xa * xb)
    z = jnp.bitwise_xor(place[1], za + zb * 3 - 2 * za * zb)
    core = jnp.bitwise_xor(place[2], pick)
    right = k - j + j // 2 + 8 * b0
    return right, (x * 4 + z) * 4 + core * 2 + t


def fold(p):
    return jnp.sum(p.reshape(BLK // 8, 8, BLK), axis=0)


def total(acc):
    return jnp.sum(jnp.sum(acc, axis=0, keepdims=True), axis=1, keepdims=True)


def solve_kernel(ids, src_all, dst_all, lq_ref, rq_ref, psi_hbm, diag_hbm, *rest):
    groups = rest[:16]
    out_ref = rest[16]
    lbuf, rbuf, xv, hv, tv, gv, dv, vb, sems = rest[17:]
    site, op = ids[0], ids[1]
    place = (op // 4, op % 4, site % 2)

    copies = {}
    first = pltpu.make_async_copy(psi_hbm.at[0], vb, sems.at[16])
    first.start()
    for pick in range(2):
        for t in range(2):
            for side, buf in enumerate((lbuf, rbuf)):
                for half in range(2):
                    which = pick * 8 + half * 4 + t * 2 + side
                    begin = pick * 32 + t * 16 + half * 8
                    copy = pltpu.make_async_copy(
                        groups[which], buf.at[pl.ds(begin, 8)], sems.at[which]
                    )
                    copy.start()
                    copies.setdefault((pick, t), []).append(copy)
    second = pltpu.make_async_copy(diag_hbm.at[0], dv, sems.at[17])
    second.start()

    lq = lq_ref[...]
    lq_t = lq.T
    rq = rq_ref[...]
    rq_t = rq.T
    zero = jnp.zeros((8, BLK), F32)

    def over_blocks(step, count):
        return lax.fori_loop(0, NB, step, (zero,) * count)

    first.wait()

    def square(b, sums):
        v = vb[b].astype(F32)
        return (sums[0] + fold(v * v),)

    (norm,) = over_blocks(square, 1)
    scale = lax.rsqrt(total(norm) + 1e-12)

    def start(b, sums):
        v = vb[b].astype(F32) * scale
        xv[b] = v
        vb[b] = v.astype(BF16)
        hv[b] = jnp.zeros((BLK, BLK), F32)
        return sums

    over_blocks(start, 0)

    def term(k):
        right, which = term_slots(k, place)
        return k, right, src_all[which], dst_all[which]

    def apply_terms(terms, lefts, rights, acc):
        mids = []
        for (_, _, s, d), r in zip(terms, rights):
            mids.append((dot(vb[s], r).astype(BF16), dot_nt(vb[d], r).astype(BF16)))
        for (_, _, s, d), l, (f, b) in zip(terms, lefts, mids):
            acc[d] += dot(l, f)
            acc[s] += dot_tn(l, b)

    unroll = 4
    for pick in range(2):
        for t in range(2):
            for copy in copies[(pick, t)]:
                copy.wait()
            base = pick * 32 + t * 16

            def build(i, carry):
                terms = [term(base + i * unroll + u) for u in range(unroll)]
                temps = [
                    (dot(lbuf[k], lq).astype(BF16), dot(rbuf[r], rq_t).astype(BF16))
                    for k, r, _, _ in terms
                ]
                lefts = [dot(lq_t, lt).astype(BF16) for lt, _ in temps]
                rights = [dot(rq, rt).astype(BF16) for _, rt in temps]
                for (k, r, _, _), l, g in zip(terms, lefts, rights):
                    lbuf[k] = l
                    rbuf[r] = g
                apply_terms(terms, lefts, rights, hv)
                return carry

            lax.fori_loop(0, 16 // unroll, build, 0)

    second.wait()

    def finish_h(b, sums):
        x = xv[b]
        h = hv[b] + dv[b] * x
        hv[b] = h
        return (sums[0] + fold(x * h),)

    (theta_sum,) = over_blocks(finish_h, 1)
    theta = total(theta_sum)

    def correction(theta):
        def residual(b, sums):
            x = xv[b]
            t = (hv[b] - theta * x) / dv[b]
            tv[b] = t
            return (sums[0] + fold(x * t),)

        (along,) = over_blocks(residual, 1)
        along = total(along)

        def orthogonal(b, sums):
            t = tv[b] - along * xv[b]
            tv[b] = t
            return (sums[0] + fold(t * t),)

        (size,) = over_blocks(orthogonal, 1)
        return lax.rsqrt(total(size) + 1e-12)

    def rotation(theta, b, c):
        low = (c - theta) / 2 + jnp.sqrt(((theta - c) / 2) ** 2 + b * b)
        inv = 1.0 / jnp.sqrt(low * low + b * b)
        return low * inv, b * inv

    for step in range(ITERS - 1):
        scale_t = correction(theta)

        def unit(b, sums):
            t = tv[b] * scale_t
            tv[b] = t
            vb[b] = t.astype(BF16)
            gv[b] = dv[b] * t
            return sums

        over_blocks(unit, 0)

        def apply_step(i, carry):
            terms = [term(i * unroll + u) for u in range(unroll)]
            lefts = [lbuf[k] for k, _, _, _ in terms]
            rights = [rbuf[r] for _, r, _, _ in terms]
            apply_terms(terms, lefts, rights, gv)
            return carry

        lax.fori_loop(0, 64 // unroll, apply_step, 0)

        def couplings(b, sums):
            g = gv[b]
            return (sums[0] + fold(xv[b] * g), sums[1] + fold(tv[b] * g))

        cross, curve = over_blocks(couplings, 2)
        keep, move = rotation(theta, total(cross), total(curve))

        def update(b, sums):
            x = keep * xv[b] - move * tv[b]
            h = keep * hv[b] - move * gv[b]
            xv[b] = x
            hv[b] = h
            return (sums[0] + fold(x * h),)

        (theta_sum,) = over_blocks(update, 1)
        theta = total(theta_sum)

    scale_t = correction(theta)

    def last_unit(b, sums):
        t = tv[b] * scale_t
        tv[b] = t
        vb[b] = t.astype(BF16)
        return (sums[0] + fold(hv[b] * t), sums[1] + fold(dv[b] * t * t))

    cross, curve_diag = over_blocks(last_unit, 2)

    def last_step(i, acc):
        terms = [term(i * unroll + u) for u in range(unroll)]
        mids = [dot(vb[s], rbuf[r]).astype(BF16) for _, r, s, _ in terms]
        for (k, _, _, d), f in zip(terms, mids):
            acc = acc + fold(tv[d] * dot(lbuf[k], f))
        return acc

    curve_terms = lax.fori_loop(0, 64 // unroll, last_step, zero)
    curve = total(curve_diag) + 2.0 * total(curve_terms)
    keep, move = rotation(theta, total(cross), curve)
    amplitude = float(NB * BLK * BLK) ** 0.5
    out_ref[0, 0] = (keep * xv[op] - move * tv[op]) * amplitude


def solve(ids, src_all, dst_all, lq, rq, psi, diagonal, groups):
    smem = pl.BlockSpec(memory_space=pltpu.SMEM)
    vmem = pl.BlockSpec(memory_space=pltpu.VMEM)
    anywhere = pl.BlockSpec(memory_space=pl.ANY)
    full = (NB, BLK, BLK)
    return pl.pallas_call(
        solve_kernel,
        out_shape=jax.ShapeDtypeStruct((1, 1, BLK, BLK), F32),
        in_specs=[smem] * 3 + [vmem] * 2 + [anywhere] * 18,
        out_specs=vmem,
        scratch_shapes=[
            pltpu.VMEM((64, BLK, BLK), BF16),
            pltpu.VMEM((64, BLK, BLK), BF16),
            pltpu.VMEM(full, F32),
            pltpu.VMEM(full, F32),
            pltpu.VMEM(full, F32),
            pltpu.VMEM(full, F32),
            pltpu.VMEM(full, F32),
            pltpu.VMEM(full, BF16),
            pltpu.SemaphoreType.DMA((18,)),
        ],
        compiler_params=pltpu.CompilerParams(vmem_limit_bytes=56 * MIB),
        cost_estimate=pl.CostEstimate(
            flops=2 * 900 * BLK**3, bytes_accessed=24 * MIB, transcendentals=0
        ),
    )(ids, src_all, dst_all, lq, rq, psi, diagonal, *groups)


def body(psi, diagonal, left_step, right_step, left_env, right_env, src_block, dst_block):
    site = lax.axis_index("site")
    op = lax.axis_index("op")
    ids = jnp.stack([site, op]).astype(jnp.int32)
    core = site % 2
    left = lax.dynamic_slice_in_dim(left_env, 2 * core, 2, 0)
    right = lax.dynamic_slice_in_dim(right_env, 2 * core, 2, 0)
    held, last, held_across, last_across = gather_terms((left[0], right[0], left[1], right[1]))
    table = lax.all_gather(jnp.stack([src_block, dst_block]), "op")
    src_all = table[:, 0].reshape(-1)
    dst_all = table[:, 1].reshape(-1)
    lq, rq = transfers(ids, left_step, right_step)
    groups = held + last + held_across + last_across
    return solve(ids, src_all, dst_all, lq, rq, psi, diagonal, groups)


def solution(mesh):
    placed = (
        P("site", None, None, None),
        P("site", None, None, None),
        P("site", None, None),
        P("site", None, None),
        P("op", None, None),
        P("op", None, None),
        P("op"),
        P("op"),
    )
    return jax.shard_map(
        body, mesh=mesh, in_specs=placed, out_specs=P("site", "op", None, None), check_vma=False
    )
```

time: 544 us -> 188 us (0.35)
  waiting for transfers between devices: 339 us -> 57.6 us
  other arithmetic: 101 us -> 6.87 us
  Pallas kernels: 0 us -> 62 us
  matrix products: 35.9 us -> 0 us
  local copies, waits for them, and re-layouts: 40 us -> 6.1 us
  starting transfers between devices: 0.6 us -> 31.7 us
  between operations: 24.2 us -> 0.6 us
  blocking collectives: 0 us -> 23 us
    psum x3 -> x0, waiting for transfers between devices: 310 us -> none  [apply_ham(): lax.psum(collect(first, second, src_block, dst_block, 0, nblocks), 'op')]
    pallas_call x0 -> x3, Pallas kernels: none -> 62 us  [the longest x1 55.6 us: solve(): pl.pallas_call(solve_kernel, out_shape=jax.ShapeDtypeStruct((1, 1, BLK, B...]
    ppermute x0 -> x31, waiting for transfers between devices: none -> 57.6 us  [the longest x16 52 us: swap_op(): return lax.ppermute(value, 'op', pairs)]
    reduce_sum x9 -> x0, other arithmetic: 45 us -> none  [the longest x6 26.3 us: inner_one(): return jnp.sum(left * right)]
    dot_general x22 -> x0, matrix products: 35.9 us -> none  [the longest x7 10.9 us: body(): jnp.dot(early, late, precision=HIGH)]
    ppermute x0 -> x31, starting transfers between devices: none -> 31.7 us  [the longest x16 21.9 us: swap_op(): return lax.ppermute(value, 'op', pairs)]
    all_gather x2 -> x0, waiting for transfers between devices: 28.8 us -> none  [carried_in(): pieces = lax.all_gather(value, axis)]
    all_gather x0 -> x1, blocking collectives: none -> 23 us  [body(): table = lax.all_gather(jnp.stack([src_block, dst_block]), 'op')]
  transfers between devices with their start and end apart: 5 -> 31, of which waited for: 5 -> 10; matrix products, arithmetic and copies ran while one was open for 5% -> 6% of each run, Pallas kernels for 0% -> 3%
where the time goes in v1:
time: 188 us
  Pallas kernels  62 us (33%)
  waiting for transfers between devices  57.6 us (31%)
  starting transfers between devices  31.7 us (17%)
  blocking collectives  23 us (12%)
  other arithmetic  6.87 us (4%)
  local copies, waits for them, and re-layouts  6.1 us (3%)
    pallas_call x1, Pallas kernels, solve(): pl.pallas_call(solve_kernel, out_shape=jax.ShapeDtypeStruct((1, 1, BLK, B...  55.6 us
    ppermute x16, waiting for transfers between devices, swap_op(): return lax.ppermute(value, 'op', pairs)  52 us
    all_gather x1, blocking collectives, body(): table = lax.all_gather(jnp.stack([src_block, dst_block]), 'op')  23 us
    ppermute x16, starting transfers between devices, swap_op(): return lax.ppermute(value, 'op', pairs)  21.9 us
    ppermute x3, starting transfers between devices, transfers(): received.append(lax.ppermute(mine, 'site', pairs))  7.66 us
    concatenate x12, other arithmetic, gather_terms(): held = [jnp.concatenate(pair, 0) for pair in zip(held, got)]  6.22 us
    ppermute x3, waiting for transfers between devices, transfers(): received.append(lax.ppermute(mine, 'site', pairs))  5.58 us
    pallas_call x1, Pallas kernels, chain_products(): pl.pallas_call(chain_kernel, out_shape=(out, out), in_specs=[pl.BlockSpec...  4.15 us
  transfers between devices with their start and end apart: 31, of which 10 were waited for; matrix products, arithmetic and copies ran while one was open for 6% of the time, Pallas kernels for 3%

profile of v1, /device:TPU:0, one launch (start us, length us, event | category | flops | bytes accessed | tf_op | source)
XLA Modules:
  0.0 188.0 jit_solution(15206412355117481501)
XLA Ops:
  1.0 2.1 %collective-permute-start.10 = (bf16[1,256,256]{2,1,0:T(8,128)(2,1)S(1)}, bf16[1,256,256]{2,1,0:T(8,128)(2,1)S(1)}, u32[]{:S(2)}, u32[]{:S(2)}) collective-permute-start(bf16[1,256,256]{2,1,0:T(8,128)(2,1)S(1)} %get-tuple-element.12), channel_id=1, source_target_pairs={{0,1},{1,0},{2,3},{3,2},{4,5},{5,4},{6,7},{7,6},{8,9},{9,8},{10,11... | collective-permute-start | bytes 393224 | tf_op jit(solution)/shard_map/ppermute | solution.py:25
  3.1 3.5 %collective-permute-done.10 = bf16[1,256,256]{2,1,0:T(8,128)(2,1)S(1)} collective-permute-done((bf16[1,256,256]{2,1,0:T(8,128)(2,1)S(1)}, bf16[1,256,256]{2,1,0:T(8,128)(2,1)S(1)}, u32[]{:S(2)}, u32[]{:S(2)}) %collective-permute-start.10) | collective-permute-done | bytes 131104 | tf_op jit(solution)/shard_map/ppermute | solution.py:25
  6.6 2.8 %collective-permute-start.11 = (bf16[2,256,256]{2,1,0:T(8,128)(2,1)S(1)}, bf16[2,256,256]{2,1,0:T(8,128)(2,1)S(1)}, u32[]{:S(2)}, u32[]{:S(2)}) collective-permute-start(bf16[2,256,256]{2,1,0:T(8,128)(2,1)S(1)} %pad_maximum_fusion.9), channel_id=1, source_target_pairs={{0,12},{1,13},{2,14},{3,15},{4,8},{5,9},{6,10},{7,11},{8,4},{9,5},... | collective-permute-start | bytes 786440 | tf_op jit(solution)/shard_map/ppermute | solution.py:25
  11.3 3.9 %collective-permute-start.16 = (bf16[1,256,256]{2,1,0:T(8,128)(2,1)S(1)}, bf16[1,256,256]{2,1,0:T(8,128)(2,1)S(1)}, u32[]{:S(2)}, u32[]{:S(2)}) collective-permute-start(bf16[1,256,256]{2,1,0:T(8,128)(2,1)S(1)} %get-tuple-element.11), channel_id=1, source_target_pairs={{0,3},{1,2},{2,1},{3,0},{4,7},{5,6},{6,5},{7,4},{8,11},{9,10},{10,... | collective-permute-start | bytes 393224 | tf_op jit(solution)/shard_map/ppermute | solution.py:25
  18.1 3.1 %collective-permute-start.12 = (bf16[4,256,256]{2,1,0:T(8,128)(2,1)}, bf16[4,256,256]{2,1,0:T(8,128)(2,1)}, u32[]{:S(2)}, u32[]{:S(2)}) collective-permute-start(bf16[4,256,256]{2,1,0:T(8,128)(2,1)} %pad_maximum_fusion.5), channel_id=1, source_target_pairs={{0,3},{1,2},{2,1},{3,0},{4,7},{5,6},{6,5},{7,4},{8,11},{9,10},{10,... | collective-permute-start | bytes 1572872 | tf_op jit(solution)/shard_map/ppermute | solution.py:25
  23.4 1.3 collective-permute-start.17
  24.7 14.7 %collective-permute-done.14 = bf16[2,256,256]{2,1,0:T(8,128)(2,1)S(1)} collective-permute-done((bf16[2,256,256]{2,1,0:T(8,128)(2,1)S(1)}, bf16[2,256,256]{2,1,0:T(8,128)(2,1)S(1)}, u32[]{:S(2)}, u32[]{:S(2)}) %collective-permute-start.14) | collective-permute-done | bytes 262176 | tf_op jit(solution)/shard_map/ppermute | solution.py:25
  40.3 1.7 collective-permute-start.15
  42.8 2.3 %shard_map.82 = f32[256,256]{1,0:T(8,128)} custom-call(s32[2]{0:T(128)} %pad_add_fusion.site_ref.ids, f32[2,256,256]{2,1,0:T(8,128)} %copy-done, f32[2,256,256]{2,1,0:T(8,128)} %copy-done.6), custom_call_target="tpu_custom_call" | custom-call | flops 201326592 | bytes 1048576 | tf_op jit(solution)/shard_map/pallas_call | solution.py:69
  45.2 5.1 %collective-permute-start.3 = (f32[256,256]{1,0:T(8,128)}, f32[256,256]{1,0:T(8,128)S(1)}, u32[]{:S(2)}, u32[]{:S(2)}) collective-permute-start(f32[256,256]{1,0:T(8,128)} %shard_map.82), channel_id=1, source_target_pairs={{0,96},{112,16},{1,97},{113,17},{2,98},{114,18},{3,99},{115,19},{4... | collective-permute-start | bytes 786440 | tf_op jit(solution)/shard_map/ppermute | solution.py:124
  53.4 3.9 %collective-permute-done.3.m3 = f32[256,256]{1,0:T(8,128)S(1)} collective-permute-done((f32[256,256]{1,0:T(8,128)}, f32[256,256]{1,0:T(8,128)S(1)}, u32[]{:S(2)}, u32[]{:S(2)}) %collective-permute-start.3) | collective-permute-done | bytes 262176 | tf_op jit(solution)/shard_map/ppermute | solution.py:124
  57.2 2.8 %collective-permute-start.9 = (bf16[4,256,256]{2,1,0:T(8,128)(2,1)S(1)}, bf16[4,256,256]{2,1,0:T(8,128)(2,1)S(1)}, u32[]{:S(2)}, u32[]{:S(2)}) collective-permute-start(bf16[4,256,256]{2,1,0:T(8,128)(2,1)S(1)} %pad_maximum_fusion.4), channel_id=1, source_target_pairs={{0,12},{1,13},{2,14},{3,15},{4,8},{5,9},{6,10},{7,11},{8,4},{9,5},... | collective-permute-start | bytes 1572872 | tf_op jit(solution)/shard_map/ppermute | solution.py:25
  60.0 1.3 collective-permute-start.1
  61.4 2.1 %pad_maximum_fusion.2.rest_2_ = bf16[8,256,256]{2,1,0:T(8,128)(2,1)} fusion(bf16[4,256,256]{2,1,0:T(8,128)(2,1)} %collective-permute-done.15, bf16[2,256,256]{2,1,0:T(8,128)(2,1)S(1)} %copy-done.5, bf16[1,256,256]{2,1,0:T(8,128)(2,1)S(1)} %collective-permute-done.13, bf16[1,256,256]{2,1,0:T(8,128)(2,1)S(1)} %get-tuple-element.13), kind=kLoop, calls=%fused_computation.2 | loop fusion | flops 1572864 | bytes 2097152 | tf_op jit(solution)/shard_map/concatenate | solution.py:133
  63.5 1.7 collective-permute-done.1.m1
  66.1 5.0 %collective-permute-done.9 = bf16[4,256,256]{2,1,0:T(8,128)(2,1)S(1)} collective-permute-done((bf16[4,256,256]{2,1,0:T(8,128)(2,1)S(1)}, bf16[4,256,256]{2,1,0:T(8,128)(2,1)S(1)}, u32[]{:S(2)}, u32[]{:S(2)}) %collective-permute-start.9) | collective-permute-done | bytes 524320 | tf_op jit(solution)/shard_map/ppermute | solution.py:25
  73.2 2.2 %collective-permute-start.22 = (bf16[8,256,256]{2,1,0:T(8,128)(2,1)S(1)}, bf16[8,256,256]{2,1,0:T(8,128)(2,1)}, u32[]{:S(2)}, u32[]{:S(2)}) collective-permute-start(bf16[8,256,256]{2,1,0:T(8,128)(2,1)S(1)} %pad_maximum_fusion.3.rest_3_), channel_id=1, source_target_pairs={{0,12},{1,13},{2,14},{3,15},{4,8},{5,9},{6,10},{7,11},{8,4},{9,5},... | collective-permute-start | bytes 3145736 | tf_op jit(solution)/shard_map/ppermute | solution.py:25
  75.5 3.1 %collective-permute-done.20.rest_5_ = bf16[8,256,256]{2,1,0:T(8,128)(2,1)} collective-permute-done((bf16[8,256,256]{2,1,0:T(8,128)(2,1)S(1)}, bf16[8,256,256]{2,1,0:T(8,128)(2,1)}, u32[]{:S(2)}, u32[]{:S(2)}) %collective-permute-start.20) | collective-permute-done | bytes 1048608 | tf_op jit(solution)/shard_map/ppermute | solution.py:25
  78.7 21.0 %collective-permute-done.22.rest_7_ = bf16[8,256,256]{2,1,0:T(8,128)(2,1)} collective-permute-done((bf16[8,256,256]{2,1,0:T(8,128)(2,1)S(1)}, bf16[8,256,256]{2,1,0:T(8,128)(2,1)}, u32[]{:S(2)}, u32[]{:S(2)}) %collective-permute-start.22) | collective-permute-done | bytes 1048608 | tf_op jit(solution)/shard_map/ppermute | solution.py:25
  100.2 2.1 %collective-permute-done.19.rest_4_ = bf16[8,256,256]{2,1,0:T(8,128)(2,1)} collective-permute-done((bf16[8,256,256]{2,1,0:T(8,128)(2,1)S(1)}, bf16[8,256,256]{2,1,0:T(8,128)(2,1)}, u32[]{:S(2)}, u32[]{:S(2)}) %collective-permute-start.19) | collective-permute-done | bytes 1048608 | tf_op jit(solution)/shard_map/ppermute | solution.py:25
  102.3 1.3 collective-permute-done.21.rest_6_
  103.7 23.0 %all-gather.1 = s32[16,2,4]{2,1,0:T(2,128)S(1)} all-gather(s32[1,2,4]{2,1,0:T(2,128)S(1)} %add_bitcast_fusion), channel_id=2, replica_groups=mesh['site'=8,'op'=16] {'op'}, dimensions={0}, use_global_device_ids=true | all-gather | bytes 544 | tf_op jit(solution)/shard_map/all_gather | solution.py:376
  128.0 4.2 %shard_map.83 = (bf16[256,256]{1,0:T(8,128)(2,1)}, bf16[256,256]{1,0:T(8,128)(2,1)}) custom-call(s32[2]{0:T(128)} %pad_add_fusion.site_ref.ids, f32[2,256,256]{2,1,0:T(8,128)} %copy-done.6, f32[256,256]{1,0:T(8,128)} %copy-done.15, f32[256,256]{1,0:T(8,128)} %copy-done.14, f32[256,256]{1,0:T(8,128)} %copy-done.13, f32[256,256]{1,0:T(8,128)} %copy-done.18, ...), custom_call_target="tpu_custom_call" | custom-call | flops 1207959552 | bytes 2097152 | tf_op jit(solution)/shard_map/pallas_call | solution.py:107
  132.2 55.6 %shard_map.84 = f32[1,1,256,256]{3,2,1,0:T(8,128)} custom-call(s32[2]{0:T(128)} %pad_add_fusion.site_ref.ids, s32[64]{0:T(128)} %reshape_squeeze.6.src_all, s32[64]{0:T(128)} %reshape_squeeze.7.dst_all, bf16[256,256]{1,0:T(8,128)(2,1)} %get-tuple-element.7.lq_ref, bf16[256,256]{1,0:T(8,128)(2,1)} %get-tuple-element.8.rq_ref, ...), custom_call_target="tpu_custom_call" | custom-call | flops 30198988800 | bytes 25165824 | tf_op jit(solution)/shard_map/pallas_call | solution.py:345
  (101 shorter events, 17.7 us)
Async XLA Ops:
  6.6 10.6 %collective-permute-start.11 = (bf16[2,256,256]{2,1,0:T(8,128)(2,1)S(1)}, bf16[2,256,256]{2,1,0:T(8,128)(2,1)S(1)}, u32[]{:S(2)}, u32[]{:S(2)}) collective-permute-start(bf16[2,256,256]{2,1,0:T(8,128)(2,1)S(1)} %pad_maximum_fusion.9), channel_id=1, source_target_pairs={{0,12},{1,13},{2,14},{3,15},{4,8},{5,9},{6,10},{7,11},{8,4},{9,5},... | collective-permute-start | bytes 786440 | tf_op jit(solution)/shard_map/ppermute | solution.py:25
  10.4 10.8 %collective-permute-start.13 = (bf16[1,256,256]{2,1,0:T(8,128)(2,1)S(1)}, bf16[1,256,256]{2,1,0:T(8,128)(2,1)S(1)}, u32[]{:S(2)}, u32[]{:S(2)}) collective-permute-start(bf16[1,256,256]{2,1,0:T(8,128)(2,1)S(1)} %get-tuple-element.13), channel_id=1, source_target_pairs={{0,12},{1,13},{2,14},{3,15},{4,8},{5,9},{6,10},{7,11},{8,4},{9,5},... | collective-permute-start | bytes 393224 | tf_op jit(solution)/shard_map/ppermute | solution.py:25
  11.0 11.5 %collective-permute-start.7 = (bf16[1,256,256]{2,1,0:T(8,128)(2,1)S(1)}, bf16[1,256,256]{2,1,0:T(8,128)(2,1)S(1)}, u32[]{:S(2)}, u32[]{:S(2)}) collective-permute-start(bf16[1,256,256]{2,1,0:T(8,128)(2,1)S(1)} %get-tuple-element.14), channel_id=1, source_target_pairs={{0,4},{1,5},{2,6},{3,7},{4,0},{5,1},{6,2},{7,3},{8,12},{9,13},{10,... | collective-permute-start | bytes 393224 | tf_op jit(solution)/shard_map/ppermute | solution.py:25
  11.3 11.4 %collective-permute-start.16 = (bf16[1,256,256]{2,1,0:T(8,128)(2,1)S(1)}, bf16[1,256,256]{2,1,0:T(8,128)(2,1)S(1)}, u32[]{:S(2)}, u32[]{:S(2)}) collective-permute-start(bf16[1,256,256]{2,1,0:T(8,128)(2,1)S(1)} %get-tuple-element.11), channel_id=1, source_target_pairs={{0,3},{1,2},{2,1},{3,0},{4,7},{5,6},{6,5},{7,4},{8,11},{9,10},{10,... | collective-permute-start | bytes 393224 | tf_op jit(solution)/shard_map/ppermute | solution.py:25
  17.1 25.0 %collective-permute-start = (f32[2,256,256]{2,1,0:T(8,128)S(1)}, f32[2,256,256]{2,1,0:T(8,128)S(1)}, u32[]{:S(2)}, u32[]{:S(2)}) collective-permute-start(f32[2,256,256]{2,1,0:T(8,128)S(1)} %constant_dynamic-update-slice_fusion.own_ref), channel_id=1, source_target_pairs={{0,16},{16,0},{32,48},{48,32},{64,80},{80,64},{96,112},{112,96},{1... | collective-permute-start | bytes 1572872 | tf_op jit(solution)/shard_map/ppermute | solution.py:29
  18.1 32.2 %collective-permute-start.12 = (bf16[4,256,256]{2,1,0:T(8,128)(2,1)}, bf16[4,256,256]{2,1,0:T(8,128)(2,1)}, u32[]{:S(2)}, u32[]{:S(2)}) collective-permute-start(bf16[4,256,256]{2,1,0:T(8,128)(2,1)} %pad_maximum_fusion.5), channel_id=1, source_target_pairs={{0,3},{1,2},{2,1},{3,0},{4,7},{5,6},{6,5},{7,4},{8,11},{9,10},{10,... | collective-permute-start | bytes 1572872 | tf_op jit(solution)/shard_map/ppermute | solution.py:25
  21.2 18.2 %collective-permute-start.14 = (bf16[2,256,256]{2,1,0:T(8,128)(2,1)S(1)}, bf16[2,256,256]{2,1,0:T(8,128)(2,1)S(1)}, u32[]{:S(2)}, u32[]{:S(2)}) collective-permute-start(bf16[2,256,256]{2,1,0:T(8,128)(2,1)S(1)} %pad_maximum_fusion.10), channel_id=1, source_target_pairs={{0,3},{1,2},{2,1},{3,0},{4,7},{5,6},{6,5},{7,4},{8,11},{9,10},{10,... | collective-permute-start | bytes 786440 | tf_op jit(solution)/shard_map/ppermute | solution.py:25
  22.5 30.3 %collective-permute-start.8 = (bf16[2,256,256]{2,1,0:T(8,128)(2,1)S(1)}, bf16[2,256,256]{2,1,0:T(8,128)(2,1)S(1)}, u32[]{:S(2)}, u32[]{:S(2)}) collective-permute-start(bf16[2,256,256]{2,1,0:T(8,128)(2,1)S(1)} %pad_maximum_fusion.8), channel_id=1, source_target_pairs={{0,1},{1,0},{2,3},{3,2},{4,5},{5,4},{6,7},{7,6},{8,9},{9,8},{10,11... | collective-permute-start | bytes 786440 | tf_op jit(solution)/shard_map/ppermute | solution.py:25
  23.4 29.5 %collective-permute-start.17 = (bf16[2,256,256]{2,1,0:T(8,128)(2,1)}, bf16[2,256,256]{2,1,0:T(8,128)(2,1)S(1)}, u32[]{:S(2)}, u32[]{:S(2)}) collective-permute-start(bf16[2,256,256]{2,1,0:T(8,128)(2,1)} %pad_maximum_fusion.11), channel_id=1, source_target_pairs={{0,4},{1,5},{2,6},{3,7},{4,0},{5,1},{6,2},{7,3},{8,12},{9,13},{10,... | collective-permute-start | bytes 786440 | tf_op jit(solution)/shard_map/ppermute | solution.py:25
  40.3 19.7 %collective-permute-start.15 = (bf16[4,256,256]{2,1,0:T(8,128)(2,1)}, bf16[4,256,256]{2,1,0:T(8,128)(2,1)}, u32[]{:S(2)}, u32[]{:S(2)}) collective-permute-start(bf16[4,256,256]{2,1,0:T(8,128)(2,1)} %pad_maximum_fusion.6), channel_id=1, source_target_pairs={{0,4},{1,5},{2,6},{3,7},{4,0},{5,1},{6,2},{7,3},{8,12},{9,13},{10,... | collective-permute-start | bytes 1572872 | tf_op jit(solution)/shard_map/ppermute | solution.py:25
  45.2 12.1 %collective-permute-start.3 = (f32[256,256]{1,0:T(8,128)}, f32[256,256]{1,0:T(8,128)S(1)}, u32[]{:S(2)}, u32[]{:S(2)}) collective-permute-start(f32[256,256]{1,0:T(8,128)} %shard_map.82), channel_id=1, source_target_pairs={{0,96},{112,16},{1,97},{113,17},{2,98},{114,18},{3,99},{115,19},{4... | collective-permute-start | bytes 786440 | tf_op jit(solution)/shard_map/ppermute | solution.py:124
  52.8 22.6 %collective-permute-start.24 = (bf16[8,256,256]{2,1,0:T(8,128)(2,1)S(1)}, bf16[8,256,256]{2,1,0:T(8,128)(2,1)S(1)}, u32[]{:S(2)}, u32[]{:S(2)}) collective-permute-start(bf16[8,256,256]{2,1,0:T(8,128)(2,1)S(1)} %pad_maximum_fusion.1.rest_1_), channel_id=1, source_target_pairs={{0,16},{16,0},{32,48},{48,32},{64,80},{80,64},{96,112},{112,96},{1... | collective-permute-start | bytes 3145736 | tf_op jit(solution)/shard_map/ppermute | solution.py:29
  52.9 25.7 %collective-permute-start.20 = (bf16[8,256,256]{2,1,0:T(8,128)(2,1)S(1)}, bf16[8,256,256]{2,1,0:T(8,128)(2,1)}, u32[]{:S(2)}, u32[]{:S(2)}) collective-permute-start(bf16[8,256,256]{2,1,0:T(8,128)(2,1)S(1)} %pad_maximum_fusion.1.rest_1_), channel_id=1, source_target_pairs={{0,4},{1,5},{2,6},{3,7},{4,0},{5,1},{6,2},{7,3},{8,12},{9,13},{10,... | collective-permute-start | bytes 3145736 | tf_op jit(solution)/shard_map/ppermute | solution.py:25
  57.2 13.8 %collective-permute-start.9 = (bf16[4,256,256]{2,1,0:T(8,128)(2,1)S(1)}, bf16[4,256,256]{2,1,0:T(8,128)(2,1)S(1)}, u32[]{:S(2)}, u32[]{:S(2)}) collective-permute-start(bf16[4,256,256]{2,1,0:T(8,128)(2,1)S(1)} %pad_maximum_fusion.4), channel_id=1, source_target_pairs={{0,12},{1,13},{2,14},{3,15},{4,8},{5,9},{6,10},{7,11},{8,4},{9,5},... | collective-permute-start | bytes 1572872 | tf_op jit(solution)/shard_map/ppermute | solution.py:25
  60.0 12.3 %collective-permute-start.18 = (bf16[4,256,256]{2,1,0:T(8,128)(2,1)S(1)}, bf16[4,256,256]{2,1,0:T(8,128)(2,1)S(1)}, u32[]{:S(2)}, u32[]{:S(2)}) collective-permute-start(bf16[4,256,256]{2,1,0:T(8,128)(2,1)S(1)} %pad_maximum_fusion.7), channel_id=1, source_target_pairs={{0,1},{1,0},{2,3},{3,2},{4,5},{5,4},{6,7},{7,6},{8,9},{9,8},{10,11... | collective-permute-start | bytes 1572872 | tf_op jit(solution)/shard_map/ppermute | solution.py:25
  73.2 26.5 %collective-permute-start.22 = (bf16[8,256,256]{2,1,0:T(8,128)(2,1)S(1)}, bf16[8,256,256]{2,1,0:T(8,128)(2,1)}, u32[]{:S(2)}, u32[]{:S(2)}) collective-permute-start(bf16[8,256,256]{2,1,0:T(8,128)(2,1)S(1)} %pad_maximum_fusion.3.rest_3_), channel_id=1, source_target_pairs={{0,12},{1,13},{2,14},{3,15},{4,8},{5,9},{6,10},{7,11},{8,4},{9,5},... | collective-permute-start | bytes 3145736 | tf_op jit(solution)/shard_map/ppermute | solution.py:25
  75.4 24.3 %collective-permute-start.23 = (bf16[8,256,256]{2,1,0:T(8,128)(2,1)S(1)}, bf16[8,256,256]{2,1,0:T(8,128)(2,1)S(1)}, u32[]{:S(2)}, u32[]{:S(2)}) collective-permute-start(bf16[8,256,256]{2,1,0:T(8,128)(2,1)S(1)} %pad_maximum_fusion.rest_0_), channel_id=1, source_target_pairs={{0,16},{16,0},{32,48},{48,32},{64,80},{80,64},{96,112},{112,96},{1... | collective-permute-start | bytes 3145736 | tf_op jit(solution)/shard_map/ppermute | solution.py:29
  75.4 26.9 %collective-permute-start.19 = (bf16[8,256,256]{2,1,0:T(8,128)(2,1)S(1)}, bf16[8,256,256]{2,1,0:T(8,128)(2,1)}, u32[]{:S(2)}, u32[]{:S(2)}) collective-permute-start(bf16[8,256,256]{2,1,0:T(8,128)(2,1)S(1)} %pad_maximum_fusion.rest_0_), channel_id=1, source_target_pairs={{0,3},{1,2},{2,1},{3,0},{4,7},{5,6},{6,5},{7,4},{8,11},{9,10},{10,... | collective-permute-start | bytes 3145736 | tf_op jit(solution)/shard_map/ppermute | solution.py:25
  78.6 25.0 %collective-permute-start.21 = (bf16[8,256,256]{2,1,0:T(8,128)(2,1)}, bf16[8,256,256]{2,1,0:T(8,128)(2,1)}, u32[]{:S(2)}, u32[]{:S(2)}) collective-permute-start(bf16[8,256,256]{2,1,0:T(8,128)(2,1)} %pad_maximum_fusion.2.rest_2_), channel_id=1, source_target_pairs={{0,1},{1,0},{2,3},{3,2},{4,5},{5,4},{6,7},{7,6},{8,9},{9,8},{10,11... | collective-permute-start | bytes 3145736 | tf_op jit(solution)/shard_map/ppermute | solution.py:25
  78.6 53.6 %collective-permute-start.25 = (bf16[8,256,256]{2,1,0:T(8,128)(2,1)}, bf16[8,256,256]{2,1,0:T(8,128)(2,1)}, u32[]{:S(2)}, u32[]{:S(2)}) collective-permute-start(bf16[8,256,256]{2,1,0:T(8,128)(2,1)} %pad_maximum_fusion.2.rest_2_), channel_id=1, source_target_pairs={{0,16},{16,0},{32,48},{48,32},{64,80},{80,64},{96,112},{112,96},{1... | collective-permute-start | bytes 3145736 | tf_op jit(solution)/shard_map/ppermute | solution.py:29
  99.7 32.5 %collective-permute-start.28 = (bf16[8,256,256]{2,1,0:T(8,128)(2,1)}, bf16[8,256,256]{2,1,0:T(8,128)(2,1)}, u32[]{:S(2)}, u32[]{:S(2)}) collective-permute-start(bf16[8,256,256]{2,1,0:T(8,128)(2,1)} %collective-permute-done.20.rest_5_), channel_id=1, source_target_pairs={{0,16},{16,0},{32,48},{48,32},{64,80},{80,64},{96,112},{112,96},{1... | collective-permute-start | bytes 3145736 | tf_op jit(solution)/shard_map/ppermute | solution.py:29
  99.7 32.5 %collective-permute-start.30 = (bf16[8,256,256]{2,1,0:T(8,128)(2,1)}, bf16[8,256,256]{2,1,0:T(8,128)(2,1)}, u32[]{:S(2)}, u32[]{:S(2)}) collective-permute-start(bf16[8,256,256]{2,1,0:T(8,128)(2,1)} %collective-permute-done.22.rest_7_), channel_id=1, source_target_pairs={{0,16},{16,0},{32,48},{48,32},{64,80},{80,64},{96,112},{112,96},{1... | collective-permute-start | bytes 3145736 | tf_op jit(solution)/shard_map/ppermute | solution.py:29
  102.3 29.9 %collective-permute-start.27 = (bf16[8,256,256]{2,1,0:T(8,128)(2,1)}, bf16[8,256,256]{2,1,0:T(8,128)(2,1)}, u32[]{:S(2)}, u32[]{:S(2)}) collective-permute-start(bf16[8,256,256]{2,1,0:T(8,128)(2,1)} %collective-permute-done.19.rest_4_), channel_id=1, source_target_pairs={{0,16},{16,0},{32,48},{48,32},{64,80},{80,64},{96,112},{112,96},{1... | collective-permute-start | bytes 3145736 | tf_op jit(solution)/shard_map/ppermute | solution.py:29
  103.6 28.6 %collective-permute-start.29 = (bf16[8,256,256]{2,1,0:T(8,128)(2,1)}, bf16[8,256,256]{2,1,0:T(8,128)(2,1)}, u32[]{:S(2)}, u32[]{:S(2)}) collective-permute-start(bf16[8,256,256]{2,1,0:T(8,128)(2,1)} %collective-permute-done.21.rest_6_), channel_id=1, source_target_pairs={{0,16},{16,0},{32,48},{48,32},{64,80},{80,64},{96,112},{112,96},{1... | collective-permute-start | bytes 3145736 | tf_op jit(solution)/shard_map/ppermute | solution.py:29
  (26 other events, 732.7 us)

commit v2 on v1

v2 whole, which is shorter than its diff:
```python
import jax
import jax.numpy as jnp
from jax import lax
from jax.experimental import pallas as pl
from jax.experimental.pallas import tpu as pltpu
from jax.sharding import PartitionSpec as P

ITERS = 2
BLK = 256
NB = 16
TAIL = 16
ROWS = 2 * BLK + TAIL
BF16 = jnp.bfloat16
F32 = jnp.float32
I32 = jnp.int32
HIGH = lax.Precision.HIGHEST
MIB = 1 << 20
FULL = (NB, BLK, BLK)

XA, XB, ZA, ZB = (1, 0), (3, 0), (0, 1), (0, 3)
ORDERS = (
    ((XA, ZA, XB, ZB), (ZA, XB, ZB, XA)),
    ((XB, ZB, XA, ZA), (ZB, XA, ZA, XB)),
)

SMEM = pl.BlockSpec(memory_space=pltpu.SMEM)
VMEM = pl.BlockSpec(memory_space=pltpu.VMEM)
HBM = pl.BlockSpec(memory_space=pltpu.HBM)


def swap_op(value, part, stage):
    pairs = []
    for site in range(8):
        mx, mz = ORDERS[site % 2][part][stage]
        for x in range(4):
            for z in range(4):
                pairs.append((site * 16 + x * 4 + z, site * 16 + (x ^ mx) * 4 + (z ^ mz)))
    return lax.ppermute(value, ("site", "op"), pairs)


def swap_core(value):
    return lax.ppermute(value, "site", [(i, i ^ 1) for i in range(8)])


def dot(a, b):
    return jnp.dot(a, b, preferred_element_type=F32)


def dot_nt(a, b):
    return lax.dot_general(a, b, (((1,), (1,)), ((), ())), preferred_element_type=F32)


def dot_tn(a, b):
    return lax.dot_general(a, b, (((0,), (0,)), ((), ())), preferred_element_type=F32)


def dot_high(a, b):
    return jnp.dot(a, b, precision=HIGH, preferred_element_type=F32)


def identity():
    rows = lax.broadcasted_iota(I32, (BLK, BLK), 0)
    cols = lax.broadcasted_iota(I32, (BLK, BLK), 1)
    return jnp.where(rows == cols, 1.0, 0.0).astype(F32)


def pair_kernel(site_ref, own_ref, other_ref, out_ref):
    eye = identity()
    first = site_ref[0] % 2 == 0
    a = jnp.where(first, own_ref[0], other_ref[1])
    b = jnp.where(first, other_ref[0], own_ref[1])
    out_ref[...] = dot_high(eye + 0.3 * a, eye + 0.3 * b)


def pair_product(site, own, other):
    return pl.pallas_call(
        pair_kernel,
        out_shape=jax.ShapeDtypeStruct((BLK, BLK), F32),
        in_specs=[SMEM, VMEM, VMEM],
        out_specs=VMEM,
        cost_estimate=pl.CostEstimate(flops=12 * BLK**3, bytes_accessed=MIB, transcendentals=0),
    )(site, own, other)


def chain_kernel(site_ref, other_ref, m1, m2, m3, across, lq_ref, rq_ref):
    eye = identity()
    site = site_ref[0]
    core, y = site % 2, site // 2
    own = (m1, m2, m3)
    lefts, rights = [], []
    for k in range(3):
        left = jnp.where(core == 0, own[k][...], across[k])
        right = jnp.where(core == 0, across[k], own[k][...])
        lefts.append(jnp.where(y >= k + 1, left, eye))
        rights.append(jnp.where(y + k + 1 <= 3, right, eye))
    s_part = jnp.where(core == 1, eye + 0.3 * other_ref[0], eye)
    t_part = jnp.where(core == 0, eye + 0.3 * other_ref[1], eye)
    a = dot_high(lefts[2], lefts[1])
    b = dot_high(lefts[0], s_part)
    c = dot_high(t_part, rights[0])
    d = dot_high(rights[1], rights[2])
    lq_ref[...] = dot_high(a, b).astype(BF16)
    rq_ref[...] = dot_high(c, d).astype(BF16)


def chain_products(site, other, received, across):
    out = jax.ShapeDtypeStruct((BLK, BLK), BF16)
    return pl.pallas_call(
        chain_kernel,
        out_shape=(out, out),
        in_specs=[SMEM] + [VMEM] * 5,
        out_specs=(VMEM, VMEM),
        cost_estimate=pl.CostEstimate(flops=72 * BLK**3, bytes_accessed=2 * MIB, transcendentals=0),
    )(site, other, *received, across)


UNROLL = 4


def apply_terms(terms, lefts, rights, vb, acc):
    mids = []
    for (s, d), r in zip(terms, rights):
        mids.append((dot(vb[s], r).astype(BF16), dot_nt(vb[d], r).astype(BF16)))
    for (s, d), l, (f, b) in zip(terms, lefts, mids):
        acc[d] += dot(l, f)
        acc[s] += dot_tn(l, b)


def group_copies(group, lbuf, rbuf, tails, sems, g):
    spot = pl.ds(4 * g, 4)
    return (
        pltpu.make_async_copy(group.at[:, pl.ds(0, BLK)], lbuf.at[spot], sems.at[3 * g]),
        pltpu.make_async_copy(group.at[:, pl.ds(BLK, BLK)], rbuf.at[spot], sems.at[3 * g + 1]),
        pltpu.make_async_copy(group.at[:, pl.ds(2 * BLK, TAIL)], tails.at[spot], sems.at[3 * g + 2]),
    )


def load_terms(groups, lbuf, rbuf, tails, sems):
    copies = [
        group_copies(group, lbuf, rbuf, tails, sems, g) for g, group in enumerate(groups)
    ]
    for copy in [c[2] for c in copies] + [c for pair in copies for c in pair[:2]]:
        copy.start()


def read_blocks(groups, lbuf, rbuf, tails, sems, table_v, table, sem):
    for g, group in enumerate(groups):
        group_copies(group, lbuf, rbuf, tails, sems, g)[2].wait()
    table_v[...] = tails[:, 0, :128].astype(I32)
    move = pltpu.make_async_copy(table_v, table, sem)
    move.start()
    move.wait()


def build_and_apply(groups, lbuf, rbuf, tails, sems, table, lq_ref, rq_ref, vb, acc, done):
    lq = lq_ref[...]
    lq_t = lq.T
    rq = rq_ref[...]
    rq_t = rq.T

    def some(g, carry):
        left, right, _ = group_copies(groups[0], lbuf, rbuf, tails, sems, g)
        left.wait()
        right.wait()
        spots = [4 * g + u for u in range(4)]
        terms = [(table[k, 0], table[k, 1]) for k in spots]
        temps = [(dot(lbuf[k], lq).astype(BF16), dot(rbuf[k], rq_t).astype(BF16)) for k in spots]
        lefts = [dot(lq_t, lt).astype(BF16) for lt, _ in temps]
        rights = [dot(rq, rt).astype(BF16) for _, rt in temps]
        for k, l, r in zip(spots, lefts, rights):
            lbuf[k] = l
            rbuf[k] = r
        done(g)
        apply_terms(terms, lefts, rights, vb, acc)
        return carry

    lax.fori_loop(0, len(groups), some, 0)


def part_kernel(count, carried, lq_ref, rq_ref, vb_hbm, *rest):
    groups, rest = rest[:count], rest[count:]
    if carried:
        h_in, rest = rest[0], rest[1:]
    left_out, right_out, table_out, h_out = rest[:4]
    lbuf, rbuf, tails, table_v, table, vb, hv, sems, out_sems = rest[4:]
    load_terms(groups, lbuf, rbuf, tails, sems)
    start = pltpu.make_async_copy(vb_hbm, vb, sems.at[3 * count])
    start.start()
    if carried:
        before = pltpu.make_async_copy(h_in, hv, sems.at[3 * count + 1])
        before.start()
    else:
        def clear(b, carry):
            hv[b] = jnp.zeros((BLK, BLK), F32)
            return carry

        lax.fori_loop(0, NB, clear, 0)
    read_blocks(groups, lbuf, rbuf, tails, sems, table_v, table, sems.at[3 * count + 2])
    table_copy = pltpu.make_async_copy(table_v, table_out, out_sems.at[2 * count + 1])
    table_copy.start()

    def out_copies(g):
        spot = pl.ds(4 * g, 4)
        return (
            pltpu.make_async_copy(lbuf.at[spot], left_out.at[spot], out_sems.at[2 * g]),
            pltpu.make_async_copy(rbuf.at[spot], right_out.at[spot], out_sems.at[2 * g + 1]),
        )

    def done(g):
        for copy in out_copies(g):
            copy.start()

    start.wait()
    if carried:
        before.wait()
    build_and_apply(groups, lbuf, rbuf, tails, sems, table, lq_ref, rq_ref, vb, hv, done)
    last = pltpu.make_async_copy(hv, h_out, out_sems.at[2 * count])
    last.start()
    table_copy.wait()
    for g in range(count):
        for copy in out_copies(g):
            copy.wait()
    last.wait()


def part(groups, lq, rq, vb, h_in):
    count = len(groups)
    terms = 4 * count
    carried = h_in is not None

    def kernel(*refs):
        part_kernel(count, carried, *refs)

    env = jax.ShapeDtypeStruct((terms, BLK, BLK), BF16)
    return pl.pallas_call(
        kernel,
        out_shape=(
            env,
            env,
            jax.ShapeDtypeStruct((terms, 128), I32),
            jax.ShapeDtypeStruct(FULL, F32),
        ),
        in_specs=[VMEM, VMEM] + [HBM] * (1 + count + carried),
        out_specs=(HBM,) * 4,
        scratch_shapes=[
            pltpu.VMEM((terms, BLK, BLK), BF16),
            pltpu.VMEM((terms, BLK, BLK), BF16),
            pltpu.VMEM((terms, TAIL, BLK), BF16),
            pltpu.VMEM((terms, 128), I32),
            pltpu.SMEM((terms, 128), I32),
            pltpu.VMEM(FULL, BF16),
            pltpu.VMEM(FULL, F32),
            pltpu.SemaphoreType.DMA((3 * count + 3,)),
            pltpu.SemaphoreType.DMA((2 * count + 2,)),
        ],
        compiler_params=pltpu.CompilerParams(vmem_limit_bytes=56 * MIB),
        cost_estimate=pl.CostEstimate(
            flops=terms * 16 * BLK**3, bytes_accessed=terms * 8 * BLK * BLK, transcendentals=0
        ),
    )(lq, rq, vb, *groups, *((h_in,) if carried else ()))


def fold(p):
    return jnp.sum(p.reshape(BLK // 8, 8, BLK), axis=0)


def total(acc):
    return jnp.sum(jnp.sum(acc, axis=0, keepdims=True), axis=1, keepdims=True)


def solve_kernel(count, sizes, ids, lq_ref, rq_ref, x_hbm, diag_hbm, vb_hbm, h_hbm, *rest):
    tables, rest = rest[: len(sizes)], rest[len(sizes):]
    envs, rest = rest[: 2 * len(sizes)], rest[2 * len(sizes):]
    groups, rest = rest[:count], rest[count:]
    out_ref = rest[0]
    lbuf, rbuf, tails, table_v, table, xv, hv, tv, gv, dv, vb, sems, in_sems = rest[1:]
    op = ids[1]
    zero = jnp.zeros((8, BLK), F32)

    def over_blocks(step, sums):
        return lax.fori_loop(0, NB, step, (zero,) * sums)

    load_terms(groups, lbuf, rbuf, tails, sems)
    vectors = [
        pltpu.make_async_copy(source, target, in_sems.at[i])
        for i, (source, target) in enumerate(
            ((vb_hbm, vb), (h_hbm, hv), (x_hbm, xv), (diag_hbm.at[0], dv))
        )
    ]
    for copy in vectors:
        copy.start()
    built = []
    begin = 4 * count
    for i, size in enumerate(sizes):
        spot = pl.ds(begin, size)
        for j, (source, target) in enumerate(
            ((envs[2 * i], lbuf), (envs[2 * i + 1], rbuf), (tables[i], table))
        ):
            copy = pltpu.make_async_copy(source, target.at[spot], in_sems.at[4 + 3 * i + j])
            copy.start()
            built.append(copy)
        begin += size

    read_blocks(
        groups, lbuf, rbuf, tails, sems, table_v, table.at[pl.ds(0, 4 * count)], sems.at[3 * count]
    )
    vectors[0].wait()
    vectors[1].wait()
    build_and_apply(
        groups, lbuf, rbuf, tails, sems, table, lq_ref, rq_ref, vb, hv, lambda g: None
    )
    vectors[2].wait()
    vectors[3].wait()

    def finish_h(b, sums):
        x = xv[b]
        h = hv[b] + dv[b] * x
        hv[b] = h
        return (sums[0] + fold(x * h),)

    (theta_sum,) = over_blocks(finish_h, 1)
    theta = total(theta_sum)

    def correction(theta):
        def residual(b, sums):
            x = xv[b]
            t = (hv[b] - theta * x) / dv[b]
            tv[b] = t
            return (sums[0] + fold(x * t),)

        (along,) = over_blocks(residual, 1)
        along = total(along)

        def orthogonal(b, sums):
            t = tv[b] - along * xv[b]
            tv[b] = t
            return (sums[0] + fold(t * t),)

        (size,) = over_blocks(orthogonal, 1)
        return lax.rsqrt(total(size) + 1e-12)

    def rotation(theta, b, c):
        low = (c - theta) / 2 + jnp.sqrt(((theta - c) / 2) ** 2 + b * b)
        inv = 1.0 / jnp.sqrt(low * low + b * b)
        return low * inv, b * inv

    def over_terms(step, value):
        def some(i, value):
            spots = [i * UNROLL + u for u in range(UNROLL)]
            return step([(table[k, 0], table[k, 1]) for k in spots], spots, value)

        return lax.fori_loop(0, 64 // UNROLL, some, value)

    for step in range(ITERS - 1):
        scale_t = correction(theta)

        def unit(b, sums):
            t = tv[b] * scale_t
            tv[b] = t
            vb[b] = t.astype(BF16)
            gv[b] = dv[b] * t
            return sums

        over_blocks(unit, 0)
        if step == 0:
            for copy in built:
                copy.wait()

        def apply_step(terms, spots, value):
            apply_terms(terms, [lbuf[k] for k in spots], [rbuf[k] for k in spots], vb, gv)
            return value

        over_terms(apply_step, 0)

        def couplings(b, sums):
            g = gv[b]
            return (sums[0] + fold(xv[b] * g), sums[1] + fold(tv[b] * g))

        cross, curve = over_blocks(couplings, 2)
        keep, move = rotation(theta, total(cross), total(curve))

        def update(b, sums):
            x = keep * xv[b] - move * tv[b]
            h = keep * hv[b] - move * gv[b]
            xv[b] = x
            hv[b] = h
            return (sums[0] + fold(x * h),)

        (theta_sum,) = over_blocks(update, 1)
        theta = total(theta_sum)

    scale_t = correction(theta)

    def last_unit(b, sums):
        t = tv[b] * scale_t
        tv[b] = t
        vb[b] = t.astype(BF16)
        return (sums[0] + fold(hv[b] * t), sums[1] + fold(dv[b] * t * t))

    cross, curve_diag = over_blocks(last_unit, 2)

    def last_step(terms, spots, acc):
        mids = [dot(vb[s], rbuf[k]).astype(BF16) for (s, _), k in zip(terms, spots)]
        for (_, d), k, f in zip(terms, spots, mids):
            acc = acc + fold(tv[d] * dot(lbuf[k], f))
        return acc

    curve_terms = over_terms(last_step, zero)
    curve = total(curve_diag) + 2.0 * total(curve_terms)
    keep, move = rotation(theta, total(cross), curve)
    amplitude = float(NB * BLK * BLK) ** 0.5
    out_ref[0, 0] = (keep * xv[op] - move * tv[op]) * amplitude


def solve(ids, parts, lq, rq, x, diagonal, vb, h, groups):
    count = len(groups)
    sizes = tuple(p[0].shape[0] for p in parts)

    def kernel(*refs):
        solve_kernel(count, sizes, *refs)

    return pl.pallas_call(
        kernel,
        out_shape=jax.ShapeDtypeStruct((1, 1, BLK, BLK), F32),
        in_specs=[SMEM, VMEM, VMEM] + [HBM] * (4 + 3 * len(sizes) + count),
        out_specs=VMEM,
        scratch_shapes=[
            pltpu.VMEM((64, BLK, BLK), BF16),
            pltpu.VMEM((64, BLK, BLK), BF16),
            pltpu.VMEM((4 * count, TAIL, BLK), BF16),
            pltpu.VMEM((4 * count, 128), I32),
            pltpu.SMEM((64, 128), I32),
            pltpu.VMEM(FULL, F32),
            pltpu.VMEM(FULL, F32),
            pltpu.VMEM(FULL, F32),
            pltpu.VMEM(FULL, F32),
            pltpu.VMEM(FULL, F32),
            pltpu.VMEM(FULL, BF16),
            pltpu.SemaphoreType.DMA((3 * count + 1,)),
            pltpu.SemaphoreType.DMA((4 + 3 * len(sizes),)),
        ],
        compiler_params=pltpu.CompilerParams(vmem_limit_bytes=56 * MIB),
        cost_estimate=pl.CostEstimate(
            flops=2 * 500 * BLK**3, bytes_accessed=24 * MIB, transcendentals=0
        ),
    )(
        ids,
        lq,
        rq,
        x,
        diagonal,
        vb,
        h,
        *[p[2] for p in parts],
        *[env for p in parts for env in p[:2]],
        *groups,
    )


def start_kernel(psi_ref, x_hbm, vb_hbm, xv, vb, sems):
    def square(b, acc):
        v = psi_ref[0, b].astype(F32)
        return acc + fold(v * v)

    norm = lax.fori_loop(0, NB, square, jnp.zeros((8, BLK), F32))
    scale = lax.rsqrt(total(norm) + 1e-12)

    def unit(b, carry):
        v = psi_ref[0, b].astype(F32) * scale
        xv[b] = v
        vb[b] = v.astype(BF16)
        return carry

    lax.fori_loop(0, NB, unit, 0)
    copies = (
        pltpu.make_async_copy(xv, x_hbm, sems.at[0]),
        pltpu.make_async_copy(vb, vb_hbm, sems.at[1]),
    )
    for copy in copies:
        copy.start()
    for copy in copies:
        copy.wait()


def start_vector(psi):
    return pl.pallas_call(
        start_kernel,
        out_shape=(jax.ShapeDtypeStruct(FULL, F32), jax.ShapeDtypeStruct(FULL, BF16)),
        in_specs=[VMEM],
        out_specs=(HBM, HBM),
        scratch_shapes=[
            pltpu.VMEM(FULL, F32),
            pltpu.VMEM(FULL, BF16),
            pltpu.SemaphoreType.DMA((2,)),
        ],
        compiler_params=pltpu.CompilerParams(vmem_limit_bytes=20 * MIB),
        cost_estimate=pl.CostEstimate(flops=8 * MIB, bytes_accessed=12 * MIB, transcendentals=0),
    )(psi)


def after(values, marks):
    return lax.optimization_barrier((tuple(values), tuple(marks)))[0]


def body(psi, diagonal, left_step, right_step, left_env, right_env, src_block, dst_block):
    site = lax.axis_index("site")
    op = lax.axis_index("op")
    ids = jnp.stack([site, op]).astype(I32)
    core = site % 2

    blocks = jnp.stack([src_block, dst_block], 1).astype(BF16)
    tails = jnp.pad(blocks[:, None, :], ((0, 0), (0, TAIL - 1), (0, BLK - 2)))
    whole = jnp.concatenate([left_env, right_env, tails], 1)
    mine = lax.dynamic_slice_in_dim(whole, 2 * core, 2, 0)
    parts = (mine[:1], mine[1:])

    steps = jnp.concatenate([left_step, right_step], 0)
    first = [swap_op(p, i, 0) for i, p in enumerate(parts)]
    other = swap_core(steps)
    product = pair_product(ids, steps, other)

    two = [jnp.concatenate(pair, 0) for pair in zip(parts, first)]
    two, product = lax.optimization_barrier((two, product))
    second = [swap_op(p, i, 1) for i, p in enumerate(two)]
    received = []
    for k in (1, 2, 3):
        pairs = [(2 * y, 2 * (y + k)) for y in range(4 - k)]
        pairs += [(2 * y + 1, 2 * (y - k) + 1) for y in range(k, 4)]
        received.append(lax.ppermute(product, "site", pairs))

    four = [jnp.concatenate(pair, 0) for pair in zip(two, second)]
    third = [swap_op(p, i, 2) for i, p in enumerate(four)]
    received, (psi,) = lax.optimization_barrier((received, after((psi,), four)))
    across = swap_core(jnp.stack(received))
    x, vb = start_vector(psi)
    lq, rq = chain_products(ids, other, received, across)
    four, (lq, rq, vb) = lax.optimization_barrier((four, (lq, rq, vb)))
    old = [swap_op(p, i, 3) for i, p in enumerate(four)]
    new = [swap_op(p, i, 3) for i, p in enumerate(third)]

    def both(groups):
        return list(groups) + [swap_core(g) for g in groups]

    built = [part(both(four), lq, rq, vb, None)]
    old = after(old, built[-1][3:])
    built.append(part(both(third), lq, rq, vb, built[-1][3]))
    new = after(new, built[-1][3:])
    return solve(ids, built, lq, rq, x, diagonal, vb, built[-1][3], both(old) + both(new))


def solution(mesh):
    placed = (
        P("site", None, None, None),
        P("site", None, None, None),
        P("site", None, None),
        P("site", None, None),
        P("op", None, None),
        P("op", None, None),
        P("op"),
        P("op"),
    )
    return jax.shard_map(
        body, mesh=mesh, in_specs=placed, out_specs=P("site", "op", None, None), check_vma=False
    )
```

time: 188 us -> 142 us (0.76)
  waiting for transfers between devices: 57.6 us -> 24.3 us
  blocking collectives: 23 us -> 0 us
  Pallas kernels: 62 us -> 79.1 us
  other arithmetic: 6.87 us -> 0.86 us
  starting transfers between devices: 31.7 us -> 27.6 us
  local copies, waits for them, and re-layouts: 6.1 us -> 8.36 us
    ppermute x19 -> x13, waiting for transfers between devices: 57.6 us -> 20.6 us  [the longest x10 16.7 us: swap_op(): return lax.ppermute(value, ('site', 'op'), pairs)]
    all_gather x1 -> x0, blocking collectives: 23 us -> none  [body(): table = lax.all_gather(jnp.stack([src_block, dst_block]), 'op')]
    pallas_call x2 -> x5, Pallas kernels: 59.7 us -> 76.8 us  [the longest x1 46.6 us: solve(): pl.pallas_call(kernel, out_shape=jax.ShapeDtypeStruct((1, 1, BLK, BLK), F...]
    concatenate x12 -> x3, other arithmetic: 6.22 us -> 0.14 us  [the longest x2 0.1 us: body(): two = [jnp.concatenate(pair, 0) for pair in zip(parts, first)]]
    ppermute x19 -> x13, starting transfers between devices: 29.5 us -> 23.7 us  [the longest x10 14.1 us: swap_op(): return lax.ppermute(value, ('site', 'op'), pairs)]
    unnamed x39 -> x53, local copies, waits for them, and re-layouts: 1.84 us -> 7.17 us
    ppermute x12 -> x10, waiting for transfers between devices: 0.03 us -> 3.74 us  [swap_core(): return lax.ppermute(value, 'site', [(i, i ^ 1) for i in range(8)])]
    slice x3 -> x1, local copies, waits for them, and re-layouts: 2.02 us -> 0.04 us  [body(): parts = (mine[:1], mine[1:])]
  transfers between devices with their start and end apart: 31 -> 23, of which waited for: 10 -> 9; matrix products, arithmetic and copies ran while one was open for 6% -> 1% of each run, Pallas kernels for 3% -> 21%
where the time goes in v2:
time: 142 us; the launch traced here: 141 us
  Pallas kernels  79.1 us (56%)
  starting transfers between devices  27.6 us (19%)
  waiting for transfers between devices  24.3 us (17%)
  local copies, waits for them, and re-layouts  8.36 us (6%)
    pallas_call x1, Pallas kernels, solve(): pl.pallas_call(kernel, out_shape=jax.ShapeDtypeStruct((1, 1, BLK, BLK), F...  46.6 us
    pallas_call x2, Pallas kernels, part(): pl.pallas_call(kernel, out_shape=(env, env, jax.ShapeDtypeStruct((terms,...  24.7 us
    ppermute x10, waiting for transfers between devices, swap_op(): return lax.ppermute(value, ('site', 'op'), pairs)  16.7 us
    ppermute x10, starting transfers between devices, swap_op(): return lax.ppermute(value, ('site', 'op'), pairs)  14.1 us
    ppermute x3, starting transfers between devices, body(): received.append(lax.ppermute(product, 'site', pairs))  9.6 us
    unnamed x53, local copies, waits for them, and re-layouts  7.17 us
    pallas_call x1, Pallas kernels, chain_products(): pl.pallas_call(chain_kernel, out_shape=(out, out), in_specs=[SMEM] + [VME...  4.03 us
    ppermute x3, waiting for transfers between devices, body(): received.append(lax.ppermute(product, 'site', pairs))  3.92 us
  transfers between devices with their start and end apart: 23, of which 9 were waited for; matrix products, arithmetic and copies ran while one was open for 1% of the time, Pallas kernels for 21%

profile of v2, /device:TPU:0, one launch (start us, length us, event | category | flops | bytes accessed | tf_op | source)
XLA Modules:
  0.0 140.8 jit_solution(5753198502262504550)
XLA Ops:
  2.8 1.6 %collective-permute-start = (bf16[1,528,256]{2,1,0:T(8,128)(2,1)S(1)}, bf16[1,528,256]{2,1,0:T(8,128)(2,1)S(1)}, u32[]{:S(2)}, u32[]{:S(2)}) collective-permute-start(bf16[1,528,256]{2,1,0:T(8,128)(2,1)S(1)} %get-tuple-element.64), channel_id=1, source_target_pairs={{0,4},{1,5},{2,6},{3,7},{4,0},{5,1},{6,2},{7,3},{8,12},{9,13},{10,... | collective-permute-start | bytes 811016 | tf_op jit(solution)/shard_map/ppermute | solution.py:38
  4.4 1.9 %collective-permute-start.1 = (bf16[1,528,256]{2,1,0:T(8,128)(2,1)S(1)}, bf16[1,528,256]{2,1,0:T(8,128)(2,1)S(1)}, u32[]{:S(2)}, u32[]{:S(2)}) collective-permute-start(bf16[1,528,256]{2,1,0:T(8,128)(2,1)S(1)} %get-tuple-element.63), channel_id=1, source_target_pairs={{0,1},{1,0},{2,3},{3,2},{4,5},{5,4},{6,7},{7,6},{8,9},{9,8},{10,11... | collective-permute-start | bytes 811016 | tf_op jit(solution)/shard_map/ppermute | solution.py:38
  7.0 2.3 %collective-permute-done = bf16[1,528,256]{2,1,0:T(8,128)(2,1)S(1)} collective-permute-done((bf16[1,528,256]{2,1,0:T(8,128)(2,1)S(1)}, bf16[1,528,256]{2,1,0:T(8,128)(2,1)S(1)}, u32[]{:S(2)}, u32[]{:S(2)}) %collective-permute-start) | collective-permute-done | bytes 270368 | tf_op jit(solution)/shard_map/ppermute | solution.py:38
  9.3 1.5 %collective-permute-done.1 = bf16[1,528,256]{2,1,0:T(8,128)(2,1)S(1)} collective-permute-done((bf16[1,528,256]{2,1,0:T(8,128)(2,1)S(1)}, bf16[1,528,256]{2,1,0:T(8,128)(2,1)S(1)}, u32[]{:S(2)}, u32[]{:S(2)}) %collective-permute-start.1) | collective-permute-done | bytes 270368 | tf_op jit(solution)/shard_map/ppermute | solution.py:38
  11.8 2.3 %shard_map.82 = f32[256,256]{1,0:T(8,128)} custom-call(s32[2]{0:T(128)} %pad_add_fusion.site_ref.refs_0_, f32[2,256,256]{2,1,0:T(8,128)} %copy-done.3, f32[2,256,256]{2,1,0:T(8,128)} %copy-done.6), custom_call_target="tpu_custom_call" | custom-call | flops 201326592 | bytes 1048576 | tf_op jit(solution)/shard_map/pallas_call | solution.py:76
  14.1 1.9 %collective-permute-start.3 = (bf16[2,528,256]{2,1,0:T(8,128)(2,1)S(1)}, bf16[2,528,256]{2,1,0:T(8,128)(2,1)S(1)}, u32[]{:S(2)}, u32[]{:S(2)}) collective-permute-start(bf16[2,528,256]{2,1,0:T(8,128)(2,1)S(1)} %pad_maximum_fusion.1), channel_id=1, source_target_pairs={{0,1},{1,0},{2,3},{3,2},{4,5},{5,4},{6,7},{7,6},{8,9},{9,8},{10,11... | collective-permute-start | bytes 1622024 | tf_op jit(solution)/shard_map/ppermute | solution.py:38
  16.0 2.1 %collective-permute-start.4 = (bf16[2,528,256]{2,1,0:T(8,128)(2,1)S(1)}, bf16[2,528,256]{2,1,0:T(8,128)(2,1)S(1)}, u32[]{:S(2)}, u32[]{:S(2)}) collective-permute-start(bf16[2,528,256]{2,1,0:T(8,128)(2,1)S(1)} %pad_maximum_fusion.2), channel_id=1, source_target_pairs={{0,12},{1,13},{2,14},{3,15},{4,8},{5,9},{6,10},{7,11},{8,4},{9,5},... | collective-permute-start | bytes 1622024 | tf_op jit(solution)/shard_map/ppermute | solution.py:38
  18.1 3.5 %collective-permute-start.5 = (f32[256,256]{1,0:T(8,128)}, f32[256,256]{1,0:T(8,128)S(1)}, u32[]{:S(2)}, u32[]{:S(2)}) collective-permute-start(f32[256,256]{1,0:T(8,128)} %shard_map.82), channel_id=1, source_target_pairs={{0,32},{32,64},{64,96},{48,16},{80,48},{112,80},{1,33},{33,65},{65... | collective-permute-start | bytes 786440 | tf_op jit(solution)/shard_map/ppermute | solution.py:529
  21.6 4.8 %collective-permute-start.6 = (f32[256,256]{1,0:T(8,128)}, f32[256,256]{1,0:T(8,128)S(1)}, u32[]{:S(2)}, u32[]{:S(2)}) collective-permute-start(f32[256,256]{1,0:T(8,128)} %shard_map.82), channel_id=1, source_target_pairs={{0,64},{32,96},{80,16},{112,48},{1,65},{33,97},{81,17},{113,49},{2... | collective-permute-start | bytes 786440 | tf_op jit(solution)/shard_map/ppermute | solution.py:529
  28.0 2.6 %collective-permute-done.6.m2 = f32[256,256]{1,0:T(8,128)S(1)} collective-permute-done((f32[256,256]{1,0:T(8,128)}, f32[256,256]{1,0:T(8,128)S(1)}, u32[]{:S(2)}, u32[]{:S(2)}) %collective-permute-start.6) | collective-permute-done | bytes 262176 | tf_op jit(solution)/shard_map/ppermute | solution.py:529
  30.6 1.3 collective-permute-done.7.m3
  32.0 1.6 %collective-permute-start.8 = (f32[3,256,256]{2,1,0:T(8,128)S(1)}, f32[3,256,256]{2,1,0:T(8,128)}, u32[]{:S(2)}, u32[]{:S(2)}) collective-permute-start(f32[3,256,256]{2,1,0:T(8,128)S(1)} %pad_maximum_fusion), channel_id=1, source_target_pairs={{0,16},{16,0},{32,48},{48,32},{64,80},{80,64},{96,112},{112,96},{1... | collective-permute-start | bytes 2359304 | tf_op jit(solution)/shard_map/ppermute | solution.py:42
  35.8 1.4 %shard_map.84 = (f32[16,256,256]{2,1,0:T(8,128)S(1)}, bf16[16,256,256]{2,1,0:T(8,128)(2,1)S(1)}) custom-call(bf16[1,16,256,256]{3,2,1,0:T(8,128)(2,1)S(1)} %copy-done), custom_call_target="tpu_custom_call" | custom-call | flops 8388608 | bytes 12582912 | tf_op jit(solution)/shard_map/pallas_call | solution.py:486
  37.3 2.0 %copy-done.1 = f32[16,256,256]{2,1,0:T(8,128)} copy-done((f32[16,256,256]{2,1,0:T(8,128)}, f32[16,256,256]{2,1,0:T(8,128)S(1)}, u32[]{:S(2)}) %copy-start.1) | copy-done | bytes 4194328
  39.2 1.3 copy-done.2
  40.5 4.0 %shard_map.83 = (bf16[256,256]{1,0:T(8,128)(2,1)}, bf16[256,256]{1,0:T(8,128)(2,1)}) custom-call(s32[2]{0:T(128)} %pad_add_fusion.site_ref.refs_0_, f32[2,256,256]{2,1,0:T(8,128)} %copy-done.6, f32[256,256]{1,0:T(8,128)} %copy-done.9, f32[256,256]{1,0:T(8,128)} %copy-done.10, f32[256,256]{1,0:T(8,128)} %copy-done.11, ...), custom_call_target="tpu_custom_call" | custom-call | flops 1207959552 | bytes 2097152 | tf_op jit(solution)/shard_map/pallas_call | solution.py:108
  45.1 2.1 %collective-permute-start.15 = (bf16[4,528,256]{2,1,0:T(8,128)(2,1)S(1)}, bf16[4,528,256]{2,1,0:T(8,128)(2,1)S(1)}, u32[]{:S(2)}, u32[]{:S(2)}) collective-permute-start(bf16[4,528,256]{2,1,0:T(8,128)(2,1)S(1)} %constant_dynamic-update-slice_fusion.2.refs_3_), channel_id=1, source_target_pairs={{0,3},{1,2},{2,1},{3,0},{4,7},{5,6},{6,5},{7,4},{8,11},{9,10},{10,... | collective-permute-start | bytes 3244040 | tf_op jit(solution)/shard_map/ppermute | solution.py:38
  47.1 2.8 %collective-permute-done.9.refs_3_ = bf16[4,528,256]{2,1,0:T(8,128)(2,1)S(1)} collective-permute-done((bf16[4,528,256]{2,1,0:T(8,128)(2,1)S(1)}, bf16[4,528,256]{2,1,0:T(8,128)(2,1)S(1)}, u32[]{:S(2)}, u32[]{:S(2)}) %collective-permute-start.9) | collective-permute-done | bytes 1081376 | tf_op jit(solution)/shard_map/ppermute | solution.py:38
  53.3 9.3 %collective-permute-done.15.refs_13_ = bf16[4,528,256]{2,1,0:T(8,128)(2,1)S(1)} collective-permute-done((bf16[4,528,256]{2,1,0:T(8,128)(2,1)S(1)}, bf16[4,528,256]{2,1,0:T(8,128)(2,1)S(1)}, u32[]{:S(2)}, u32[]{:S(2)}) %collective-permute-start.15) | collective-permute-done | bytes 1081376 | tf_op jit(solution)/shard_map/ppermute | solution.py:38
  63.3 11.8 %shard_map.85 = (bf16[16,256,256]{2,1,0:T(8,128)(2,1)}, bf16[16,256,256]{2,1,0:T(8,128)(2,1)}, s32[16,128]{1,0:T(8,128)}, f32[16,256,256]{2,1,0:T(8,128)}) custom-call(bf16[256,256]{1,0:T(8,128)(2,1)} %get-tuple-element.45.refs_0_.refs_1_, bf16[256,256]{1,0:T(8,128)(2,1)} %get-tuple-element.46.refs_1_.refs_2_, bf16[16,256,256]{2,1,0:T(8,128)(2,1)} %copy-done.2, ...), custom_call_target="tpu_custom_call" | custom-call | flops 4294967296 | bytes 8388608 | tf_op jit(solution)/shard_map/pallas_call | solution.py:235
  75.7 12.9 %shard_map.86 = (bf16[16,256,256]{2,1,0:T(8,128)(2,1)}, bf16[16,256,256]{2,1,0:T(8,128)(2,1)}, s32[16,128]{1,0:T(8,128)}, f32[16,256,256]{2,1,0:T(8,128)}) custom-call(bf16[256,256]{1,0:T(8,128)(2,1)} %get-tuple-element.45.refs_0_.refs_1_, bf16[256,256]{1,0:T(8,128)(2,1)} %get-tuple-element.46.refs_1_.refs_2_, bf16[16,256,256]{2,1,0:T(8,128)(2,1)} %copy-done.2, ...), custom_call_target="tpu_custom_call" | custom-call | flops 4294967296 | bytes 8388608 | tf_op jit(solution)/shard_map/pallas_call | solution.py:235
  89.3 2.2 %collective-permute-done.21.refs_19_ = bf16[4,528,256]{2,1,0:T(8,128)(2,1)S(1)} collective-permute-done((bf16[4,528,256]{2,1,0:T(8,128)(2,1)S(1)}, bf16[4,528,256]{2,1,0:T(8,128)(2,1)S(1)}, u32[]{:S(2)}, u32[]{:S(2)}) %collective-permute-start.21) | collective-permute-done | bytes 1081376 | tf_op jit(solution)/shard_map/ppermute | solution.py:42
  91.5 1.5 %collective-permute-done.22.refs_20_ = bf16[4,528,256]{2,1,0:T(8,128)(2,1)S(1)} collective-permute-done((bf16[4,528,256]{2,1,0:T(8,128)(2,1)S(1)}, bf16[4,528,256]{2,1,0:T(8,128)(2,1)S(1)}, u32[]{:S(2)}, u32[]{:S(2)}) %collective-permute-start.22) | collective-permute-done | bytes 1081376 | tf_op jit(solution)/shard_map/ppermute | solution.py:42
  94.0 46.6 %shard_map.87 = f32[1,1,256,256]{3,2,1,0:T(8,128)} custom-call(s32[2]{0:T(128)} %pad_add_fusion.site_ref.refs_0_, bf16[256,256]{1,0:T(8,128)(2,1)} %get-tuple-element.45.refs_0_.refs_1_, bf16[256,256]{1,0:T(8,128)(2,1)} %get-tuple-element.46.refs_1_.refs_2_, f32[16,256,256]{2,1,0:T(8,128)} %copy-done.1, f32[1,16,256,256]{3,2,1,0:T(8,128)} %refs_4_.1, ...), custom_call_target="tpu_custom_call" | custom-call | flops 16777216000 | bytes 25165824 | tf_op jit(solution)/shard_map/pallas_call | solution.py:422
  (93 shorter events, 14.9 us)
Async XLA Ops:
  2.1 8.9 %collective-permute-start.2 = (f32[2,256,256]{2,1,0:T(8,128)S(1)}, f32[2,256,256]{2,1,0:T(8,128)S(1)}, u32[]{:S(2)}, u32[]{:S(2)}) collective-permute-start(f32[2,256,256]{2,1,0:T(8,128)S(1)} %constant_dynamic-update-slice_fusion.own_ref), channel_id=1, source_target_pairs={{0,16},{16,0},{32,48},{48,32},{64,80},{80,64},{96,112},{112,96},{1... | collective-permute-start | bytes 1572872 | tf_op jit(solution)/shard_map/ppermute | solution.py:42
  2.8 6.5 %collective-permute-start = (bf16[1,528,256]{2,1,0:T(8,128)(2,1)S(1)}, bf16[1,528,256]{2,1,0:T(8,128)(2,1)S(1)}, u32[]{:S(2)}, u32[]{:S(2)}) collective-permute-start(bf16[1,528,256]{2,1,0:T(8,128)(2,1)S(1)} %get-tuple-element.64), channel_id=1, source_target_pairs={{0,4},{1,5},{2,6},{3,7},{4,0},{5,1},{6,2},{7,3},{8,12},{9,13},{10,... | collective-permute-start | bytes 811016 | tf_op jit(solution)/shard_map/ppermute | solution.py:38
  4.4 6.5 %collective-permute-start.1 = (bf16[1,528,256]{2,1,0:T(8,128)(2,1)S(1)}, bf16[1,528,256]{2,1,0:T(8,128)(2,1)S(1)}, u32[]{:S(2)}, u32[]{:S(2)}) collective-permute-start(bf16[1,528,256]{2,1,0:T(8,128)(2,1)S(1)} %get-tuple-element.63), channel_id=1, source_target_pairs={{0,1},{1,0},{2,3},{3,2},{4,5},{5,4},{6,7},{7,6},{8,9},{9,8},{10,11... | collective-permute-start | bytes 811016 | tf_op jit(solution)/shard_map/ppermute | solution.py:38
  14.1 13.7 %collective-permute-start.3 = (bf16[2,528,256]{2,1,0:T(8,128)(2,1)S(1)}, bf16[2,528,256]{2,1,0:T(8,128)(2,1)S(1)}, u32[]{:S(2)}, u32[]{:S(2)}) collective-permute-start(bf16[2,528,256]{2,1,0:T(8,128)(2,1)S(1)} %pad_maximum_fusion.1), channel_id=1, source_target_pairs={{0,1},{1,0},{2,3},{3,2},{4,5},{5,4},{6,7},{7,6},{8,9},{9,8},{10,11... | collective-permute-start | bytes 1622024 | tf_op jit(solution)/shard_map/ppermute | solution.py:38
  16.0 11.9 %collective-permute-start.4 = (bf16[2,528,256]{2,1,0:T(8,128)(2,1)S(1)}, bf16[2,528,256]{2,1,0:T(8,128)(2,1)S(1)}, u32[]{:S(2)}, u32[]{:S(2)}) collective-permute-start(bf16[2,528,256]{2,1,0:T(8,128)(2,1)S(1)} %pad_maximum_fusion.2), channel_id=1, source_target_pairs={{0,12},{1,13},{2,14},{3,15},{4,8},{5,9},{6,10},{7,11},{8,4},{9,5},... | collective-permute-start | bytes 1622024 | tf_op jit(solution)/shard_map/ppermute | solution.py:38
  18.1 9.9 %collective-permute-start.5 = (f32[256,256]{1,0:T(8,128)}, f32[256,256]{1,0:T(8,128)S(1)}, u32[]{:S(2)}, u32[]{:S(2)}) collective-permute-start(f32[256,256]{1,0:T(8,128)} %shard_map.82), channel_id=1, source_target_pairs={{0,32},{32,64},{64,96},{48,16},{80,48},{112,80},{1,33},{33,65},{65... | collective-permute-start | bytes 786440 | tf_op jit(solution)/shard_map/ppermute | solution.py:529
  21.6 9.0 %collective-permute-start.6 = (f32[256,256]{1,0:T(8,128)}, f32[256,256]{1,0:T(8,128)S(1)}, u32[]{:S(2)}, u32[]{:S(2)}) collective-permute-start(f32[256,256]{1,0:T(8,128)} %shard_map.82), channel_id=1, source_target_pairs={{0,64},{32,96},{80,16},{112,48},{1,65},{33,97},{81,17},{113,49},{2... | collective-permute-start | bytes 786440 | tf_op jit(solution)/shard_map/ppermute | solution.py:529
  26.4 5.5 %collective-permute-start.7 = (f32[256,256]{1,0:T(8,128)}, f32[256,256]{1,0:T(8,128)S(1)}, u32[]{:S(2)}, u32[]{:S(2)}) collective-permute-start(f32[256,256]{1,0:T(8,128)} %shard_map.82), channel_id=1, source_target_pairs={{0,96},{112,16},{1,97},{113,17},{2,98},{114,18},{3,99},{115,19},{4... | collective-permute-start | bytes 786440 | tf_op jit(solution)/shard_map/ppermute | solution.py:529
  32.0 8.6 %collective-permute-start.8 = (f32[3,256,256]{2,1,0:T(8,128)S(1)}, f32[3,256,256]{2,1,0:T(8,128)}, u32[]{:S(2)}, u32[]{:S(2)}) collective-permute-start(f32[3,256,256]{2,1,0:T(8,128)S(1)} %pad_maximum_fusion), channel_id=1, source_target_pairs={{0,16},{16,0},{32,48},{48,32},{64,80},{80,64},{96,112},{112,96},{1... | collective-permute-start | bytes 2359304 | tf_op jit(solution)/shard_map/ppermute | solution.py:42
  33.6 16.4 %collective-permute-start.9 = (bf16[4,528,256]{2,1,0:T(8,128)(2,1)S(1)}, bf16[4,528,256]{2,1,0:T(8,128)(2,1)S(1)}, u32[]{:S(2)}, u32[]{:S(2)}) collective-permute-start(bf16[4,528,256]{2,1,0:T(8,128)(2,1)S(1)} %constant_dynamic-update-slice_fusion.2.refs_3_), channel_id=1, source_target_pairs={{0,12},{1,13},{2,14},{3,15},{4,8},{5,9},{6,10},{7,11},{8,4},{9,5},... | collective-permute-start | bytes 3244040 | tf_op jit(solution)/shard_map/ppermute | solution.py:38
  34.6 16.5 %collective-permute-start.10 = (bf16[4,528,256]{2,1,0:T(8,128)(2,1)S(1)}, bf16[4,528,256]{2,1,0:T(8,128)(2,1)}, u32[]{:S(2)}, u32[]{:S(2)}) collective-permute-start(bf16[4,528,256]{2,1,0:T(8,128)(2,1)S(1)} %constant_dynamic-update-slice_fusion.4.refs_4_), channel_id=1, source_target_pairs={{0,3},{1,2},{2,1},{3,0},{4,7},{5,6},{6,5},{7,4},{8,11},{9,10},{10,... | collective-permute-start | bytes 3244040 | tf_op jit(solution)/shard_map/ppermute | solution.py:38
  44.6 6.5 %collective-permute-start.13 = (bf16[4,528,256]{2,1,0:T(8,128)(2,1)S(1)}, bf16[4,528,256]{2,1,0:T(8,128)(2,1)S(1)}, u32[]{:S(2)}, u32[]{:S(2)}) collective-permute-start(bf16[4,528,256]{2,1,0:T(8,128)(2,1)S(1)} %constant_dynamic-update-slice_fusion.2.refs_3_), channel_id=1, source_target_pairs={{0,16},{16,0},{32,48},{48,32},{64,80},{80,64},{96,112},{112,96},{1... | collective-permute-start | bytes 3244040 | tf_op jit(solution)/shard_map/ppermute | solution.py:42
  44.6 7.5 %collective-permute-start.14 = (bf16[4,528,256]{2,1,0:T(8,128)(2,1)S(1)}, bf16[4,528,256]{2,1,0:T(8,128)(2,1)S(1)}, u32[]{:S(2)}, u32[]{:S(2)}) collective-permute-start(bf16[4,528,256]{2,1,0:T(8,128)(2,1)S(1)} %constant_dynamic-update-slice_fusion.4.refs_4_), channel_id=1, source_target_pairs={{0,16},{16,0},{32,48},{48,32},{64,80},{80,64},{96,112},{112,96},{1... | collective-permute-start | bytes 3244040 | tf_op jit(solution)/shard_map/ppermute | solution.py:42
  45.1 17.5 %collective-permute-start.15 = (bf16[4,528,256]{2,1,0:T(8,128)(2,1)S(1)}, bf16[4,528,256]{2,1,0:T(8,128)(2,1)S(1)}, u32[]{:S(2)}, u32[]{:S(2)}) collective-permute-start(bf16[4,528,256]{2,1,0:T(8,128)(2,1)S(1)} %constant_dynamic-update-slice_fusion.2.refs_3_), channel_id=1, source_target_pairs={{0,3},{1,2},{2,1},{3,0},{4,7},{5,6},{6,5},{7,4},{8,11},{9,10},{10,... | collective-permute-start | bytes 3244040 | tf_op jit(solution)/shard_map/ppermute | solution.py:38
  49.9 25.1 %copy-start.15 = (bf16[4,528,256]{2,1,0:T(8,128)(2,1)}, bf16[4,528,256]{2,1,0:T(8,128)(2,1)S(1)}, u32[]{:S(2)}) copy-start(bf16[4,528,256]{2,1,0:T(8,128)(2,1)S(1)} %collective-permute-done.9.refs_3_) | copy-start | bytes 3244036
  49.9 25.1 %collective-permute-start.16 = (bf16[4,528,256]{2,1,0:T(8,128)(2,1)S(1)}, bf16[4,528,256]{2,1,0:T(8,128)(2,1)S(1)}, u32[]{:S(2)}, u32[]{:S(2)}) collective-permute-start(bf16[4,528,256]{2,1,0:T(8,128)(2,1)S(1)} %constant_dynamic-update-slice_fusion.4.refs_4_), channel_id=1, source_target_pairs={{0,4},{1,5},{2,6},{3,7},{4,0},{5,1},{6,2},{7,3},{8,12},{9,13},{10,... | collective-permute-start | bytes 3244040 | tf_op jit(solution)/shard_map/ppermute | solution.py:38
  51.1 24.1 %collective-permute-start.11 = (bf16[4,528,256]{2,1,0:T(8,128)(2,1)S(1)}, bf16[4,528,256]{2,1,0:T(8,128)(2,1)}, u32[]{:S(2)}, u32[]{:S(2)}) collective-permute-start(bf16[4,528,256]{2,1,0:T(8,128)(2,1)S(1)} %collective-permute-done.9.refs_3_), channel_id=1, source_target_pairs={{0,16},{16,0},{32,48},{48,32},{64,80},{80,64},{96,112},{112,96},{1... | collective-permute-start | bytes 3244040 | tf_op jit(solution)/shard_map/ppermute | solution.py:42
  51.1 24.6 %collective-permute-start.12 = (bf16[4,528,256]{2,1,0:T(8,128)(2,1)}, bf16[4,528,256]{2,1,0:T(8,128)(2,1)}, u32[]{:S(2)}, u32[]{:S(2)}) collective-permute-start(bf16[4,528,256]{2,1,0:T(8,128)(2,1)} %collective-permute-done.10.refs_4_), channel_id=1, source_target_pairs={{0,16},{16,0},{32,48},{48,32},{64,80},{80,64},{96,112},{112,96},{1... | collective-permute-start | bytes 3244040 | tf_op jit(solution)/shard_map/ppermute | solution.py:42
  52.1 36.5 %collective-permute-start.19 = (bf16[4,528,256]{2,1,0:T(8,128)(2,1)S(1)}, bf16[4,528,256]{2,1,0:T(8,128)(2,1)S(1)}, u32[]{:S(2)}, u32[]{:S(2)}) collective-permute-start(bf16[4,528,256]{2,1,0:T(8,128)(2,1)S(1)} %collective-permute-done.9.refs_3_), channel_id=1, source_target_pairs={{0,3},{1,2},{2,1},{3,0},{4,7},{5,6},{6,5},{7,4},{8,11},{9,10},{10,... | collective-permute-start | bytes 3244040 | tf_op jit(solution)/shard_map/ppermute | solution.py:38
  62.6 26.1 %collective-permute-start.20 = (bf16[4,528,256]{2,1,0:T(8,128)(2,1)}, bf16[4,528,256]{2,1,0:T(8,128)(2,1)S(1)}, u32[]{:S(2)}, u32[]{:S(2)}) collective-permute-start(bf16[4,528,256]{2,1,0:T(8,128)(2,1)} %collective-permute-done.10.refs_4_), channel_id=1, source_target_pairs={{0,4},{1,5},{2,6},{3,7},{4,0},{5,1},{6,2},{7,3},{8,12},{9,13},{10,... | collective-permute-start | bytes 3244040 | tf_op jit(solution)/shard_map/ppermute | solution.py:38
  75.1 14.2 %collective-permute-start.17 = (bf16[4,528,256]{2,1,0:T(8,128)(2,1)S(1)}, bf16[4,528,256]{2,1,0:T(8,128)(2,1)S(1)}, u32[]{:S(2)}, u32[]{:S(2)}) collective-permute-start(bf16[4,528,256]{2,1,0:T(8,128)(2,1)S(1)} %collective-permute-done.15.refs_13_), channel_id=1, source_target_pairs={{0,16},{16,0},{32,48},{48,32},{64,80},{80,64},{96,112},{112,96},{1... | collective-permute-start | bytes 3244040 | tf_op jit(solution)/shard_map/ppermute | solution.py:42
  75.2 14.1 %collective-permute-start.18 = (bf16[4,528,256]{2,1,0:T(8,128)(2,1)S(1)}, bf16[4,528,256]{2,1,0:T(8,128)(2,1)S(1)}, u32[]{:S(2)}, u32[]{:S(2)}) collective-permute-start(bf16[4,528,256]{2,1,0:T(8,128)(2,1)S(1)} %collective-permute-done.16.refs_14_), channel_id=1, source_target_pairs={{0,16},{16,0},{32,48},{48,32},{64,80},{80,64},{96,112},{112,96},{1... | collective-permute-start | bytes 3244040 | tf_op jit(solution)/shard_map/ppermute | solution.py:42
  88.7 2.8 %collective-permute-start.21 = (bf16[4,528,256]{2,1,0:T(8,128)(2,1)S(1)}, bf16[4,528,256]{2,1,0:T(8,128)(2,1)S(1)}, u32[]{:S(2)}, u32[]{:S(2)}) collective-permute-start(bf16[4,528,256]{2,1,0:T(8,128)(2,1)S(1)} %collective-permute-done.19.refs_17_), channel_id=1, source_target_pairs={{0,16},{16,0},{32,48},{48,32},{64,80},{80,64},{96,112},{112,96},{1... | collective-permute-start | bytes 3244040 | tf_op jit(solution)/shard_map/ppermute | solution.py:42
  88.9 4.2 %collective-permute-start.22 = (bf16[4,528,256]{2,1,0:T(8,128)(2,1)S(1)}, bf16[4,528,256]{2,1,0:T(8,128)(2,1)S(1)}, u32[]{:S(2)}, u32[]{:S(2)}) collective-permute-start(bf16[4,528,256]{2,1,0:T(8,128)(2,1)S(1)} %collective-permute-done.20.refs_18_), channel_id=1, source_target_pairs={{0,16},{16,0},{32,48},{48,32},{64,80},{80,64},{96,112},{112,96},{1... | collective-permute-start | bytes 3244040 | tf_op jit(solution)/shard_map/ppermute | solution.py:42
  (24 other events, 128.8 us)

commit v3 on v2

--- a/solution.py
+++ b/solution.py
@@ -1,3 +1,5 @@
+import functools
+
 import jax
 import jax.numpy as jnp
 from jax import lax
@@ -23,9 +25,10 @@
     ((XB, ZB, XA, ZA), (ZB, XA, ZA, XB)),
 )
 
+LIGHT = pl.CostEstimate(flops=1, bytes_accessed=1, transcendentals=0)
 SMEM = pl.BlockSpec(memory_space=pltpu.SMEM)
 VMEM = pl.BlockSpec(memory_space=pltpu.VMEM)
-HBM = pl.BlockSpec(memory_space=pltpu.HBM)
+HBM = pl.BlockSpec(memory_space=pl.ANY)
 
 
 def swap_op(value, part, stage):
@@ -64,11 +67,11 @@
     return jnp.where(rows == cols, 1.0, 0.0).astype(F32)
 
 
-def pair_kernel(site_ref, own_ref, other_ref, out_ref):
+def pair_kernel(site_ref, own_left, own_right, other_left, other_right, out_ref):
     eye = identity()
     first = site_ref[0] % 2 == 0
-    a = jnp.where(first, own_ref[0], other_ref[1])
-    b = jnp.where(first, other_ref[0], own_ref[1])
+    a = jnp.where(first, own_left[...], other_right[...])
+    b = jnp.where(first, other_left[...], own_right[...])
     out_ref[...] = dot_high(eye + 0.3 * a, eye + 0.3 * b)
 
 
@@ -76,25 +79,25 @@
     return pl.pallas_call(
         pair_kernel,
         out_shape=jax.ShapeDtypeStruct((BLK, BLK), F32),
-        in_specs=[SMEM, VMEM, VMEM],
+        in_specs=[SMEM] + [VMEM] * 4,
         out_specs=VMEM,
-        cost_estimate=pl.CostEstimate(flops=12 * BLK**3, bytes_accessed=MIB, transcendentals=0),
-    )(site, own, other)
-
-
-def chain_kernel(site_ref, other_ref, m1, m2, m3, across, lq_ref, rq_ref):
+        cost_estimate=LIGHT,
+    )(site, *own, *other)
+
+
+def chain_kernel(site_ref, other_left, other_right, m1, m2, m3, n1, n2, n3, lq_ref, rq_ref):
     eye = identity()
     site = site_ref[0]
     core, y = site % 2, site // 2
-    own = (m1, m2, m3)
+    own, across = (m1, m2, m3), (n1, n2, n3)
     lefts, rights = [], []
     for k in range(3):
-        left = jnp.where(core == 0, own[k][...], across[k])
-        right = jnp.where(core == 0, across[k], own[k][...])
+        left = jnp.where(core == 0, own[k][...], across[k][...])
+        right = jnp.where(core == 0, across[k][...], own[k][...])
         lefts.append(jnp.where(y >= k + 1, left, eye))
         rights.append(jnp.where(y + k + 1 <= 3, right, eye))
-    s_part = jnp.where(core == 1, eye + 0.3 * other_ref[0], eye)
-    t_part = jnp.where(core == 0, eye + 0.3 * other_ref[1], eye)
+    s_part = jnp.where(core == 1, eye + 0.3 * other_left[...], eye)
+    t_part = jnp.where(core == 0, eye + 0.3 * other_right[...], eye)
     a = dot_high(lefts[2], lefts[1])
     b = dot_high(lefts[0], s_part)
     c = dot_high(t_part, rights[0])
@@ -108,10 +111,10 @@
     return pl.pallas_call(
         chain_kernel,
         out_shape=(out, out),
-        in_specs=[SMEM] + [VMEM] * 5,
+        in_specs=[SMEM] + [VMEM] * 8,
         out_specs=(VMEM, VMEM),
-        cost_estimate=pl.CostEstimate(flops=72 * BLK**3, bytes_accessed=2 * MIB, transcendentals=0),
-    )(site, other, *received, across)
+        cost_estimate=LIGHT,
+    )(site, *other, *received, *across)
 
 
 UNROLL = 4
@@ -183,13 +186,13 @@
         h_in, rest = rest[0], rest[1:]
     left_out, right_out, table_out, h_out = rest[:4]
     lbuf, rbuf, tails, table_v, table, vb, hv, sems, out_sems = rest[4:]
-    load_terms(groups, lbuf, rbuf, tails, sems)
     start = pltpu.make_async_copy(vb_hbm, vb, sems.at[3 * count])
     start.start()
     if carried:
         before = pltpu.make_async_copy(h_in, hv, sems.at[3 * count + 1])
         before.start()
-    else:
+    load_terms(groups, lbuf, rbuf, tails, sems)
+    if not carried:
         def clear(b, carry):
             hv[b] = jnp.zeros((BLK, BLK), F32)
             return carry
@@ -253,10 +256,8 @@
             pltpu.SemaphoreType.DMA((3 * count + 3,)),
             pltpu.SemaphoreType.DMA((2 * count + 2,)),
         ],
-        compiler_params=pltpu.CompilerParams(vmem_limit_bytes=56 * MIB),
-        cost_estimate=pl.CostEstimate(
-            flops=terms * 16 * BLK**3, bytes_accessed=terms * 8 * BLK * BLK, transcendentals=0
-        ),
+        compiler_params=pltpu.CompilerParams(vmem_limit_bytes=18 * MIB),
+        cost_estimate=LIGHT,
     )(lq, rq, vb, *groups, *((h_in,) if carried else ()))
 
 
@@ -268,26 +269,28 @@
     return jnp.sum(jnp.sum(acc, axis=0, keepdims=True), axis=1, keepdims=True)
 
 
-def solve_kernel(count, sizes, ids, lq_ref, rq_ref, x_hbm, diag_hbm, vb_hbm, h_hbm, *rest):
+def solve_kernel(count, sizes, ids, lq_ref, rq_ref, scale_ref, psi_hbm, diag_hbm, vb_hbm, h_hbm, *rest):
     tables, rest = rest[: len(sizes)], rest[len(sizes):]
     envs, rest = rest[: 2 * len(sizes)], rest[2 * len(sizes):]
     groups, rest = rest[:count], rest[count:]
     out_ref = rest[0]
-    lbuf, rbuf, tails, table_v, table, xv, hv, tv, gv, dv, vb, sems, in_sems = rest[1:]
+    lbuf, rbuf, tails, table_v, table, xv, hv, tv, gv, dv, vb, psi, sems, in_sems = rest[1:]
     op = ids[1]
     zero = jnp.zeros((8, BLK), F32)
 
     def over_blocks(step, sums):
         return lax.fori_loop(0, NB, step, (zero,) * sums)
 
-    load_terms(groups, lbuf, rbuf, tails, sems)
     vectors = [
         pltpu.make_async_copy(source, target, in_sems.at[i])
         for i, (source, target) in enumerate(
-            ((vb_hbm, vb), (h_hbm, hv), (x_hbm, xv), (diag_hbm.at[0], dv))
+            ((vb_hbm, vb), (h_hbm, hv), (psi_hbm.at[0], psi), (diag_hbm.at[0], dv))
         )
     ]
-    for copy in vectors:
+    for copy in vectors[:2]:
+        copy.start()
+    load_terms(groups, lbuf, rbuf, tails, sems)
+    for copy in vectors[2:]:
         copy.start()
     built = []
     begin = 4 * count
@@ -312,47 +315,46 @@
     vectors[2].wait()
     vectors[3].wait()
 
+    start_scale = scale_ref[0:1, 0:1]
+
     def finish_h(b, sums):
-        x = xv[b]
+        x = psi[b].astype(F32) * start_scale
         h = hv[b] + dv[b] * x
+        xv[b] = x
         hv[b] = h
         return (sums[0] + fold(x * h),)
 
     (theta_sum,) = over_blocks(finish_h, 1)
     theta = total(theta_sum)
 
-    def correction(theta):
-        def residual(b, sums):
-            x = xv[b]
-            t = (hv[b] - theta * x) / dv[b]
-            tv[b] = t
-            return (sums[0] + fold(x * t),)
-
-        (along,) = over_blocks(residual, 1)
-        along = total(along)
-
-        def orthogonal(b, sums):
-            t = tv[b] - along * xv[b]
-            tv[b] = t
-            return (sums[0] + fold(t * t),)
-
-        (size,) = over_blocks(orthogonal, 1)
-        return lax.rsqrt(total(size) + 1e-12)
+    def residual(b, sums):
+        x = xv[b]
+        t = (hv[b] - theta * x) / dv[b]
+        tv[b] = t
+        return (sums[0] + fold(x * t),)
+
+    (along,) = over_blocks(residual, 1)
+
+    def orthogonal(along, b, sums):
+        t = tv[b] - along * xv[b]
+        tv[b] = t
+        return (sums[0] + fold(t * t),)
 
     def rotation(theta, b, c):
         low = (c - theta) / 2 + jnp.sqrt(((theta - c) / 2) ** 2 + b * b)
         inv = 1.0 / jnp.sqrt(low * low + b * b)
         return low * inv, b * inv
 
-    def over_terms(step, value):
+    def over_terms(step, value, unroll=UNROLL):
         def some(i, value):
-            spots = [i * UNROLL + u for u in range(UNROLL)]
+            spots = [i * unroll + u for u in range(unroll)]
             return step([(table[k, 0], table[k, 1]) for k in spots], spots, value)
 
-        return lax.fori_loop(0, 64 // UNROLL, some, value)
+        return lax.fori_loop(0, 64 // unroll, some, value)
 
     for step in range(ITERS - 1):
-        scale_t = correction(theta)
+        (size,) = over_blocks(functools.partial(orthogonal, total(along)), 1)
+        scale_t = lax.rsqrt(total(size) + 1e-12)
 
         def unit(b, sums):
             t = tv[b] * scale_t
@@ -374,22 +376,27 @@
 
         def couplings(b, sums):
             g = gv[b]
-            return (sums[0] + fold(xv[b] * g), sums[1] + fold(tv[b] * g))
-
-        cross, curve = over_blocks(couplings, 2)
-        keep, move = rotation(theta, total(cross), total(curve))
-
-        def update(b, sums):
+            t = tv[b]
+            return (sums[0] + fold(xv[b] * g), sums[1] + fold(t * g), sums[2] + fold(t * hv[b]))
+
+        sums = over_blocks(couplings, 3)
+        cross, curve, back = (total(v) for v in sums)
+        keep, move = rotation(theta, cross, curve)
+        theta = keep * keep * theta - keep * move * (cross + back) + move * move * curve
+
+        def turn(keep, move, theta, b, sums):
             x = keep * xv[b] - move * tv[b]
             h = keep * hv[b] - move * gv[b]
             xv[b] = x
             hv[b] = h
-            return (sums[0] + fold(x * h),)
-
-        (theta_sum,) = over_blocks(update, 1)
-        theta = total(theta_sum)
-
-    scale_t = correction(theta)
+            t = (h - theta * x) / dv[b]
+            tv[b] = t
+            return (sums[0] + fold(x * t),)
+
+        (along,) = over_blocks(functools.partial(turn, keep, move, theta), 1)
+
+    (size,) = over_blocks(functools.partial(orthogonal, total(along)), 1)
+    scale_t = lax.rsqrt(total(size) + 1e-12)
 
     def last_unit(b, sums):
         t = tv[b] * scale_t
@@ -405,14 +412,14 @@
             acc = acc + fold(tv[d] * dot(lbuf[k], f))
         return acc
 
-    curve_terms = over_terms(last_step, zero)
+    curve_terms = over_terms(last_step, zero, 2 * UNROLL)
     curve = total(curve_diag) + 2.0 * total(curve_terms)
     keep, move = rotation(theta, total(cross), curve)
     amplitude = float(NB * BLK * BLK) ** 0.5
     out_ref[0, 0] = (keep * xv[op] - move * tv[op]) * amplitude
 
 
-def solve(ids, parts, lq, rq, x, diagonal, vb, h, groups):
+def solve(ids, parts, lq, rq, scale, psi, diagonal, vb, h, groups):
     count = len(groups)
     sizes = tuple(p[0].shape[0] for p in parts)
 
@@ -422,7 +429,7 @@
     return pl.pallas_call(
         kernel,
         out_shape=jax.ShapeDtypeStruct((1, 1, BLK, BLK), F32),
-        in_specs=[SMEM, VMEM, VMEM] + [HBM] * (4 + 3 * len(sizes) + count),
+        in_specs=[SMEM] + [VMEM] * 3 + [HBM] * (4 + 3 * len(sizes) + count),
         out_specs=VMEM,
         scratch_shapes=[
             pltpu.VMEM((64, BLK, BLK), BF16),
@@ -436,18 +443,18 @@
             pltpu.VMEM(FULL, F32),
             pltpu.VMEM(FULL, F32),
             pltpu.VMEM(FULL, BF16),
+            pltpu.VMEM(FULL, BF16),
             pltpu.SemaphoreType.DMA((3 * count + 1,)),
             pltpu.SemaphoreType.DMA((4 + 3 * len(sizes),)),
         ],
-        compiler_params=pltpu.CompilerParams(vmem_limit_bytes=56 * MIB),
-        cost_estimate=pl.CostEstimate(
-            flops=2 * 500 * BLK**3, bytes_accessed=24 * MIB, transcendentals=0
-        ),
+        compiler_params=pltpu.CompilerParams(vmem_limit_bytes=46 * MIB),
+        cost_estimate=LIGHT,
     )(
         ids,
         lq,
         rq,
-        x,
+        scale,
+        psi,
         diagonal,
         vb,
         h,
@@ -457,44 +464,33 @@
     )
 
 
-def start_kernel(psi_ref, x_hbm, vb_hbm, xv, vb, sems):
+def start_kernel(psi_ref, vb_ref, scale_ref):
     def square(b, acc):
         v = psi_ref[0, b].astype(F32)
         return acc + fold(v * v)
 
     norm = lax.fori_loop(0, NB, square, jnp.zeros((8, BLK), F32))
     scale = lax.rsqrt(total(norm) + 1e-12)
+    scale_ref[...] = jnp.broadcast_to(scale, (8, 128))
 
     def unit(b, carry):
-        v = psi_ref[0, b].astype(F32) * scale
-        xv[b] = v
-        vb[b] = v.astype(BF16)
+        vb_ref[b] = (psi_ref[0, b].astype(F32) * scale).astype(BF16)
         return carry
 
     lax.fori_loop(0, NB, unit, 0)
-    copies = (
-        pltpu.make_async_copy(xv, x_hbm, sems.at[0]),
-        pltpu.make_async_copy(vb, vb_hbm, sems.at[1]),
-    )
-    for copy in copies:
-        copy.start()
-    for copy in copies:
-        copy.wait()
 
 
 def start_vector(psi):
     return pl.pallas_call(
         start_kernel,
-        out_shape=(jax.ShapeDtypeStruct(FULL, F32), jax.ShapeDtypeStruct(FULL, BF16)),
+        out_shape=(
+            jax.ShapeDtypeStruct(FULL, BF16),
+            jax.ShapeDtypeStruct((8, 128), F32),
+        ),
         in_specs=[VMEM],
-        out_specs=(HBM, HBM),
-        scratch_shapes=[
-            pltpu.VMEM(FULL, F32),
-            pltpu.VMEM(FULL, BF16),
-            pltpu.SemaphoreType.DMA((2,)),
-        ],
-        compiler_params=pltpu.CompilerParams(vmem_limit_bytes=20 * MIB),
-        cost_estimate=pl.CostEstimate(flops=8 * MIB, bytes_accessed=12 * MIB, transcendentals=0),
+        out_specs=(VMEM, VMEM),
+        compiler_params=pltpu.CompilerParams(vmem_limit_bytes=8 * MIB),
+        cost_estimate=LIGHT,
     )(psi)
 
 
@@ -514,9 +510,9 @@
     mine = lax.dynamic_slice_in_dim(whole, 2 * core, 2, 0)
     parts = (mine[:1], mine[1:])
 
-    steps = jnp.concatenate([left_step, right_step], 0)
     first = [swap_op(p, i, 0) for i, p in enumerate(parts)]
-    other = swap_core(steps)
+    steps = (left_step[0], right_step[0])
+    other = tuple(swap_core(step) for step in steps)
     product = pair_product(ids, steps, other)
 
     two = [jnp.concatenate(pair, 0) for pair in zip(parts, first)]
@@ -527,25 +523,25 @@
         pairs = [(2 * y, 2 * (y + k)) for y in range(4 - k)]
         pairs += [(2 * y + 1, 2 * (y - k) + 1) for y in range(k, 4)]
         received.append(lax.ppermute(product, "site", pairs))
+    across = [swap_core(r) for r in received]
 
     four = [jnp.concatenate(pair, 0) for pair in zip(two, second)]
     third = [swap_op(p, i, 2) for i, p in enumerate(four)]
-    received, (psi,) = lax.optimization_barrier((received, after((psi,), four)))
-    across = swap_core(jnp.stack(received))
-    x, vb = start_vector(psi)
+    psi, received, across = after((psi, tuple(received), tuple(across)), four)
+    vb, scale = start_vector(psi)
     lq, rq = chain_products(ids, other, received, across)
-    four, (lq, rq, vb) = lax.optimization_barrier((four, (lq, rq, vb)))
     old = [swap_op(p, i, 3) for i, p in enumerate(four)]
-    new = [swap_op(p, i, 3) for i, p in enumerate(third)]
 
     def both(groups):
         return list(groups) + [swap_core(g) for g in groups]
 
     built = [part(both(four), lq, rq, vb, None)]
+    third = after(third, built[-1][3:])
+    new = [swap_op(p, i, 3) for i, p in enumerate(third)]
     old = after(old, built[-1][3:])
     built.append(part(both(third), lq, rq, vb, built[-1][3]))
     new = after(new, built[-1][3:])
-    return solve(ids, built, lq, rq, x, diagonal, vb, built[-1][3], both(old) + both(new))
+    return solve(ids, built, lq, rq, scale, psi, diagonal, vb, built[-1][3], both(old) + both(new))
 
 
 def solution(mesh):

time: 142 us -> 128 us (0.901)
  waiting for transfers between devices: 24.3 us -> 12 us
  Pallas kernels: 79.1 us -> 69.3 us
  local copies, waits for them, and re-layouts: 8.36 us -> 13.5 us
  other arithmetic: 0.86 us -> 2.56 us
  starting transfers between devices: 27.6 us -> 29.3 us
    ppermute x10, waiting for transfers between devices: 16.7 us -> 5.84 us  [swap_op(): return lax.ppermute(value, ('site', 'op'), pairs)]
    pallas_call x2, Pallas kernels: 24.7 us -> 17.6 us  [part(): pl.pallas_call(kernel, out_shape=(env, env, jax.ShapeDtypeStruct((terms,...]
    unnamed x53 -> x50, local copies, waits for them, and re-layouts: 7.17 us -> 12.5 us
    pallas_call x1, Pallas kernels: 46.6 us -> 43.8 us  [solve(): pl.pallas_call(kernel, out_shape=jax.ShapeDtypeStruct((1, 1, BLK, BLK), F...]
    ppermute x10 -> x13, starting transfers between devices: 3.84 us -> 5.78 us  [swap_core(): return lax.ppermute(value, 'site', [(i, i ^ 1) for i in range(8)])]
    ppermute x3, waiting for transfers between devices: 3.92 us -> 2.43 us  [body(): received.append(lax.ppermute(product, 'site', pairs))]
    ppermute x10 -> x13, waiting for transfers between devices: 3.74 us -> 3.76 us  [swap_core(): return lax.ppermute(value, 'site', [(i, i ^ 1) for i in range(8)])]
  transfers between devices with their start and end apart: 23 -> 26, of which waited for: 9 -> 6; matrix products, arithmetic and copies ran while one was open for 1% -> 2% of each run, Pallas kernels for 21% -> 20%
where the time goes in v3:
time: 128 us; the launch traced here: 127 us
  Pallas kernels  69.3 us (54%)
  starting transfers between devices  29.3 us (23%)
  local copies, waits for them, and re-layouts  13.5 us (11%)
  waiting for transfers between devices  12 us (9%)
  other arithmetic  2.56 us (2%)
    pallas_call x1, Pallas kernels, solve(): pl.pallas_call(kernel, out_shape=jax.ShapeDtypeStruct((1, 1, BLK, BLK), F...  43.8 us
    pallas_call x2, Pallas kernels, part(): pl.pallas_call(kernel, out_shape=(env, env, jax.ShapeDtypeStruct((terms,...  17.6 us
    ppermute x10, starting transfers between devices, swap_op(): return lax.ppermute(value, ('site', 'op'), pairs)  13.9 us
    unnamed x50, local copies, waits for them, and re-layouts  12.5 us
    ppermute x3, starting transfers between devices, body(): received.append(lax.ppermute(product, 'site', pairs))  9.6 us
    ppermute x10, waiting for transfers between devices, swap_op(): return lax.ppermute(value, ('site', 'op'), pairs)  5.84 us
    ppermute x13, starting transfers between devices, swap_core(): return lax.ppermute(value, 'site', [(i, i ^ 1) for i in range(8)])  5.78 us
    pallas_call x1, Pallas kernels, chain_products(): pl.pallas_call(chain_kernel, out_shape=(out, out), in_specs=[SMEM] + [VME...  4.74 us
  transfers between devices with their start and end apart: 26, of which 6 were waited for; matrix products, arithmetic and copies ran while one was open for 2% of the time, Pallas kernels for 20%

profile of v3, /device:TPU:0, one launch (start us, length us, event | category | flops | bytes accessed | tf_op | source)
XLA Modules:
  0.0 127.1 jit_solution(9495669250768998460)
XLA Ops:
  2.0 1.7 %collective-permute-start.2 = (bf16[1,528,256]{2,1,0:T(8,128)(2,1)S(1)}, bf16[1,528,256]{2,1,0:T(8,128)(2,1)S(1)}, u32[]{:S(2)}, u32[]{:S(2)}) collective-permute-start(bf16[1,528,256]{2,1,0:T(8,128)(2,1)S(1)} %get-tuple-element.62), channel_id=1, source_target_pairs={{0,4},{1,5},{2,6},{3,7},{4,0},{5,1},{6,2},{7,3},{8,12},{9,13},{10,... | collective-permute-start | bytes 811016 | tf_op jit(solution)/shard_map/ppermute | solution.py:41
  4.5 1.9 %collective-permute-start.3 = (bf16[1,528,256]{2,1,0:T(8,128)(2,1)S(1)}, bf16[1,528,256]{2,1,0:T(8,128)(2,1)S(1)}, u32[]{:S(2)}, u32[]{:S(2)}) collective-permute-start(bf16[1,528,256]{2,1,0:T(8,128)(2,1)S(1)} %get-tuple-element.61), channel_id=1, source_target_pairs={{0,1},{1,0},{2,3},{3,2},{4,5},{5,4},{6,7},{7,6},{8,9},{9,8},{10,11... | collective-permute-start | bytes 811016 | tf_op jit(solution)/shard_map/ppermute | solution.py:41
  8.5 2.3 %shard_map.82 = f32[256,256]{1,0:T(8,128)} custom-call(s32[2]{0:T(128)} %pad_add_fusion.site_ref.refs_0_, f32[256,256]{1,0:T(8,128)} %bitcast.8, f32[256,256]{1,0:T(8,128)} %bitcast.10, f32[256,256]{1,0:T(8,128)} %copy-done.13, f32[256,256]{1,0:T(8,128)} %copy-done.14), custom_call_target="tpu_custom_call" | custom-call | flops 1 | bytes 1 | tf_op jit(solution)/shard_map/pallas_call | solution.py:79
  11.1 2.0 %collective-permute-start.10 = (bf16[2,528,256]{2,1,0:T(8,128)(2,1)S(1)}, bf16[2,528,256]{2,1,0:T(8,128)(2,1)S(1)}, u32[]{:S(2)}, u32[]{:S(2)}) collective-permute-start(bf16[2,528,256]{2,1,0:T(8,128)(2,1)S(1)} %pad_maximum_fusion), channel_id=1, source_target_pairs={{0,1},{1,0},{2,3},{3,2},{4,5},{5,4},{6,7},{7,6},{8,9},{9,8},{10,11... | collective-permute-start | bytes 1622024 | tf_op jit(solution)/shard_map/ppermute | solution.py:41
  13.1 1.7 %collective-permute-start.11 = (bf16[2,528,256]{2,1,0:T(8,128)(2,1)S(1)}, bf16[2,528,256]{2,1,0:T(8,128)(2,1)S(1)}, u32[]{:S(2)}, u32[]{:S(2)}) collective-permute-start(bf16[2,528,256]{2,1,0:T(8,128)(2,1)S(1)} %pad_maximum_fusion.1), channel_id=1, source_target_pairs={{0,12},{1,13},{2,14},{3,15},{4,8},{5,9},{6,10},{7,11},{8,4},{9,5},... | collective-permute-start | bytes 1622024 | tf_op jit(solution)/shard_map/ppermute | solution.py:41
  14.8 3.5 %collective-permute-start.4 = (f32[256,256]{1,0:T(8,128)S(1)}, f32[256,256]{1,0:T(8,128)S(1)}, u32[]{:S(2)}, u32[]{:S(2)}) collective-permute-start(f32[256,256]{1,0:T(8,128)S(1)} %copy-done.23), channel_id=1, source_target_pairs={{0,32},{32,64},{64,96},{48,16},{80,48},{112,80},{1,33},{33,65},{65... | collective-permute-start | bytes 786440 | tf_op jit(solution)/shard_map/ppermute | solution.py:525
  18.3 4.8 %collective-permute-start.5 = (f32[256,256]{1,0:T(8,128)S(1)}, f32[256,256]{1,0:T(8,128)S(1)}, u32[]{:S(2)}, u32[]{:S(2)}) collective-permute-start(f32[256,256]{1,0:T(8,128)S(1)} %copy-done.23), channel_id=1, source_target_pairs={{0,64},{32,96},{80,16},{112,48},{1,65},{33,97},{81,17},{113,49},{2... | collective-permute-start | bytes 786440 | tf_op jit(solution)/shard_map/ppermute | solution.py:525
  23.1 1.3 %collective-permute-start.6 = (f32[256,256]{1,0:T(8,128)S(1)}, f32[256,256]{1,0:T(8,128)S(1)}, u32[]{:S(2)}, u32[]{:S(2)}) collective-permute-start(f32[256,256]{1,0:T(8,128)S(1)} %copy-done.23), channel_id=1, source_target_pairs={{0,96},{112,16},{1,97},{113,17},{2,98},{114,18},{3,99},{115,19},{4... | collective-permute-start | bytes 786440 | tf_op jit(solution)/shard_map/ppermute | solution.py:525
  24.5 2.4 %collective-permute-done.5.m2 = f32[256,256]{1,0:T(8,128)S(1)} collective-permute-done((f32[256,256]{1,0:T(8,128)S(1)}, f32[256,256]{1,0:T(8,128)S(1)}, u32[]{:S(2)}, u32[]{:S(2)}) %collective-permute-start.5) | collective-permute-done | bytes 262176 | tf_op jit(solution)/shard_map/ppermute | solution.py:525
  28.2 1.3 %collective-permute-start.9 = (f32[256,256]{1,0:T(8,128)S(1)}, f32[256,256]{1,0:T(8,128)S(1)}, u32[]{:S(2)}, u32[]{:S(2)}) collective-permute-start(f32[256,256]{1,0:T(8,128)S(1)} %collective-permute-done.6.m3), channel_id=1, source_target_pairs={{0,16},{16,0},{32,48},{48,32},{64,80},{80,64},{96,112},{112,96},{1... | collective-permute-start | bytes 786440 | tf_op jit(solution)/shard_map/ppermute | solution.py:45
  31.9 2.3 %collective-permute-start.12 = (bf16[4,528,256]{2,1,0:T(8,128)(2,1)S(1)}, bf16[4,528,256]{2,1,0:T(8,128)(2,1)}, u32[]{:S(2)}, u32[]{:S(2)}) collective-permute-start(bf16[4,528,256]{2,1,0:T(8,128)(2,1)S(1)} %constant_dynamic-update-slice_fusion.refs_3_), channel_id=1, source_target_pairs={{0,12},{1,13},{2,14},{3,15},{4,8},{5,9},{6,10},{7,11},{8,4},{9,5},... | collective-permute-start | bytes 3244040 | tf_op jit(solution)/shard_map/ppermute | solution.py:41
  34.8 2.8 %collective-permute-start.18 = (bf16[4,528,256]{2,1,0:T(8,128)(2,1)S(1)}, bf16[4,528,256]{2,1,0:T(8,128)(2,1)}, u32[]{:S(2)}, u32[]{:S(2)}) collective-permute-start(bf16[4,528,256]{2,1,0:T(8,128)(2,1)S(1)} %constant_dynamic-update-slice_fusion.refs_3_), channel_id=1, source_target_pairs={{0,3},{1,2},{2,1},{3,0},{4,7},{5,6},{6,5},{7,4},{8,11},{9,10},{10,... | collective-permute-start | bytes 3244040 | tf_op jit(solution)/shard_map/ppermute | solution.py:41
  38.4 4.7 %shard_map.83 = (bf16[256,256]{1,0:T(8,128)(2,1)}, bf16[256,256]{1,0:T(8,128)(2,1)}) custom-call(s32[2]{0:T(128)} %pad_add_fusion.site_ref.refs_0_, f32[256,256]{1,0:T(8,128)} %copy-done.13, f32[256,256]{1,0:T(8,128)} %copy-done.14, f32[256,256]{1,0:T(8,128)} %copy-done.17, f32[256,256]{1,0:T(8,128)} %copy-done.18, f32[256,256]{1,0:T(8,128)} %copy-done.19, ...), custom_call_target="tpu_custom_call" | custom-call | flops 1 | bytes 1 | tf_op jit(solution)/shard_map/pallas_call | solution.py:111
  45.0 8.7 %shard_map.85 = (bf16[16,256,256]{2,1,0:T(8,128)(2,1)S(1)}, bf16[16,256,256]{2,1,0:T(8,128)(2,1)S(1)}, s32[16,128]{1,0:T(8,128)S(1)}, f32[16,256,256]{2,1,0:T(8,128)S(1)}) custom-call(bf16[256,256]{1,0:T(8,128)(2,1)S(1)} %copy-done.7, bf16[256,256]{1,0:T(8,128)(2,1)S(1)} %copy-done.9, bf16[16,256,256]{2,1,0:T(8,128)(2,1)S(1)} %get-tuple-element.46.refs_2_.refs_6_, ...), custom_call_target="tpu_custom_call" | custom-call | flops 1 | bytes 1 | tf_op jit(solution)/shard_map/pallas_call | solution.py:238
  53.7 1.4 %copy-done.3 = bf16[16,256,256]{2,1,0:T(8,128)(2,1)} copy-done((bf16[16,256,256]{2,1,0:T(8,128)(2,1)}, bf16[16,256,256]{2,1,0:T(8,128)(2,1)S(1)}, u32[]{:S(2)}) %copy-start.3) | copy-done | bytes 2097176
  55.1 1.3 %copy-done.4 = bf16[16,256,256]{2,1,0:T(8,128)(2,1)} copy-done((bf16[16,256,256]{2,1,0:T(8,128)(2,1)}, bf16[16,256,256]{2,1,0:T(8,128)(2,1)S(1)}, u32[]{:S(2)}) %copy-start.4) | copy-done | bytes 2097176
  58.0 4.5 %collective-permute-done.18.refs_14_ = bf16[4,528,256]{2,1,0:T(8,128)(2,1)} collective-permute-done((bf16[4,528,256]{2,1,0:T(8,128)(2,1)S(1)}, bf16[4,528,256]{2,1,0:T(8,128)(2,1)}, u32[]{:S(2)}, u32[]{:S(2)}) %collective-permute-start.18) | collective-permute-done | bytes 1081376 | tf_op jit(solution)/shard_map/ppermute | solution.py:41
  63.0 8.9 %shard_map.86 = (bf16[16,256,256]{2,1,0:T(8,128)(2,1)S(1)}, bf16[16,256,256]{2,1,0:T(8,128)(2,1)S(1)}, s32[16,128]{1,0:T(8,128)S(1)}, f32[16,256,256]{2,1,0:T(8,128)S(1)}) custom-call(bf16[256,256]{1,0:T(8,128)(2,1)S(1)} %copy-done.7, bf16[256,256]{1,0:T(8,128)(2,1)S(1)} %copy-done.9, bf16[16,256,256]{2,1,0:T(8,128)(2,1)S(1)} %get-tuple-element.46.refs_2_.refs_6_, ...), custom_call_target="tpu_custom_call" | custom-call | flops 1 | bytes 1 | tf_op jit(solution)/shard_map/pallas_call | solution.py:238
  71.9 2.0 %copy-done.2 = f32[16,256,256]{2,1,0:T(8,128)} copy-done((f32[16,256,256]{2,1,0:T(8,128)}, f32[16,256,256]{2,1,0:T(8,128)S(1)}, u32[]{:S(2)}) %copy-start.2) | copy-done | bytes 4194328
  73.9 1.4 %copy-done.5 = bf16[16,256,256]{2,1,0:T(8,128)(2,1)} copy-done((bf16[16,256,256]{2,1,0:T(8,128)(2,1)}, bf16[16,256,256]{2,1,0:T(8,128)(2,1)S(1)}, u32[]{:S(2)}) %copy-start.5) | copy-done | bytes 2097176
  75.3 1.3 %copy-done.6 = bf16[16,256,256]{2,1,0:T(8,128)(2,1)} copy-done((bf16[16,256,256]{2,1,0:T(8,128)(2,1)}, bf16[16,256,256]{2,1,0:T(8,128)(2,1)S(1)}, u32[]{:S(2)}) %copy-start.6) | copy-done | bytes 2097176
  78.4 2.2 %collective-permute-done.24.refs_20_ = bf16[4,528,256]{2,1,0:T(8,128)(2,1)S(1)} collective-permute-done((bf16[4,528,256]{2,1,0:T(8,128)(2,1)S(1)}, bf16[4,528,256]{2,1,0:T(8,128)(2,1)S(1)}, u32[]{:S(2)}, u32[]{:S(2)}) %collective-permute-start.24) | collective-permute-done | bytes 1081376 | tf_op jit(solution)/shard_map/ppermute | solution.py:45
  80.5 1.5 %collective-permute-done.25.refs_21_ = bf16[4,528,256]{2,1,0:T(8,128)(2,1)S(1)} collective-permute-done((bf16[4,528,256]{2,1,0:T(8,128)(2,1)S(1)}, bf16[4,528,256]{2,1,0:T(8,128)(2,1)S(1)}, u32[]{:S(2)}, u32[]{:S(2)}) %collective-permute-start.25) | collective-permute-done | bytes 1081376 | tf_op jit(solution)/shard_map/ppermute | solution.py:45
  83.1 43.8 %shard_map.87 = f32[1,1,256,256]{3,2,1,0:T(8,128)} custom-call(s32[2]{0:T(128)S(1)} %copy-done.11, bf16[256,256]{1,0:T(8,128)(2,1)S(1)} %copy-done.8, bf16[256,256]{1,0:T(8,128)(2,1)S(1)} %copy-done.10, f32[8,128]{1,0:T(8,128)S(1)} %get-tuple-element.45.refs_3_, bf16[1,16,256,256]{3,2,1,0:T(8,128)(2,1)} %refs_4_, f32[1,16,256,256]{3,2,1,0:T(8,128)} %refs_5_.1, ...), custom_call_target="tpu_custom_call" | custom-call | flops 1 | bytes 1 | tf_op jit(solution)/shard_map/pallas_call | solution.py:429
  (94 shorter events, 17.0 us)
Async XLA Ops:
  2.0 8.8 %collective-permute-start.2 = (bf16[1,528,256]{2,1,0:T(8,128)(2,1)S(1)}, bf16[1,528,256]{2,1,0:T(8,128)(2,1)S(1)}, u32[]{:S(2)}, u32[]{:S(2)}) collective-permute-start(bf16[1,528,256]{2,1,0:T(8,128)(2,1)S(1)} %get-tuple-element.62), channel_id=1, source_target_pairs={{0,4},{1,5},{2,6},{3,7},{4,0},{5,1},{6,2},{7,3},{8,12},{9,13},{10,... | collective-permute-start | bytes 811016 | tf_op jit(solution)/shard_map/ppermute | solution.py:41
  3.6 3.5 %collective-permute-start = (f32[256,256]{1,0:T(8,128)S(1)}, f32[256,256]{1,0:T(8,128)S(1)}, u32[]{:S(2)}, u32[]{:S(2)}) collective-permute-start(f32[256,256]{1,0:T(8,128)S(1)} %bitcast.9), channel_id=1, source_target_pairs={{0,16},{16,0},{32,48},{48,32},{64,80},{80,64},{96,112},{112,96},{1... | collective-permute-start | bytes 786440 | tf_op jit(solution)/shard_map/ppermute | solution.py:45
  4.5 6.5 %collective-permute-start.3 = (bf16[1,528,256]{2,1,0:T(8,128)(2,1)S(1)}, bf16[1,528,256]{2,1,0:T(8,128)(2,1)S(1)}, u32[]{:S(2)}, u32[]{:S(2)}) collective-permute-start(bf16[1,528,256]{2,1,0:T(8,128)(2,1)S(1)} %get-tuple-element.61), channel_id=1, source_target_pairs={{0,1},{1,0},{2,3},{3,2},{4,5},{5,4},{6,7},{7,6},{8,9},{9,8},{10,11... | collective-permute-start | bytes 811016 | tf_op jit(solution)/shard_map/ppermute | solution.py:41
  11.1 19.4 %collective-permute-start.10 = (bf16[2,528,256]{2,1,0:T(8,128)(2,1)S(1)}, bf16[2,528,256]{2,1,0:T(8,128)(2,1)S(1)}, u32[]{:S(2)}, u32[]{:S(2)}) collective-permute-start(bf16[2,528,256]{2,1,0:T(8,128)(2,1)S(1)} %pad_maximum_fusion), channel_id=1, source_target_pairs={{0,1},{1,0},{2,3},{3,2},{4,5},{5,4},{6,7},{7,6},{8,9},{9,8},{10,11... | collective-permute-start | bytes 1622024 | tf_op jit(solution)/shard_map/ppermute | solution.py:41
  13.1 17.6 %collective-permute-start.11 = (bf16[2,528,256]{2,1,0:T(8,128)(2,1)S(1)}, bf16[2,528,256]{2,1,0:T(8,128)(2,1)S(1)}, u32[]{:S(2)}, u32[]{:S(2)}) collective-permute-start(bf16[2,528,256]{2,1,0:T(8,128)(2,1)S(1)} %pad_maximum_fusion.1), channel_id=1, source_target_pairs={{0,12},{1,13},{2,14},{3,15},{4,8},{5,9},{6,10},{7,11},{8,4},{9,5},... | collective-permute-start | bytes 1622024 | tf_op jit(solution)/shard_map/ppermute | solution.py:41
  14.8 9.7 %collective-permute-start.4 = (f32[256,256]{1,0:T(8,128)S(1)}, f32[256,256]{1,0:T(8,128)S(1)}, u32[]{:S(2)}, u32[]{:S(2)}) collective-permute-start(f32[256,256]{1,0:T(8,128)S(1)} %copy-done.23), channel_id=1, source_target_pairs={{0,32},{32,64},{64,96},{48,16},{80,48},{112,80},{1,33},{33,65},{65... | collective-permute-start | bytes 786440 | tf_op jit(solution)/shard_map/ppermute | solution.py:525
  18.3 8.7 %collective-permute-start.5 = (f32[256,256]{1,0:T(8,128)S(1)}, f32[256,256]{1,0:T(8,128)S(1)}, u32[]{:S(2)}, u32[]{:S(2)}) collective-permute-start(f32[256,256]{1,0:T(8,128)S(1)} %copy-done.23), channel_id=1, source_target_pairs={{0,64},{32,96},{80,16},{112,48},{1,65},{33,97},{81,17},{113,49},{2... | collective-permute-start | bytes 786440 | tf_op jit(solution)/shard_map/ppermute | solution.py:525
  23.1 5.2 %collective-permute-start.6 = (f32[256,256]{1,0:T(8,128)S(1)}, f32[256,256]{1,0:T(8,128)S(1)}, u32[]{:S(2)}, u32[]{:S(2)}) collective-permute-start(f32[256,256]{1,0:T(8,128)S(1)} %copy-done.23), channel_id=1, source_target_pairs={{0,96},{112,16},{1,97},{113,17},{2,98},{114,18},{3,99},{115,19},{4... | collective-permute-start | bytes 786440 | tf_op jit(solution)/shard_map/ppermute | solution.py:525
  24.4 7.5 %collective-permute-start.7 = (f32[256,256]{1,0:T(8,128)S(1)}, f32[256,256]{1,0:T(8,128)S(1)}, u32[]{:S(2)}, u32[]{:S(2)}) collective-permute-start(f32[256,256]{1,0:T(8,128)S(1)} %collective-permute-done.4.m1), channel_id=1, source_target_pairs={{0,16},{16,0},{32,48},{48,32},{64,80},{80,64},{96,112},{112,96},{1... | collective-permute-start | bytes 786440 | tf_op jit(solution)/shard_map/ppermute | solution.py:45
  26.9 7.3 %collective-permute-start.8 = (f32[256,256]{1,0:T(8,128)S(1)}, f32[256,256]{1,0:T(8,128)S(1)}, u32[]{:S(2)}, u32[]{:S(2)}) collective-permute-start(f32[256,256]{1,0:T(8,128)S(1)} %collective-permute-done.5.m2), channel_id=1, source_target_pairs={{0,16},{16,0},{32,48},{48,32},{64,80},{80,64},{96,112},{112,96},{1... | collective-permute-start | bytes 786440 | tf_op jit(solution)/shard_map/ppermute | solution.py:45
  28.2 6.5 %collective-permute-start.9 = (f32[256,256]{1,0:T(8,128)S(1)}, f32[256,256]{1,0:T(8,128)S(1)}, u32[]{:S(2)}, u32[]{:S(2)}) collective-permute-start(f32[256,256]{1,0:T(8,128)S(1)} %collective-permute-done.6.m3), channel_id=1, source_target_pairs={{0,16},{16,0},{32,48},{48,32},{64,80},{80,64},{96,112},{112,96},{1... | collective-permute-start | bytes 786440 | tf_op jit(solution)/shard_map/ppermute | solution.py:45
  30.5 12.7 %collective-permute-start.14 = (bf16[4,528,256]{2,1,0:T(8,128)(2,1)S(1)}, bf16[4,528,256]{2,1,0:T(8,128)(2,1)}, u32[]{:S(2)}, u32[]{:S(2)}) collective-permute-start(bf16[4,528,256]{2,1,0:T(8,128)(2,1)S(1)} %constant_dynamic-update-slice_fusion.refs_3_), channel_id=1, source_target_pairs={{0,16},{16,0},{32,48},{48,32},{64,80},{80,64},{96,112},{112,96},{1... | collective-permute-start | bytes 3244040 | tf_op jit(solution)/shard_map/ppermute | solution.py:45
  31.5 11.7 %collective-permute-start.15 = (bf16[4,528,256]{2,1,0:T(8,128)(2,1)}, bf16[4,528,256]{2,1,0:T(8,128)(2,1)}, u32[]{:S(2)}, u32[]{:S(2)}) collective-permute-start(bf16[4,528,256]{2,1,0:T(8,128)(2,1)} %constant_dynamic-update-slice_fusion.2.refs_4_), channel_id=1, source_target_pairs={{0,16},{16,0},{32,48},{48,32},{64,80},{80,64},{96,112},{112,96},{1... | collective-permute-start | bytes 3244040 | tf_op jit(solution)/shard_map/ppermute | solution.py:45
  31.9 24.4 %collective-permute-start.12 = (bf16[4,528,256]{2,1,0:T(8,128)(2,1)S(1)}, bf16[4,528,256]{2,1,0:T(8,128)(2,1)}, u32[]{:S(2)}, u32[]{:S(2)}) collective-permute-start(bf16[4,528,256]{2,1,0:T(8,128)(2,1)S(1)} %constant_dynamic-update-slice_fusion.refs_3_), channel_id=1, source_target_pairs={{0,12},{1,13},{2,14},{3,15},{4,8},{5,9},{6,10},{7,11},{8,4},{9,5},... | collective-permute-start | bytes 3244040 | tf_op jit(solution)/shard_map/ppermute | solution.py:41
  34.2 22.2 %collective-permute-start.13 = (bf16[4,528,256]{2,1,0:T(8,128)(2,1)}, bf16[4,528,256]{2,1,0:T(8,128)(2,1)}, u32[]{:S(2)}, u32[]{:S(2)}) collective-permute-start(bf16[4,528,256]{2,1,0:T(8,128)(2,1)} %constant_dynamic-update-slice_fusion.2.refs_4_), channel_id=1, source_target_pairs={{0,3},{1,2},{2,1},{3,0},{4,7},{5,6},{6,5},{7,4},{8,11},{9,10},{10,... | collective-permute-start | bytes 3244040 | tf_op jit(solution)/shard_map/ppermute | solution.py:41
  34.8 27.7 %collective-permute-start.18 = (bf16[4,528,256]{2,1,0:T(8,128)(2,1)S(1)}, bf16[4,528,256]{2,1,0:T(8,128)(2,1)}, u32[]{:S(2)}, u32[]{:S(2)}) collective-permute-start(bf16[4,528,256]{2,1,0:T(8,128)(2,1)S(1)} %constant_dynamic-update-slice_fusion.refs_3_), channel_id=1, source_target_pairs={{0,3},{1,2},{2,1},{3,0},{4,7},{5,6},{6,5},{7,4},{8,11},{9,10},{10,... | collective-permute-start | bytes 3244040 | tf_op jit(solution)/shard_map/ppermute | solution.py:41
  43.2 19.3 %collective-permute-start.19 = (bf16[4,528,256]{2,1,0:T(8,128)(2,1)}, bf16[4,528,256]{2,1,0:T(8,128)(2,1)S(1)}, u32[]{:S(2)}, u32[]{:S(2)}) collective-permute-start(bf16[4,528,256]{2,1,0:T(8,128)(2,1)} %constant_dynamic-update-slice_fusion.2.refs_4_), channel_id=1, source_target_pairs={{0,4},{1,5},{2,6},{3,7},{4,0},{5,1},{6,2},{7,3},{8,12},{9,13},{10,... | collective-permute-start | bytes 3244040 | tf_op jit(solution)/shard_map/ppermute | solution.py:41
  56.4 6.1 %collective-permute-start.16 = (bf16[4,528,256]{2,1,0:T(8,128)(2,1)}, bf16[4,528,256]{2,1,0:T(8,128)(2,1)S(1)}, u32[]{:S(2)}, u32[]{:S(2)}) collective-permute-start(bf16[4,528,256]{2,1,0:T(8,128)(2,1)} %collective-permute-done.12.refs_3_), channel_id=1, source_target_pairs={{0,16},{16,0},{32,48},{48,32},{64,80},{80,64},{96,112},{112,96},{1... | collective-permute-start | bytes 3244040 | tf_op jit(solution)/shard_map/ppermute | solution.py:45
  56.5 6.5 %collective-permute-start.17 = (bf16[4,528,256]{2,1,0:T(8,128)(2,1)}, bf16[4,528,256]{2,1,0:T(8,128)(2,1)S(1)}, u32[]{:S(2)}, u32[]{:S(2)}) collective-permute-start(bf16[4,528,256]{2,1,0:T(8,128)(2,1)} %collective-permute-done.13.refs_4_), channel_id=1, source_target_pairs={{0,16},{16,0},{32,48},{48,32},{64,80},{80,64},{96,112},{112,96},{1... | collective-permute-start | bytes 3244040 | tf_op jit(solution)/shard_map/ppermute | solution.py:45
  57.0 19.6 %collective-permute-start.22 = (bf16[4,528,256]{2,1,0:T(8,128)(2,1)}, bf16[4,528,256]{2,1,0:T(8,128)(2,1)S(1)}, u32[]{:S(2)}, u32[]{:S(2)}) collective-permute-start(bf16[4,528,256]{2,1,0:T(8,128)(2,1)} %collective-permute-done.12.refs_3_), channel_id=1, source_target_pairs={{0,3},{1,2},{2,1},{3,0},{4,7},{5,6},{6,5},{7,4},{8,11},{9,10},{10,... | collective-permute-start | bytes 3244040 | tf_op jit(solution)/shard_map/ppermute | solution.py:41
  62.5 15.4 %collective-permute-start.23 = (bf16[4,528,256]{2,1,0:T(8,128)(2,1)}, bf16[4,528,256]{2,1,0:T(8,128)(2,1)S(1)}, u32[]{:S(2)}, u32[]{:S(2)}) collective-permute-start(bf16[4,528,256]{2,1,0:T(8,128)(2,1)} %collective-permute-done.13.refs_4_), channel_id=1, source_target_pairs={{0,4},{1,5},{2,6},{3,7},{4,0},{5,1},{6,2},{7,3},{8,12},{9,13},{10,... | collective-permute-start | bytes 3244040 | tf_op jit(solution)/shard_map/ppermute | solution.py:41
  62.5 15.9 %collective-permute-start.20 = (bf16[4,528,256]{2,1,0:T(8,128)(2,1)}, bf16[4,528,256]{2,1,0:T(8,128)(2,1)S(1)}, u32[]{:S(2)}, u32[]{:S(2)}) collective-permute-start(bf16[4,528,256]{2,1,0:T(8,128)(2,1)} %collective-permute-done.18.refs_14_), channel_id=1, source_target_pairs={{0,16},{16,0},{32,48},{48,32},{64,80},{80,64},{96,112},{112,96},{1... | collective-permute-start | bytes 3244040 | tf_op jit(solution)/shard_map/ppermute | solution.py:45
  62.5 15.9 %collective-permute-start.21 = (bf16[4,528,256]{2,1,0:T(8,128)(2,1)S(1)}, bf16[4,528,256]{2,1,0:T(8,128)(2,1)S(1)}, u32[]{:S(2)}, u32[]{:S(2)}) collective-permute-start(bf16[4,528,256]{2,1,0:T(8,128)(2,1)S(1)} %collective-permute-done.19.refs_15_), channel_id=1, source_target_pairs={{0,16},{16,0},{32,48},{48,32},{64,80},{80,64},{96,112},{112,96},{1... | collective-permute-start | bytes 3244040 | tf_op jit(solution)/shard_map/ppermute | solution.py:45
  77.8 4.3 %collective-permute-start.25 = (bf16[4,528,256]{2,1,0:T(8,128)(2,1)S(1)}, bf16[4,528,256]{2,1,0:T(8,128)(2,1)S(1)}, u32[]{:S(2)}, u32[]{:S(2)}) collective-permute-start(bf16[4,528,256]{2,1,0:T(8,128)(2,1)S(1)} %collective-permute-done.23.refs_19_), channel_id=1, source_target_pairs={{0,16},{16,0},{32,48},{48,32},{64,80},{80,64},{96,112},{112,96},{1... | collective-permute-start | bytes 3244040 | tf_op jit(solution)/shard_map/ppermute | solution.py:45
  (26 other events, 160.0 us)

commit v4 on v3

--- a/solution.py
+++ b/solution.py
@@ -138,12 +138,17 @@
     )
 
 
-def load_terms(groups, lbuf, rbuf, tails, sems):
+def load_terms(groups, lbuf, rbuf, tails, sems, vectors):
     copies = [
         group_copies(group, lbuf, rbuf, tails, sems, g) for g, group in enumerate(groups)
     ]
-    for copy in [c[2] for c in copies] + [c for pair in copies for c in pair[:2]]:
+    for copy in copies[0][:2]:
         copy.start()
+    for copy in [c[2] for c in copies] + vectors:
+        copy.start()
+    for pair in copies[1:]:
+        for copy in pair[:2]:
+            copy.start()
 
 
 def read_blocks(groups, lbuf, rbuf, tails, sems, table_v, table, sem):
@@ -155,7 +160,7 @@
     move.wait()
 
 
-def build_and_apply(groups, lbuf, rbuf, tails, sems, table, lq_ref, rq_ref, vb, acc, done):
+def build_and_apply(groups, lbuf, rbuf, tails, sems, table, lq_ref, rq_ref, vb, acc, done, ready):
     lq = lq_ref[...]
     lq_t = lq.T
     rq = rq_ref[...]
@@ -166,7 +171,6 @@
         left.wait()
         right.wait()
         spots = [4 * g + u for u in range(4)]
-        terms = [(table[k, 0], table[k, 1]) for k in spots]
         temps = [(dot(lbuf[k], lq).astype(BF16), dot(rbuf[k], rq_t).astype(BF16)) for k in spots]
         lefts = [dot(lq_t, lt).astype(BF16) for lt, _ in temps]
         rights = [dot(rq, rt).astype(BF16) for _, rt in temps]
@@ -174,56 +178,37 @@
             lbuf[k] = l
             rbuf[k] = r
         done(g)
+        pl.when(g == 0)(ready)
+        terms = [(table[k, 0], table[k, 1]) for k in spots]
         apply_terms(terms, lefts, rights, vb, acc)
         return carry
 
     lax.fori_loop(0, len(groups), some, 0)
 
 
-def part_kernel(count, carried, lq_ref, rq_ref, vb_hbm, *rest):
-    groups, rest = rest[:count], rest[count:]
+def part_kernel(count, carried, lq_ref, rq_ref, vb, *rest):
     if carried:
         h_in, rest = rest[0], rest[1:]
-    left_out, right_out, table_out, h_out = rest[:4]
-    lbuf, rbuf, tails, table_v, table, vb, hv, sems, out_sems = rest[4:]
-    start = pltpu.make_async_copy(vb_hbm, vb, sems.at[3 * count])
-    start.start()
-    if carried:
-        before = pltpu.make_async_copy(h_in, hv, sems.at[3 * count + 1])
-        before.start()
-    load_terms(groups, lbuf, rbuf, tails, sems)
-    if not carried:
-        def clear(b, carry):
-            hv[b] = jnp.zeros((BLK, BLK), F32)
-            return carry
-
-        lax.fori_loop(0, NB, clear, 0)
-    read_blocks(groups, lbuf, rbuf, tails, sems, table_v, table, sems.at[3 * count + 2])
-    table_copy = pltpu.make_async_copy(table_v, table_out, out_sems.at[2 * count + 1])
-    table_copy.start()
-
-    def out_copies(g):
-        spot = pl.ds(4 * g, 4)
-        return (
-            pltpu.make_async_copy(lbuf.at[spot], left_out.at[spot], out_sems.at[2 * g]),
-            pltpu.make_async_copy(rbuf.at[spot], right_out.at[spot], out_sems.at[2 * g + 1]),
-        )
-
-    def done(g):
-        for copy in out_copies(g):
-            copy.start()
-
-    start.wait()
-    if carried:
-        before.wait()
-    build_and_apply(groups, lbuf, rbuf, tails, sems, table, lq_ref, rq_ref, vb, hv, done)
-    last = pltpu.make_async_copy(hv, h_out, out_sems.at[2 * count])
-    last.start()
+    groups, rest = rest[:count], rest[count:]
+    lbuf, rbuf, table_out, hv = rest[:4]
+    tails, table_v, table, sems = rest[4:]
+    load_terms(groups, lbuf, rbuf, tails, sems, [])
+
+    def clear(b, carry):
+        hv[b] = h_in[b] if carried else jnp.zeros((BLK, BLK), F32)
+        return carry
+
+    lax.fori_loop(0, NB, clear, 0)
+    table_copy = pltpu.make_async_copy(table_v, table_out, sems.at[3 * count + 1])
+
+    def ready():
+        read_blocks(groups, lbuf, rbuf, tails, sems, table_v, table, sems.at[3 * count])
+        table_copy.start()
+
+    build_and_apply(
+        groups, lbuf, rbuf, tails, sems, table, lq_ref, rq_ref, vb, hv, lambda g: None, ready
+    )
     table_copy.wait()
-    for g in range(count):
-        for copy in out_copies(g):
-            copy.wait()
-    last.wait()
 
 
 def part(groups, lq, rq, vb, h_in):
@@ -243,22 +228,17 @@
             jax.ShapeDtypeStruct((terms, 128), I32),
             jax.ShapeDtypeStruct(FULL, F32),
         ),
-        in_specs=[VMEM, VMEM] + [HBM] * (1 + count + carried),
-        out_specs=(HBM,) * 4,
+        in_specs=[VMEM] * (3 + carried) + [HBM] * count,
+        out_specs=(VMEM, VMEM, HBM, VMEM),
         scratch_shapes=[
-            pltpu.VMEM((terms, BLK, BLK), BF16),
-            pltpu.VMEM((terms, BLK, BLK), BF16),
             pltpu.VMEM((terms, TAIL, BLK), BF16),
             pltpu.VMEM((terms, 128), I32),
             pltpu.SMEM((terms, 128), I32),
-            pltpu.VMEM(FULL, BF16),
-            pltpu.VMEM(FULL, F32),
-            pltpu.SemaphoreType.DMA((3 * count + 3,)),
-            pltpu.SemaphoreType.DMA((2 * count + 2,)),
+            pltpu.SemaphoreType.DMA((3 * count + 2,)),
         ],
-        compiler_params=pltpu.CompilerParams(vmem_limit_bytes=18 * MIB),
+        compiler_params=pltpu.CompilerParams(vmem_limit_bytes=24 * MIB),
         cost_estimate=LIGHT,
-    )(lq, rq, vb, *groups, *((h_in,) if carried else ()))
+    )(lq, rq, vb, *((h_in,) if carried else ()), *groups)
 
 
 def fold(p):
@@ -287,9 +267,7 @@
             ((vb_hbm, vb), (h_hbm, hv), (psi_hbm.at[0], psi), (diag_hbm.at[0], dv))
         )
     ]
-    for copy in vectors[:2]:
-        copy.start()
-    load_terms(groups, lbuf, rbuf, tails, sems)
+    load_terms(groups, lbuf, rbuf, tails, sems, vectors[:2])
     for copy in vectors[2:]:
         copy.start()
     built = []
@@ -304,13 +282,14 @@
             built.append(copy)
         begin += size
 
-    read_blocks(
-        groups, lbuf, rbuf, tails, sems, table_v, table.at[pl.ds(0, 4 * count)], sems.at[3 * count]
-    )
-    vectors[0].wait()
-    vectors[1].wait()
+    def ready():
+        mine = table.at[pl.ds(0, 4 * count)]
+        read_blocks(groups, lbuf, rbuf, tails, sems, table_v, mine, sems.at[3 * count])
+        vectors[0].wait()
+        vectors[1].wait()
+
     build_and_apply(
-        groups, lbuf, rbuf, tails, sems, table, lq_ref, rq_ref, vb, hv, lambda g: None
+        groups, lbuf, rbuf, tails, sems, table, lq_ref, rq_ref, vb, hv, lambda g: None, ready
     )
     vectors[2].wait()
     vectors[3].wait()
@@ -372,7 +351,7 @@
             apply_terms(terms, [lbuf[k] for k in spots], [rbuf[k] for k in spots], vb, gv)
             return value
 
-        over_terms(apply_step, 0)
+        over_terms(apply_step, 0, 2 * UNROLL)
 
         def couplings(b, sums):
             g = gv[b]
@@ -395,16 +374,22 @@
 
         (along,) = over_blocks(functools.partial(turn, keep, move, theta), 1)
 
-    (size,) = over_blocks(functools.partial(orthogonal, total(along)), 1)
-    scale_t = lax.rsqrt(total(size) + 1e-12)
+    along = total(along)
+
+    def last_orthogonal(b, sums):
+        t = tv[b] - along * xv[b]
+        tv[b] = t
+        t2 = t * t
+        return (sums[0] + fold(t2), sums[1] + fold(hv[b] * t), sums[2] + fold(dv[b] * t2))
+
+    size, cross, curve_diag = (total(v) for v in over_blocks(last_orthogonal, 3))
+    scale_t = lax.rsqrt(size + 1e-12)
 
     def last_unit(b, sums):
-        t = tv[b] * scale_t
-        tv[b] = t
-        vb[b] = t.astype(BF16)
-        return (sums[0] + fold(hv[b] * t), sums[1] + fold(dv[b] * t * t))
-
-    cross, curve_diag = over_blocks(last_unit, 2)
+        vb[b] = (tv[b] * scale_t).astype(BF16)
+        return sums
+
+    over_blocks(last_unit, 0)
 
     def last_step(terms, spots, acc):
         mids = [dot(vb[s], rbuf[k]).astype(BF16) for (s, _), k in zip(terms, spots)]
@@ -413,8 +398,9 @@
         return acc
 
     curve_terms = over_terms(last_step, zero, 2 * UNROLL)
-    curve = total(curve_diag) + 2.0 * total(curve_terms)
-    keep, move = rotation(theta, total(cross), curve)
+    curve = (curve_diag * scale_t + 2.0 * total(curve_terms)) * scale_t
+    keep, move = rotation(theta, cross * scale_t, curve)
+    move = move * scale_t
     amplitude = float(NB * BLK * BLK) ** 0.5
     out_ref[0, 0] = (keep * xv[op] - move * tv[op]) * amplitude
 
@@ -447,7 +433,7 @@
             pltpu.SemaphoreType.DMA((3 * count + 1,)),
             pltpu.SemaphoreType.DMA((4 + 3 * len(sizes),)),
         ],
-        compiler_params=pltpu.CompilerParams(vmem_limit_bytes=46 * MIB),
+        compiler_params=pltpu.CompilerParams(vmem_limit_bytes=45 * MIB),
         cost_estimate=LIGHT,
     )(
         ids,
@@ -523,11 +509,11 @@
         pairs = [(2 * y, 2 * (y + k)) for y in range(4 - k)]
         pairs += [(2 * y + 1, 2 * (y - k) + 1) for y in range(k, 4)]
         received.append(lax.ppermute(product, "site", pairs))
-    across = [swap_core(r) for r in received]
 
     four = [jnp.concatenate(pair, 0) for pair in zip(two, second)]
     third = [swap_op(p, i, 2) for i, p in enumerate(four)]
-    psi, received, across = after((psi, tuple(received), tuple(across)), four)
+    psi, received = after((psi, tuple(received)), four)
+    across = [swap_core(r) for r in received]
     vb, scale = start_vector(psi)
     lq, rq = chain_products(ids, other, received, across)
     old = [swap_op(p, i, 3) for i, p in enumerate(four)]
@@ -536,11 +522,11 @@
         return list(groups) + [swap_core(g) for g in groups]
 
     built = [part(both(four), lq, rq, vb, None)]
-    third = after(third, built[-1][3:])
+    third = after(third, built[-1][2:3])
     new = [swap_op(p, i, 3) for i, p in enumerate(third)]
-    old = after(old, built[-1][3:])
+    old = after(old, built[-1][2:3])
     built.append(part(both(third), lq, rq, vb, built[-1][3]))
-    new = after(new, built[-1][3:])
+    new = after(new, built[-1][2:3])
     return solve(ids, built, lq, rq, scale, psi, diagonal, vb, built[-1][3], both(old) + both(new))
 
 

time: 128 us -> 125 us (0.977)
  Pallas kernels: 69.3 us -> 66.4 us
  local copies, waits for them, and re-layouts: 13.5 us -> 11.2 us
  waiting for transfers between devices: 12 us -> 14.3 us
    ppermute x10, waiting for transfers between devices: 5.84 us -> 8.36 us  [swap_op(): return lax.ppermute(value, ('site', 'op'), pairs)]
    unnamed x50 -> x48, local copies, waits for them, and re-layouts: 12.5 us -> 10.1 us
    pallas_call x1, Pallas kernels: 43.8 us -> 42.3 us  [solve(): pl.pallas_call(kernel, out_shape=jax.ShapeDtypeStruct((1, 1, BLK, BLK), F...]
    pallas_call x2, Pallas kernels: 17.6 us -> 16.1 us  [part(): pl.pallas_call(kernel, out_shape=(env, env, jax.ShapeDtypeStruct((terms,...]
  transfers between devices with their start and end apart: 26 -> 26, of which waited for: 6 -> 8; matrix products, arithmetic and copies ran while one was open for 2% -> 2% of each run, Pallas kernels for 20% -> 20%
where the time goes in v4:
time: 125 us; the launch traced here: 123 us
  Pallas kernels  66.4 us (53%)
  starting transfers between devices  28.4 us (23%)
  waiting for transfers between devices  14.3 us (11%)
  local copies, waits for them, and re-layouts  11.2 us (9%)
  other arithmetic  2.56 us (2%)
    pallas_call x1, Pallas kernels, solve(): pl.pallas_call(kernel, out_shape=jax.ShapeDtypeStruct((1, 1, BLK, BLK), F...  42.3 us
    pallas_call x2, Pallas kernels, part(): pl.pallas_call(kernel, out_shape=(env, env, jax.ShapeDtypeStruct((terms,...  16.1 us
    ppermute x10, starting transfers between devices, swap_op(): return lax.ppermute(value, ('site', 'op'), pairs)  13.9 us
    unnamed x48, local copies, waits for them, and re-layouts  10.1 us
    ppermute x3, starting transfers between devices, body(): received.append(lax.ppermute(product, 'site', pairs))  9.6 us
    ppermute x10, waiting for transfers between devices, swap_op(): return lax.ppermute(value, ('site', 'op'), pairs)  8.36 us
    ppermute x13, starting transfers between devices, swap_core(): return lax.ppermute(value, 'site', [(i, i ^ 1) for i in range(8)])  4.85 us
    pallas_call x1, Pallas kernels, chain_products(): pl.pallas_call(chain_kernel, out_shape=(out, out), in_specs=[SMEM] + [VME...  4.74 us
  transfers between devices with their start and end apart: 26, of which 8 were waited for; matrix products, arithmetic and copies ran while one was open for 2% of the time, Pallas kernels for 20%

profile of v4, /device:TPU:0, one launch (start us, length us, event | category | flops | bytes accessed | tf_op | source)
XLA Modules:
  0.0 123.2 jit_solution(16754397011408947639)
XLA Ops:
  2.0 1.7 %collective-permute-start.2 = (bf16[1,528,256]{2,1,0:T(8,128)(2,1)S(1)}, bf16[1,528,256]{2,1,0:T(8,128)(2,1)S(1)}, u32[]{:S(2)}, u32[]{:S(2)}) collective-permute-start(bf16[1,528,256]{2,1,0:T(8,128)(2,1)S(1)} %get-tuple-element.56), channel_id=1, source_target_pairs={{0,4},{1,5},{2,6},{3,7},{4,0},{5,1},{6,2},{7,3},{8,12},{9,13},{10,... | collective-permute-start | bytes 811016 | tf_op jit(solution)/shard_map/ppermute | solution.py:41
  4.5 1.9 %collective-permute-start.3 = (bf16[1,528,256]{2,1,0:T(8,128)(2,1)S(1)}, bf16[1,528,256]{2,1,0:T(8,128)(2,1)S(1)}, u32[]{:S(2)}, u32[]{:S(2)}) collective-permute-start(bf16[1,528,256]{2,1,0:T(8,128)(2,1)S(1)} %get-tuple-element.55), channel_id=1, source_target_pairs={{0,1},{1,0},{2,3},{3,2},{4,5},{5,4},{6,7},{7,6},{8,9},{9,8},{10,11... | collective-permute-start | bytes 811016 | tf_op jit(solution)/shard_map/ppermute | solution.py:41
  8.5 2.3 %shard_map.82 = f32[256,256]{1,0:T(8,128)} custom-call(s32[2]{0:T(128)} %pad_add_fusion.site_ref.refs_0_, f32[256,256]{1,0:T(8,128)} %bitcast.8, f32[256,256]{1,0:T(8,128)} %bitcast.10, f32[256,256]{1,0:T(8,128)} %copy-done.12, f32[256,256]{1,0:T(8,128)} %copy-done.13), custom_call_target="tpu_custom_call" | custom-call | flops 1 | bytes 1 | tf_op jit(solution)/shard_map/pallas_call | solution.py:79
  11.1 2.0 %collective-permute-start.7 = (bf16[2,528,256]{2,1,0:T(8,128)(2,1)S(1)}, bf16[2,528,256]{2,1,0:T(8,128)(2,1)S(1)}, u32[]{:S(2)}, u32[]{:S(2)}) collective-permute-start(bf16[2,528,256]{2,1,0:T(8,128)(2,1)S(1)} %pad_maximum_fusion), channel_id=1, source_target_pairs={{0,1},{1,0},{2,3},{3,2},{4,5},{5,4},{6,7},{7,6},{8,9},{9,8},{10,11... | collective-permute-start | bytes 1622024 | tf_op jit(solution)/shard_map/ppermute | solution.py:41
  13.1 1.7 %collective-permute-start.8 = (bf16[2,528,256]{2,1,0:T(8,128)(2,1)S(1)}, bf16[2,528,256]{2,1,0:T(8,128)(2,1)S(1)}, u32[]{:S(2)}, u32[]{:S(2)}) collective-permute-start(bf16[2,528,256]{2,1,0:T(8,128)(2,1)S(1)} %pad_maximum_fusion.1), channel_id=1, source_target_pairs={{0,12},{1,13},{2,14},{3,15},{4,8},{5,9},{6,10},{7,11},{8,4},{9,5},... | collective-permute-start | bytes 1622024 | tf_op jit(solution)/shard_map/ppermute | solution.py:41
  14.8 3.5 %collective-permute-start.4 = (f32[256,256]{1,0:T(8,128)S(1)}, f32[256,256]{1,0:T(8,128)S(1)}, u32[]{:S(2)}, u32[]{:S(2)}) collective-permute-start(f32[256,256]{1,0:T(8,128)S(1)} %copy-done.19), channel_id=1, source_target_pairs={{0,32},{32,64},{64,96},{48,16},{80,48},{112,80},{1,33},{33,65},{65... | collective-permute-start | bytes 786440 | tf_op jit(solution)/shard_map/ppermute | solution.py:511
  18.3 4.8 %collective-permute-start.5 = (f32[256,256]{1,0:T(8,128)S(1)}, f32[256,256]{1,0:T(8,128)S(1)}, u32[]{:S(2)}, u32[]{:S(2)}) collective-permute-start(f32[256,256]{1,0:T(8,128)S(1)} %copy-done.19), channel_id=1, source_target_pairs={{0,64},{32,96},{80,16},{112,48},{1,65},{33,97},{81,17},{113,49},{2... | collective-permute-start | bytes 786440 | tf_op jit(solution)/shard_map/ppermute | solution.py:511
  23.1 1.3 %collective-permute-start.6 = (f32[256,256]{1,0:T(8,128)S(1)}, f32[256,256]{1,0:T(8,128)S(1)}, u32[]{:S(2)}, u32[]{:S(2)}) collective-permute-start(f32[256,256]{1,0:T(8,128)S(1)} %copy-done.19), channel_id=1, source_target_pairs={{0,96},{112,16},{1,97},{113,17},{2,98},{114,18},{3,99},{115,19},{4... | collective-permute-start | bytes 786440 | tf_op jit(solution)/shard_map/ppermute | solution.py:511
  26.9 1.3 %collective-permute-done.6.m3 = f32[256,256]{1,0:T(8,128)S(1)} collective-permute-done((f32[256,256]{1,0:T(8,128)S(1)}, f32[256,256]{1,0:T(8,128)S(1)}, u32[]{:S(2)}, u32[]{:S(2)}) %collective-permute-start.6) | collective-permute-done | bytes 262176 | tf_op jit(solution)/shard_map/ppermute | solution.py:511
  28.2 1.3 %collective-permute-start.9 = (f32[256,256]{1,0:T(8,128)S(1)}, f32[256,256]{1,0:T(8,128)S(1)}, u32[]{:S(2)}, u32[]{:S(2)}) collective-permute-start(f32[256,256]{1,0:T(8,128)S(1)} %collective-permute-done.4.m1), channel_id=1, source_target_pairs={{0,16},{16,0},{32,48},{48,32},{64,80},{80,64},{96,112},{112,96},{1... | collective-permute-start | bytes 786440 | tf_op jit(solution)/shard_map/ppermute | solution.py:45
  30.7 2.3 %collective-permute-start.14 = (bf16[4,528,256]{2,1,0:T(8,128)(2,1)}, bf16[4,528,256]{2,1,0:T(8,128)(2,1)}, u32[]{:S(2)}, u32[]{:S(2)}) collective-permute-start(bf16[4,528,256]{2,1,0:T(8,128)(2,1)} %constant_dynamic-update-slice_fusion.refs_3_), channel_id=1, source_target_pairs={{0,12},{1,13},{2,14},{3,15},{4,8},{5,9},{6,10},{7,11},{8,4},{9,5},... | collective-permute-start | bytes 3244040 | tf_op jit(solution)/shard_map/ppermute | solution.py:41
  33.9 2.5 %collective-permute-start.18 = (bf16[4,528,256]{2,1,0:T(8,128)(2,1)}, bf16[4,528,256]{2,1,0:T(8,128)(2,1)}, u32[]{:S(2)}, u32[]{:S(2)}) collective-permute-start(bf16[4,528,256]{2,1,0:T(8,128)(2,1)} %constant_dynamic-update-slice_fusion.refs_3_), channel_id=1, source_target_pairs={{0,3},{1,2},{2,1},{3,0},{4,7},{5,6},{6,5},{7,4},{8,11},{9,10},{10,... | collective-permute-start | bytes 3244040 | tf_op jit(solution)/shard_map/ppermute | solution.py:41
  37.2 4.7 %shard_map.83 = (bf16[256,256]{1,0:T(8,128)(2,1)}, bf16[256,256]{1,0:T(8,128)(2,1)}) custom-call(s32[2]{0:T(128)} %pad_add_fusion.site_ref.refs_0_, f32[256,256]{1,0:T(8,128)} %copy-done.12, f32[256,256]{1,0:T(8,128)} %copy-done.13, f32[256,256]{1,0:T(8,128)} %copy-done.16, f32[256,256]{1,0:T(8,128)} %copy-done.17, f32[256,256]{1,0:T(8,128)} %copy-done.18, ...), custom_call_target="tpu_custom_call" | custom-call | flops 1 | bytes 1 | tf_op jit(solution)/shard_map/pallas_call | solution.py:111
  43.8 8.0 %shard_map.85 = (bf16[16,256,256]{2,1,0:T(8,128)(2,1)S(1)}, bf16[16,256,256]{2,1,0:T(8,128)(2,1)S(1)}, s32[16,128]{1,0:T(8,128)S(1)}, f32[16,256,256]{2,1,0:T(8,128)S(1)}) custom-call(bf16[256,256]{1,0:T(8,128)(2,1)S(1)} %copy-done.7, bf16[256,256]{1,0:T(8,128)(2,1)S(1)} %copy-done.9, bf16[16,256,256]{2,1,0:T(8,128)(2,1)S(1)} %get-tuple-element.40.refs_2_.refs_6_, ...), custom_call_target="tpu_custom_call" | custom-call | flops 1 | bytes 1 | tf_op jit(solution)/shard_map/pallas_call | solution.py:223
  51.9 1.3 %copy-done.4 = bf16[16,256,256]{2,1,0:T(8,128)(2,1)} copy-done((bf16[16,256,256]{2,1,0:T(8,128)(2,1)}, bf16[16,256,256]{2,1,0:T(8,128)(2,1)S(1)}, u32[]{:S(2)}) %copy-start.4) | copy-done | bytes 2097176
  54.9 6.2 %collective-permute-done.18.refs_14_ = bf16[4,528,256]{2,1,0:T(8,128)(2,1)} collective-permute-done((bf16[4,528,256]{2,1,0:T(8,128)(2,1)}, bf16[4,528,256]{2,1,0:T(8,128)(2,1)}, u32[]{:S(2)}, u32[]{:S(2)}) %collective-permute-start.18) | collective-permute-done | bytes 1081376 | tf_op jit(solution)/shard_map/ppermute | solution.py:41
  61.6 8.1 %shard_map.86 = (bf16[16,256,256]{2,1,0:T(8,128)(2,1)S(1)}, bf16[16,256,256]{2,1,0:T(8,128)(2,1)S(1)}, s32[16,128]{1,0:T(8,128)S(1)}, f32[16,256,256]{2,1,0:T(8,128)S(1)}) custom-call(bf16[256,256]{1,0:T(8,128)(2,1)S(1)} %copy-done.7, bf16[256,256]{1,0:T(8,128)(2,1)S(1)} %copy-done.9, bf16[16,256,256]{2,1,0:T(8,128)(2,1)S(1)} %get-tuple-element.40.refs_2_.refs_6_, ...), custom_call_target="tpu_custom_call" | custom-call | flops 1 | bytes 1 | tf_op jit(solution)/shard_map/pallas_call | solution.py:223
  69.7 2.0 %copy-done.2 = f32[16,256,256]{2,1,0:T(8,128)} copy-done((f32[16,256,256]{2,1,0:T(8,128)}, f32[16,256,256]{2,1,0:T(8,128)S(1)}, u32[]{:S(2)}) %copy-start.2) | copy-done | bytes 4194328
  71.7 1.4 %copy-done.5 = bf16[16,256,256]{2,1,0:T(8,128)(2,1)} copy-done((bf16[16,256,256]{2,1,0:T(8,128)(2,1)}, bf16[16,256,256]{2,1,0:T(8,128)(2,1)S(1)}, u32[]{:S(2)}) %copy-start.5) | copy-done | bytes 2097176
  73.1 1.3 %copy-done.6 = bf16[16,256,256]{2,1,0:T(8,128)(2,1)} copy-done((bf16[16,256,256]{2,1,0:T(8,128)(2,1)}, bf16[16,256,256]{2,1,0:T(8,128)(2,1)S(1)}, u32[]{:S(2)}) %copy-start.6) | copy-done | bytes 2097176
  74.4 2.0 %collective-permute-done.23.refs_19_ = bf16[4,528,256]{2,1,0:T(8,128)(2,1)S(1)} collective-permute-done((bf16[4,528,256]{2,1,0:T(8,128)(2,1)}, bf16[4,528,256]{2,1,0:T(8,128)(2,1)S(1)}, u32[]{:S(2)}, u32[]{:S(2)}) %collective-permute-start.23) | collective-permute-done | bytes 1081376 | tf_op jit(solution)/shard_map/ppermute | solution.py:41
  76.9 2.2 %collective-permute-done.24.refs_20_ = bf16[4,528,256]{2,1,0:T(8,128)(2,1)S(1)} collective-permute-done((bf16[4,528,256]{2,1,0:T(8,128)(2,1)S(1)}, bf16[4,528,256]{2,1,0:T(8,128)(2,1)S(1)}, u32[]{:S(2)}, u32[]{:S(2)}) %collective-permute-start.24) | collective-permute-done | bytes 1081376 | tf_op jit(solution)/shard_map/ppermute | solution.py:45
  79.1 1.5 %collective-permute-done.25.refs_21_ = bf16[4,528,256]{2,1,0:T(8,128)(2,1)S(1)} collective-permute-done((bf16[4,528,256]{2,1,0:T(8,128)(2,1)S(1)}, bf16[4,528,256]{2,1,0:T(8,128)(2,1)S(1)}, u32[]{:S(2)}, u32[]{:S(2)}) %collective-permute-start.25) | collective-permute-done | bytes 1081376 | tf_op jit(solution)/shard_map/ppermute | solution.py:45
  80.7 42.3 %shard_map.87 = f32[1,1,256,256]{3,2,1,0:T(8,128)} custom-call(s32[2]{0:T(128)S(1)} %copy-done.11, bf16[256,256]{1,0:T(8,128)(2,1)S(1)} %copy-done.8, bf16[256,256]{1,0:T(8,128)(2,1)S(1)} %copy-done.10, f32[8,128]{1,0:T(8,128)S(1)} %get-tuple-element.39.refs_3_, bf16[1,16,256,256]{3,2,1,0:T(8,128)(2,1)} %refs_4_, f32[1,16,256,256]{3,2,1,0:T(8,128)} %refs_5_.1, ...), custom_call_target="tpu_custom_call" | custom-call | flops 1 | bytes 1 | tf_op jit(solution)/shard_map/pallas_call | solution.py:415
  (92 shorter events, 15.0 us)
Async XLA Ops:
  2.0 8.8 %collective-permute-start.2 = (bf16[1,528,256]{2,1,0:T(8,128)(2,1)S(1)}, bf16[1,528,256]{2,1,0:T(8,128)(2,1)S(1)}, u32[]{:S(2)}, u32[]{:S(2)}) collective-permute-start(bf16[1,528,256]{2,1,0:T(8,128)(2,1)S(1)} %get-tuple-element.56), channel_id=1, source_target_pairs={{0,4},{1,5},{2,6},{3,7},{4,0},{5,1},{6,2},{7,3},{8,12},{9,13},{10,... | collective-permute-start | bytes 811016 | tf_op jit(solution)/shard_map/ppermute | solution.py:41
  3.6 3.5 %collective-permute-start = (f32[256,256]{1,0:T(8,128)S(1)}, f32[256,256]{1,0:T(8,128)S(1)}, u32[]{:S(2)}, u32[]{:S(2)}) collective-permute-start(f32[256,256]{1,0:T(8,128)S(1)} %bitcast.9), channel_id=1, source_target_pairs={{0,16},{16,0},{32,48},{48,32},{64,80},{80,64},{96,112},{112,96},{1... | collective-permute-start | bytes 786440 | tf_op jit(solution)/shard_map/ppermute | solution.py:45
  4.5 6.5 %collective-permute-start.3 = (bf16[1,528,256]{2,1,0:T(8,128)(2,1)S(1)}, bf16[1,528,256]{2,1,0:T(8,128)(2,1)S(1)}, u32[]{:S(2)}, u32[]{:S(2)}) collective-permute-start(bf16[1,528,256]{2,1,0:T(8,128)(2,1)S(1)} %get-tuple-element.55), channel_id=1, source_target_pairs={{0,1},{1,0},{2,3},{3,2},{4,5},{5,4},{6,7},{7,6},{8,9},{9,8},{10,11... | collective-permute-start | bytes 811016 | tf_op jit(solution)/shard_map/ppermute | solution.py:41
  11.1 14.2 %collective-permute-start.7 = (bf16[2,528,256]{2,1,0:T(8,128)(2,1)S(1)}, bf16[2,528,256]{2,1,0:T(8,128)(2,1)S(1)}, u32[]{:S(2)}, u32[]{:S(2)}) collective-permute-start(bf16[2,528,256]{2,1,0:T(8,128)(2,1)S(1)} %pad_maximum_fusion), channel_id=1, source_target_pairs={{0,1},{1,0},{2,3},{3,2},{4,5},{5,4},{6,7},{7,6},{8,9},{9,8},{10,11... | collective-permute-start | bytes 1622024 | tf_op jit(solution)/shard_map/ppermute | solution.py:41
  13.1 13.1 %collective-permute-start.8 = (bf16[2,528,256]{2,1,0:T(8,128)(2,1)S(1)}, bf16[2,528,256]{2,1,0:T(8,128)(2,1)S(1)}, u32[]{:S(2)}, u32[]{:S(2)}) collective-permute-start(bf16[2,528,256]{2,1,0:T(8,128)(2,1)S(1)} %pad_maximum_fusion.1), channel_id=1, source_target_pairs={{0,12},{1,13},{2,14},{3,15},{4,8},{5,9},{6,10},{7,11},{8,4},{9,5},... | collective-permute-start | bytes 1622024 | tf_op jit(solution)/shard_map/ppermute | solution.py:41
  14.8 11.4 %collective-permute-start.4 = (f32[256,256]{1,0:T(8,128)S(1)}, f32[256,256]{1,0:T(8,128)S(1)}, u32[]{:S(2)}, u32[]{:S(2)}) collective-permute-start(f32[256,256]{1,0:T(8,128)S(1)} %copy-done.19), channel_id=1, source_target_pairs={{0,32},{32,64},{64,96},{48,16},{80,48},{112,80},{1,33},{33,65},{65... | collective-permute-start | bytes 786440 | tf_op jit(solution)/shard_map/ppermute | solution.py:511
  18.3 8.7 %collective-permute-start.5 = (f32[256,256]{1,0:T(8,128)S(1)}, f32[256,256]{1,0:T(8,128)S(1)}, u32[]{:S(2)}, u32[]{:S(2)}) collective-permute-start(f32[256,256]{1,0:T(8,128)S(1)} %copy-done.19), channel_id=1, source_target_pairs={{0,64},{32,96},{80,16},{112,48},{1,65},{33,97},{81,17},{113,49},{2... | collective-permute-start | bytes 786440 | tf_op jit(solution)/shard_map/ppermute | solution.py:511
  23.1 5.2 %collective-permute-start.6 = (f32[256,256]{1,0:T(8,128)S(1)}, f32[256,256]{1,0:T(8,128)S(1)}, u32[]{:S(2)}, u32[]{:S(2)}) collective-permute-start(f32[256,256]{1,0:T(8,128)S(1)} %copy-done.19), channel_id=1, source_target_pairs={{0,96},{112,16},{1,97},{113,17},{2,98},{114,18},{3,99},{115,19},{4... | collective-permute-start | bytes 786440 | tf_op jit(solution)/shard_map/ppermute | solution.py:511
  29.6 3.4 %collective-permute-start.10 = (f32[256,256]{1,0:T(8,128)S(1)}, f32[256,256]{1,0:T(8,128)S(1)}, u32[]{:S(2)}, u32[]{:S(2)}) collective-permute-start(f32[256,256]{1,0:T(8,128)S(1)} %collective-permute-done.5.m2), channel_id=1, source_target_pairs={{0,16},{16,0},{32,48},{48,32},{64,80},{80,64},{96,112},{112,96},{1... | collective-permute-start | bytes 786440 | tf_op jit(solution)/shard_map/ppermute | solution.py:45
  29.6 4.3 %collective-permute-start.11 = (f32[256,256]{1,0:T(8,128)S(1)}, f32[256,256]{1,0:T(8,128)S(1)}, u32[]{:S(2)}, u32[]{:S(2)}) collective-permute-start(f32[256,256]{1,0:T(8,128)S(1)} %collective-permute-done.6.m3), channel_id=1, source_target_pairs={{0,16},{16,0},{32,48},{48,32},{64,80},{80,64},{96,112},{112,96},{1... | collective-permute-start | bytes 786440 | tf_op jit(solution)/shard_map/ppermute | solution.py:45
  30.1 11.9 %collective-permute-start.12 = (bf16[4,528,256]{2,1,0:T(8,128)(2,1)}, bf16[4,528,256]{2,1,0:T(8,128)(2,1)}, u32[]{:S(2)}, u32[]{:S(2)}) collective-permute-start(bf16[4,528,256]{2,1,0:T(8,128)(2,1)} %constant_dynamic-update-slice_fusion.refs_3_), channel_id=1, source_target_pairs={{0,16},{16,0},{32,48},{48,32},{64,80},{80,64},{96,112},{112,96},{1... | collective-permute-start | bytes 3244040 | tf_op jit(solution)/shard_map/ppermute | solution.py:45
  30.1 11.9 %collective-permute-start.13 = (bf16[4,528,256]{2,1,0:T(8,128)(2,1)S(1)}, bf16[4,528,256]{2,1,0:T(8,128)(2,1)}, u32[]{:S(2)}, u32[]{:S(2)}) collective-permute-start(bf16[4,528,256]{2,1,0:T(8,128)(2,1)S(1)} %constant_dynamic-update-slice_fusion.2.refs_4_), channel_id=1, source_target_pairs={{0,16},{16,0},{32,48},{48,32},{64,80},{80,64},{96,112},{112,96},{1... | collective-permute-start | bytes 3244040 | tf_op jit(solution)/shard_map/ppermute | solution.py:45
  30.7 22.5 %collective-permute-start.14 = (bf16[4,528,256]{2,1,0:T(8,128)(2,1)}, bf16[4,528,256]{2,1,0:T(8,128)(2,1)}, u32[]{:S(2)}, u32[]{:S(2)}) collective-permute-start(bf16[4,528,256]{2,1,0:T(8,128)(2,1)} %constant_dynamic-update-slice_fusion.refs_3_), channel_id=1, source_target_pairs={{0,12},{1,13},{2,14},{3,15},{4,8},{5,9},{6,10},{7,11},{8,4},{9,5},... | collective-permute-start | bytes 3244040 | tf_op jit(solution)/shard_map/ppermute | solution.py:41
  33.0 20.2 %collective-permute-start.15 = (bf16[4,528,256]{2,1,0:T(8,128)(2,1)S(1)}, bf16[4,528,256]{2,1,0:T(8,128)(2,1)}, u32[]{:S(2)}, u32[]{:S(2)}) collective-permute-start(bf16[4,528,256]{2,1,0:T(8,128)(2,1)S(1)} %constant_dynamic-update-slice_fusion.2.refs_4_), channel_id=1, source_target_pairs={{0,3},{1,2},{2,1},{3,0},{4,7},{5,6},{6,5},{7,4},{8,11},{9,10},{10,... | collective-permute-start | bytes 3244040 | tf_op jit(solution)/shard_map/ppermute | solution.py:41
  33.9 27.2 %collective-permute-start.18 = (bf16[4,528,256]{2,1,0:T(8,128)(2,1)}, bf16[4,528,256]{2,1,0:T(8,128)(2,1)}, u32[]{:S(2)}, u32[]{:S(2)}) collective-permute-start(bf16[4,528,256]{2,1,0:T(8,128)(2,1)} %constant_dynamic-update-slice_fusion.refs_3_), channel_id=1, source_target_pairs={{0,3},{1,2},{2,1},{3,0},{4,7},{5,6},{6,5},{7,4},{8,11},{9,10},{10,... | collective-permute-start | bytes 3244040 | tf_op jit(solution)/shard_map/ppermute | solution.py:41
  42.0 19.1 %collective-permute-start.19 = (bf16[4,528,256]{2,1,0:T(8,128)(2,1)S(1)}, bf16[4,528,256]{2,1,0:T(8,128)(2,1)S(1)}, u32[]{:S(2)}, u32[]{:S(2)}) collective-permute-start(bf16[4,528,256]{2,1,0:T(8,128)(2,1)S(1)} %constant_dynamic-update-slice_fusion.2.refs_4_), channel_id=1, source_target_pairs={{0,4},{1,5},{2,6},{3,7},{4,0},{5,1},{6,2},{7,3},{8,12},{9,13},{10,... | collective-permute-start | bytes 3244040 | tf_op jit(solution)/shard_map/ppermute | solution.py:41
  53.2 7.9 %collective-permute-start.16 = (bf16[4,528,256]{2,1,0:T(8,128)(2,1)}, bf16[4,528,256]{2,1,0:T(8,128)(2,1)S(1)}, u32[]{:S(2)}, u32[]{:S(2)}) collective-permute-start(bf16[4,528,256]{2,1,0:T(8,128)(2,1)} %collective-permute-done.14.refs_4_), channel_id=1, source_target_pairs={{0,16},{16,0},{32,48},{48,32},{64,80},{80,64},{96,112},{112,96},{1... | collective-permute-start | bytes 3244040 | tf_op jit(solution)/shard_map/ppermute | solution.py:45
  53.3 8.3 %collective-permute-start.17 = (bf16[4,528,256]{2,1,0:T(8,128)(2,1)}, bf16[4,528,256]{2,1,0:T(8,128)(2,1)S(1)}, u32[]{:S(2)}, u32[]{:S(2)}) collective-permute-start(bf16[4,528,256]{2,1,0:T(8,128)(2,1)} %collective-permute-done.15.refs_5_), channel_id=1, source_target_pairs={{0,16},{16,0},{32,48},{48,32},{64,80},{80,64},{96,112},{112,96},{1... | collective-permute-start | bytes 3244040 | tf_op jit(solution)/shard_map/ppermute | solution.py:45
  53.8 20.6 %collective-permute-start.22 = (bf16[4,528,256]{2,1,0:T(8,128)(2,1)}, bf16[4,528,256]{2,1,0:T(8,128)(2,1)S(1)}, u32[]{:S(2)}, u32[]{:S(2)}) collective-permute-start(bf16[4,528,256]{2,1,0:T(8,128)(2,1)} %collective-permute-done.14.refs_4_), channel_id=1, source_target_pairs={{0,3},{1,2},{2,1},{3,0},{4,7},{5,6},{6,5},{7,4},{8,11},{9,10},{10,... | collective-permute-start | bytes 3244040 | tf_op jit(solution)/shard_map/ppermute | solution.py:41
  61.1 15.4 %collective-permute-start.23 = (bf16[4,528,256]{2,1,0:T(8,128)(2,1)}, bf16[4,528,256]{2,1,0:T(8,128)(2,1)S(1)}, u32[]{:S(2)}, u32[]{:S(2)}) collective-permute-start(bf16[4,528,256]{2,1,0:T(8,128)(2,1)} %collective-permute-done.15.refs_5_), channel_id=1, source_target_pairs={{0,4},{1,5},{2,6},{3,7},{4,0},{5,1},{6,2},{7,3},{8,12},{9,13},{10,... | collective-permute-start | bytes 3244040 | tf_op jit(solution)/shard_map/ppermute | solution.py:41
  61.1 15.9 %collective-permute-start.20 = (bf16[4,528,256]{2,1,0:T(8,128)(2,1)}, bf16[4,528,256]{2,1,0:T(8,128)(2,1)S(1)}, u32[]{:S(2)}, u32[]{:S(2)}) collective-permute-start(bf16[4,528,256]{2,1,0:T(8,128)(2,1)} %collective-permute-done.18.refs_14_), channel_id=1, source_target_pairs={{0,16},{16,0},{32,48},{48,32},{64,80},{80,64},{96,112},{112,96},{1... | collective-permute-start | bytes 3244040 | tf_op jit(solution)/shard_map/ppermute | solution.py:45
  61.1 15.9 %collective-permute-start.21 = (bf16[4,528,256]{2,1,0:T(8,128)(2,1)S(1)}, bf16[4,528,256]{2,1,0:T(8,128)(2,1)S(1)}, u32[]{:S(2)}, u32[]{:S(2)}) collective-permute-start(bf16[4,528,256]{2,1,0:T(8,128)(2,1)S(1)} %collective-permute-done.19.refs_15_), channel_id=1, source_target_pairs={{0,16},{16,0},{32,48},{48,32},{64,80},{80,64},{96,112},{112,96},{1... | collective-permute-start | bytes 3244040 | tf_op jit(solution)/shard_map/ppermute | solution.py:45
  76.4 2.7 %collective-permute-start.24 = (bf16[4,528,256]{2,1,0:T(8,128)(2,1)S(1)}, bf16[4,528,256]{2,1,0:T(8,128)(2,1)S(1)}, u32[]{:S(2)}, u32[]{:S(2)}) collective-permute-start(bf16[4,528,256]{2,1,0:T(8,128)(2,1)S(1)} %collective-permute-done.22.refs_18_), channel_id=1, source_target_pairs={{0,16},{16,0},{32,48},{48,32},{64,80},{80,64},{96,112},{112,96},{1... | collective-permute-start | bytes 3244040 | tf_op jit(solution)/shard_map/ppermute | solution.py:45
  76.4 4.3 %collective-permute-start.25 = (bf16[4,528,256]{2,1,0:T(8,128)(2,1)S(1)}, bf16[4,528,256]{2,1,0:T(8,128)(2,1)S(1)}, u32[]{:S(2)}, u32[]{:S(2)}) collective-permute-start(bf16[4,528,256]{2,1,0:T(8,128)(2,1)S(1)} %collective-permute-done.23.refs_19_), channel_id=1, source_target_pairs={{0,16},{16,0},{32,48},{48,32},{64,80},{80,64},{96,112},{112,96},{1... | collective-permute-start | bytes 3244040 | tf_op jit(solution)/shard_map/ppermute | solution.py:45
  (25 other events, 171.5 us)

commit v5 on v4

--- a/solution.py
+++ b/solution.py
@@ -397,7 +397,7 @@
             acc = acc + fold(tv[d] * dot(lbuf[k], f))
         return acc
 
-    curve_terms = over_terms(last_step, zero, 2 * UNROLL)
+    curve_terms = over_terms(last_step, zero, 4 * UNROLL)
     curve = (curve_diag * scale_t + 2.0 * total(curve_terms)) * scale_t
     keep, move = rotation(theta, cross * scale_t, curve)
     move = move * scale_t

time: 125 us -> 124 us (level)
  no operation moved by 1% of the time
where the time goes in v5:
time: 124 us; the launch traced here: 123 us
  Pallas kernels  65.7 us (53%)
  starting transfers between devices  28.4 us (23%)
  waiting for transfers between devices  14.3 us (12%)
  local copies, waits for them, and re-layouts  11.2 us (9%)
  other arithmetic  2.56 us (2%)
    pallas_call x1, Pallas kernels, solve(): pl.pallas_call(kernel, out_shape=jax.ShapeDtypeStruct((1, 1, BLK, BLK), F...  41.7 us
    pallas_call x2, Pallas kernels, part(): pl.pallas_call(kernel, out_shape=(env, env, jax.ShapeDtypeStruct((terms,...  16.1 us
    ppermute x10, starting transfers between devices, swap_op(): return lax.ppermute(value, ('site', 'op'), pairs)  13.9 us
    unnamed x48, local copies, waits for them, and re-layouts  10.1 us
    ppermute x3, starting transfers between devices, body(): received.append(lax.ppermute(product, 'site', pairs))  9.6 us
    ppermute x10, waiting for transfers between devices, swap_op(): return lax.ppermute(value, ('site', 'op'), pairs)  8.36 us
    ppermute x13, starting transfers between devices, swap_core(): return lax.ppermute(value, 'site', [(i, i ^ 1) for i in range(8)])  4.85 us
    pallas_call x1, Pallas kernels, chain_products(): pl.pallas_call(chain_kernel, out_shape=(out, out), in_specs=[SMEM] + [VME...  4.74 us
  transfers between devices with their start and end apart: 26, of which 8 were waited for; matrix products, arithmetic and copies ran while one was open for 2% of the time, Pallas kernels for 20%

profile of v5, /device:TPU:0, one launch (start us, length us, event | category | flops | bytes accessed | tf_op | source)
XLA Modules:
  0.0 122.5 jit_solution(7840213958279531023)
XLA Ops:
  2.0 1.7 %collective-permute-start.2 = (bf16[1,528,256]{2,1,0:T(8,128)(2,1)S(1)}, bf16[1,528,256]{2,1,0:T(8,128)(2,1)S(1)}, u32[]{:S(2)}, u32[]{:S(2)}) collective-permute-start(bf16[1,528,256]{2,1,0:T(8,128)(2,1)S(1)} %get-tuple-element.56), channel_id=1, source_target_pairs={{0,4},{1,5},{2,6},{3,7},{4,0},{5,1},{6,2},{7,3},{8,12},{9,13},{10,... | collective-permute-start | bytes 811016 | tf_op jit(solution)/shard_map/ppermute | solution.py:41
  4.5 1.9 %collective-permute-start.3 = (bf16[1,528,256]{2,1,0:T(8,128)(2,1)S(1)}, bf16[1,528,256]{2,1,0:T(8,128)(2,1)S(1)}, u32[]{:S(2)}, u32[]{:S(2)}) collective-permute-start(bf16[1,528,256]{2,1,0:T(8,128)(2,1)S(1)} %get-tuple-element.55), channel_id=1, source_target_pairs={{0,1},{1,0},{2,3},{3,2},{4,5},{5,4},{6,7},{7,6},{8,9},{9,8},{10,11... | collective-permute-start | bytes 811016 | tf_op jit(solution)/shard_map/ppermute | solution.py:41
  8.5 2.3 %shard_map.82 = f32[256,256]{1,0:T(8,128)} custom-call(s32[2]{0:T(128)} %pad_add_fusion.site_ref.refs_0_, f32[256,256]{1,0:T(8,128)} %bitcast.8, f32[256,256]{1,0:T(8,128)} %bitcast.10, f32[256,256]{1,0:T(8,128)} %copy-done.12, f32[256,256]{1,0:T(8,128)} %copy-done.13), custom_call_target="tpu_custom_call" | custom-call | flops 1 | bytes 1 | tf_op jit(solution)/shard_map/pallas_call | solution.py:79
  11.1 2.0 %collective-permute-start.7 = (bf16[2,528,256]{2,1,0:T(8,128)(2,1)S(1)}, bf16[2,528,256]{2,1,0:T(8,128)(2,1)S(1)}, u32[]{:S(2)}, u32[]{:S(2)}) collective-permute-start(bf16[2,528,256]{2,1,0:T(8,128)(2,1)S(1)} %pad_maximum_fusion), channel_id=1, source_target_pairs={{0,1},{1,0},{2,3},{3,2},{4,5},{5,4},{6,7},{7,6},{8,9},{9,8},{10,11... | collective-permute-start | bytes 1622024 | tf_op jit(solution)/shard_map/ppermute | solution.py:41
  13.1 1.7 %collective-permute-start.8 = (bf16[2,528,256]{2,1,0:T(8,128)(2,1)S(1)}, bf16[2,528,256]{2,1,0:T(8,128)(2,1)S(1)}, u32[]{:S(2)}, u32[]{:S(2)}) collective-permute-start(bf16[2,528,256]{2,1,0:T(8,128)(2,1)S(1)} %pad_maximum_fusion.1), channel_id=1, source_target_pairs={{0,12},{1,13},{2,14},{3,15},{4,8},{5,9},{6,10},{7,11},{8,4},{9,5},... | collective-permute-start | bytes 1622024 | tf_op jit(solution)/shard_map/ppermute | solution.py:41
  14.8 3.5 %collective-permute-start.4 = (f32[256,256]{1,0:T(8,128)S(1)}, f32[256,256]{1,0:T(8,128)S(1)}, u32[]{:S(2)}, u32[]{:S(2)}) collective-permute-start(f32[256,256]{1,0:T(8,128)S(1)} %copy-done.19), channel_id=1, source_target_pairs={{0,32},{32,64},{64,96},{48,16},{80,48},{112,80},{1,33},{33,65},{65... | collective-permute-start | bytes 786440 | tf_op jit(solution)/shard_map/ppermute | solution.py:511
  18.3 4.8 %collective-permute-start.5 = (f32[256,256]{1,0:T(8,128)S(1)}, f32[256,256]{1,0:T(8,128)S(1)}, u32[]{:S(2)}, u32[]{:S(2)}) collective-permute-start(f32[256,256]{1,0:T(8,128)S(1)} %copy-done.19), channel_id=1, source_target_pairs={{0,64},{32,96},{80,16},{112,48},{1,65},{33,97},{81,17},{113,49},{2... | collective-permute-start | bytes 786440 | tf_op jit(solution)/shard_map/ppermute | solution.py:511
  23.1 1.3 %collective-permute-start.6 = (f32[256,256]{1,0:T(8,128)S(1)}, f32[256,256]{1,0:T(8,128)S(1)}, u32[]{:S(2)}, u32[]{:S(2)}) collective-permute-start(f32[256,256]{1,0:T(8,128)S(1)} %copy-done.19), channel_id=1, source_target_pairs={{0,96},{112,16},{1,97},{113,17},{2,98},{114,18},{3,99},{115,19},{4... | collective-permute-start | bytes 786440 | tf_op jit(solution)/shard_map/ppermute | solution.py:511
  26.9 1.3 %collective-permute-done.6.m3 = f32[256,256]{1,0:T(8,128)S(1)} collective-permute-done((f32[256,256]{1,0:T(8,128)S(1)}, f32[256,256]{1,0:T(8,128)S(1)}, u32[]{:S(2)}, u32[]{:S(2)}) %collective-permute-start.6) | collective-permute-done | bytes 262176 | tf_op jit(solution)/shard_map/ppermute | solution.py:511
  28.2 1.3 %collective-permute-start.9 = (f32[256,256]{1,0:T(8,128)S(1)}, f32[256,256]{1,0:T(8,128)S(1)}, u32[]{:S(2)}, u32[]{:S(2)}) collective-permute-start(f32[256,256]{1,0:T(8,128)S(1)} %collective-permute-done.4.m1), channel_id=1, source_target_pairs={{0,16},{16,0},{32,48},{48,32},{64,80},{80,64},{96,112},{112,96},{1... | collective-permute-start | bytes 786440 | tf_op jit(solution)/shard_map/ppermute | solution.py:45
  30.7 2.3 %collective-permute-start.14 = (bf16[4,528,256]{2,1,0:T(8,128)(2,1)}, bf16[4,528,256]{2,1,0:T(8,128)(2,1)}, u32[]{:S(2)}, u32[]{:S(2)}) collective-permute-start(bf16[4,528,256]{2,1,0:T(8,128)(2,1)} %constant_dynamic-update-slice_fusion.refs_3_), channel_id=1, source_target_pairs={{0,12},{1,13},{2,14},{3,15},{4,8},{5,9},{6,10},{7,11},{8,4},{9,5},... | collective-permute-start | bytes 3244040 | tf_op jit(solution)/shard_map/ppermute | solution.py:41
  33.9 2.5 %collective-permute-start.18 = (bf16[4,528,256]{2,1,0:T(8,128)(2,1)}, bf16[4,528,256]{2,1,0:T(8,128)(2,1)}, u32[]{:S(2)}, u32[]{:S(2)}) collective-permute-start(bf16[4,528,256]{2,1,0:T(8,128)(2,1)} %constant_dynamic-update-slice_fusion.refs_3_), channel_id=1, source_target_pairs={{0,3},{1,2},{2,1},{3,0},{4,7},{5,6},{6,5},{7,4},{8,11},{9,10},{10,... | collective-permute-start | bytes 3244040 | tf_op jit(solution)/shard_map/ppermute | solution.py:41
  37.2 4.7 %shard_map.83 = (bf16[256,256]{1,0:T(8,128)(2,1)}, bf16[256,256]{1,0:T(8,128)(2,1)}) custom-call(s32[2]{0:T(128)} %pad_add_fusion.site_ref.refs_0_, f32[256,256]{1,0:T(8,128)} %copy-done.12, f32[256,256]{1,0:T(8,128)} %copy-done.13, f32[256,256]{1,0:T(8,128)} %copy-done.16, f32[256,256]{1,0:T(8,128)} %copy-done.17, f32[256,256]{1,0:T(8,128)} %copy-done.18, ...), custom_call_target="tpu_custom_call" | custom-call | flops 1 | bytes 1 | tf_op jit(solution)/shard_map/pallas_call | solution.py:111
  43.8 8.0 %shard_map.85 = (bf16[16,256,256]{2,1,0:T(8,128)(2,1)S(1)}, bf16[16,256,256]{2,1,0:T(8,128)(2,1)S(1)}, s32[16,128]{1,0:T(8,128)S(1)}, f32[16,256,256]{2,1,0:T(8,128)S(1)}) custom-call(bf16[256,256]{1,0:T(8,128)(2,1)S(1)} %copy-done.7, bf16[256,256]{1,0:T(8,128)(2,1)S(1)} %copy-done.9, bf16[16,256,256]{2,1,0:T(8,128)(2,1)S(1)} %get-tuple-element.40.refs_2_.refs_6_, ...), custom_call_target="tpu_custom_call" | custom-call | flops 1 | bytes 1 | tf_op jit(solution)/shard_map/pallas_call | solution.py:223
  51.9 1.3 %copy-done.4 = bf16[16,256,256]{2,1,0:T(8,128)(2,1)} copy-done((bf16[16,256,256]{2,1,0:T(8,128)(2,1)}, bf16[16,256,256]{2,1,0:T(8,128)(2,1)S(1)}, u32[]{:S(2)}) %copy-start.4) | copy-done | bytes 2097176
  54.9 6.2 %collective-permute-done.18.refs_14_ = bf16[4,528,256]{2,1,0:T(8,128)(2,1)} collective-permute-done((bf16[4,528,256]{2,1,0:T(8,128)(2,1)}, bf16[4,528,256]{2,1,0:T(8,128)(2,1)}, u32[]{:S(2)}, u32[]{:S(2)}) %collective-permute-start.18) | collective-permute-done | bytes 1081376 | tf_op jit(solution)/shard_map/ppermute | solution.py:41
  61.6 8.1 %shard_map.86 = (bf16[16,256,256]{2,1,0:T(8,128)(2,1)S(1)}, bf16[16,256,256]{2,1,0:T(8,128)(2,1)S(1)}, s32[16,128]{1,0:T(8,128)S(1)}, f32[16,256,256]{2,1,0:T(8,128)S(1)}) custom-call(bf16[256,256]{1,0:T(8,128)(2,1)S(1)} %copy-done.7, bf16[256,256]{1,0:T(8,128)(2,1)S(1)} %copy-done.9, bf16[16,256,256]{2,1,0:T(8,128)(2,1)S(1)} %get-tuple-element.40.refs_2_.refs_6_, ...), custom_call_target="tpu_custom_call" | custom-call | flops 1 | bytes 1 | tf_op jit(solution)/shard_map/pallas_call | solution.py:223
  69.7 2.0 %copy-done.2 = f32[16,256,256]{2,1,0:T(8,128)} copy-done((f32[16,256,256]{2,1,0:T(8,128)}, f32[16,256,256]{2,1,0:T(8,128)S(1)}, u32[]{:S(2)}) %copy-start.2) | copy-done | bytes 4194328
  71.7 1.4 %copy-done.5 = bf16[16,256,256]{2,1,0:T(8,128)(2,1)} copy-done((bf16[16,256,256]{2,1,0:T(8,128)(2,1)}, bf16[16,256,256]{2,1,0:T(8,128)(2,1)S(1)}, u32[]{:S(2)}) %copy-start.5) | copy-done | bytes 2097176
  73.1 1.3 %copy-done.6 = bf16[16,256,256]{2,1,0:T(8,128)(2,1)} copy-done((bf16[16,256,256]{2,1,0:T(8,128)(2,1)}, bf16[16,256,256]{2,1,0:T(8,128)(2,1)S(1)}, u32[]{:S(2)}) %copy-start.6) | copy-done | bytes 2097176
  74.4 2.0 %collective-permute-done.23.refs_19_ = bf16[4,528,256]{2,1,0:T(8,128)(2,1)S(1)} collective-permute-done((bf16[4,528,256]{2,1,0:T(8,128)(2,1)}, bf16[4,528,256]{2,1,0:T(8,128)(2,1)S(1)}, u32[]{:S(2)}, u32[]{:S(2)}) %collective-permute-start.23) | collective-permute-done | bytes 1081376 | tf_op jit(solution)/shard_map/ppermute | solution.py:41
  76.9 2.2 %collective-permute-done.24.refs_20_ = bf16[4,528,256]{2,1,0:T(8,128)(2,1)S(1)} collective-permute-done((bf16[4,528,256]{2,1,0:T(8,128)(2,1)S(1)}, bf16[4,528,256]{2,1,0:T(8,128)(2,1)S(1)}, u32[]{:S(2)}, u32[]{:S(2)}) %collective-permute-start.24) | collective-permute-done | bytes 1081376 | tf_op jit(solution)/shard_map/ppermute | solution.py:45
  79.1 1.5 %collective-permute-done.25.refs_21_ = bf16[4,528,256]{2,1,0:T(8,128)(2,1)S(1)} collective-permute-done((bf16[4,528,256]{2,1,0:T(8,128)(2,1)S(1)}, bf16[4,528,256]{2,1,0:T(8,128)(2,1)S(1)}, u32[]{:S(2)}, u32[]{:S(2)}) %collective-permute-start.25) | collective-permute-done | bytes 1081376 | tf_op jit(solution)/shard_map/ppermute | solution.py:45
  80.7 41.7 %shard_map.87 = f32[1,1,256,256]{3,2,1,0:T(8,128)} custom-call(s32[2]{0:T(128)S(1)} %copy-done.11, bf16[256,256]{1,0:T(8,128)(2,1)S(1)} %copy-done.8, bf16[256,256]{1,0:T(8,128)(2,1)S(1)} %copy-done.10, f32[8,128]{1,0:T(8,128)S(1)} %get-tuple-element.39.refs_3_, bf16[1,16,256,256]{3,2,1,0:T(8,128)(2,1)} %refs_4_, f32[1,16,256,256]{3,2,1,0:T(8,128)} %refs_5_.1, ...), custom_call_target="tpu_custom_call" | custom-call | flops 1 | bytes 1 | tf_op jit(solution)/shard_map/pallas_call | solution.py:415
  (92 shorter events, 15.0 us)
Async XLA Ops:
  2.0 8.8 %collective-permute-start.2 = (bf16[1,528,256]{2,1,0:T(8,128)(2,1)S(1)}, bf16[1,528,256]{2,1,0:T(8,128)(2,1)S(1)}, u32[]{:S(2)}, u32[]{:S(2)}) collective-permute-start(bf16[1,528,256]{2,1,0:T(8,128)(2,1)S(1)} %get-tuple-element.56), channel_id=1, source_target_pairs={{0,4},{1,5},{2,6},{3,7},{4,0},{5,1},{6,2},{7,3},{8,12},{9,13},{10,... | collective-permute-start | bytes 811016 | tf_op jit(solution)/shard_map/ppermute | solution.py:41
  3.6 3.5 %collective-permute-start = (f32[256,256]{1,0:T(8,128)S(1)}, f32[256,256]{1,0:T(8,128)S(1)}, u32[]{:S(2)}, u32[]{:S(2)}) collective-permute-start(f32[256,256]{1,0:T(8,128)S(1)} %bitcast.9), channel_id=1, source_target_pairs={{0,16},{16,0},{32,48},{48,32},{64,80},{80,64},{96,112},{112,96},{1... | collective-permute-start | bytes 786440 | tf_op jit(solution)/shard_map/ppermute | solution.py:45
  4.5 6.5 %collective-permute-start.3 = (bf16[1,528,256]{2,1,0:T(8,128)(2,1)S(1)}, bf16[1,528,256]{2,1,0:T(8,128)(2,1)S(1)}, u32[]{:S(2)}, u32[]{:S(2)}) collective-permute-start(bf16[1,528,256]{2,1,0:T(8,128)(2,1)S(1)} %get-tuple-element.55), channel_id=1, source_target_pairs={{0,1},{1,0},{2,3},{3,2},{4,5},{5,4},{6,7},{7,6},{8,9},{9,8},{10,11... | collective-permute-start | bytes 811016 | tf_op jit(solution)/shard_map/ppermute | solution.py:41
  11.1 14.2 %collective-permute-start.7 = (bf16[2,528,256]{2,1,0:T(8,128)(2,1)S(1)}, bf16[2,528,256]{2,1,0:T(8,128)(2,1)S(1)}, u32[]{:S(2)}, u32[]{:S(2)}) collective-permute-start(bf16[2,528,256]{2,1,0:T(8,128)(2,1)S(1)} %pad_maximum_fusion), channel_id=1, source_target_pairs={{0,1},{1,0},{2,3},{3,2},{4,5},{5,4},{6,7},{7,6},{8,9},{9,8},{10,11... | collective-permute-start | bytes 1622024 | tf_op jit(solution)/shard_map/ppermute | solution.py:41
  13.1 13.1 %collective-permute-start.8 = (bf16[2,528,256]{2,1,0:T(8,128)(2,1)S(1)}, bf16[2,528,256]{2,1,0:T(8,128)(2,1)S(1)}, u32[]{:S(2)}, u32[]{:S(2)}) collective-permute-start(bf16[2,528,256]{2,1,0:T(8,128)(2,1)S(1)} %pad_maximum_fusion.1), channel_id=1, source_target_pairs={{0,12},{1,13},{2,14},{3,15},{4,8},{5,9},{6,10},{7,11},{8,4},{9,5},... | collective-permute-start | bytes 1622024 | tf_op jit(solution)/shard_map/ppermute | solution.py:41
  14.8 11.4 %collective-permute-start.4 = (f32[256,256]{1,0:T(8,128)S(1)}, f32[256,256]{1,0:T(8,128)S(1)}, u32[]{:S(2)}, u32[]{:S(2)}) collective-permute-start(f32[256,256]{1,0:T(8,128)S(1)} %copy-done.19), channel_id=1, source_target_pairs={{0,32},{32,64},{64,96},{48,16},{80,48},{112,80},{1,33},{33,65},{65... | collective-permute-start | bytes 786440 | tf_op jit(solution)/shard_map/ppermute | solution.py:511
  18.3 8.7 %collective-permute-start.5 = (f32[256,256]{1,0:T(8,128)S(1)}, f32[256,256]{1,0:T(8,128)S(1)}, u32[]{:S(2)}, u32[]{:S(2)}) collective-permute-start(f32[256,256]{1,0:T(8,128)S(1)} %copy-done.19), channel_id=1, source_target_pairs={{0,64},{32,96},{80,16},{112,48},{1,65},{33,97},{81,17},{113,49},{2... | collective-permute-start | bytes 786440 | tf_op jit(solution)/shard_map/ppermute | solution.py:511
  23.1 5.2 %collective-permute-start.6 = (f32[256,256]{1,0:T(8,128)S(1)}, f32[256,256]{1,0:T(8,128)S(1)}, u32[]{:S(2)}, u32[]{:S(2)}) collective-permute-start(f32[256,256]{1,0:T(8,128)S(1)} %copy-done.19), channel_id=1, source_target_pairs={{0,96},{112,16},{1,97},{113,17},{2,98},{114,18},{3,99},{115,19},{4... | collective-permute-start | bytes 786440 | tf_op jit(solution)/shard_map/ppermute | solution.py:511
  29.6 3.4 %collective-permute-start.10 = (f32[256,256]{1,0:T(8,128)S(1)}, f32[256,256]{1,0:T(8,128)S(1)}, u32[]{:S(2)}, u32[]{:S(2)}) collective-permute-start(f32[256,256]{1,0:T(8,128)S(1)} %collective-permute-done.5.m2), channel_id=1, source_target_pairs={{0,16},{16,0},{32,48},{48,32},{64,80},{80,64},{96,112},{112,96},{1... | collective-permute-start | bytes 786440 | tf_op jit(solution)/shard_map/ppermute | solution.py:45
  29.6 4.3 %collective-permute-start.11 = (f32[256,256]{1,0:T(8,128)S(1)}, f32[256,256]{1,0:T(8,128)S(1)}, u32[]{:S(2)}, u32[]{:S(2)}) collective-permute-start(f32[256,256]{1,0:T(8,128)S(1)} %collective-permute-done.6.m3), channel_id=1, source_target_pairs={{0,16},{16,0},{32,48},{48,32},{64,80},{80,64},{96,112},{112,96},{1... | collective-permute-start | bytes 786440 | tf_op jit(solution)/shard_map/ppermute | solution.py:45
  30.1 11.9 %collective-permute-start.12 = (bf16[4,528,256]{2,1,0:T(8,128)(2,1)}, bf16[4,528,256]{2,1,0:T(8,128)(2,1)}, u32[]{:S(2)}, u32[]{:S(2)}) collective-permute-start(bf16[4,528,256]{2,1,0:T(8,128)(2,1)} %constant_dynamic-update-slice_fusion.refs_3_), channel_id=1, source_target_pairs={{0,16},{16,0},{32,48},{48,32},{64,80},{80,64},{96,112},{112,96},{1... | collective-permute-start | bytes 3244040 | tf_op jit(solution)/shard_map/ppermute | solution.py:45
  30.1 11.9 %collective-permute-start.13 = (bf16[4,528,256]{2,1,0:T(8,128)(2,1)S(1)}, bf16[4,528,256]{2,1,0:T(8,128)(2,1)}, u32[]{:S(2)}, u32[]{:S(2)}) collective-permute-start(bf16[4,528,256]{2,1,0:T(8,128)(2,1)S(1)} %constant_dynamic-update-slice_fusion.2.refs_4_), channel_id=1, source_target_pairs={{0,16},{16,0},{32,48},{48,32},{64,80},{80,64},{96,112},{112,96},{1... | collective-permute-start | bytes 3244040 | tf_op jit(solution)/shard_map/ppermute | solution.py:45
  30.7 22.5 %collective-permute-start.14 = (bf16[4,528,256]{2,1,0:T(8,128)(2,1)}, bf16[4,528,256]{2,1,0:T(8,128)(2,1)}, u32[]{:S(2)}, u32[]{:S(2)}) collective-permute-start(bf16[4,528,256]{2,1,0:T(8,128)(2,1)} %constant_dynamic-update-slice_fusion.refs_3_), channel_id=1, source_target_pairs={{0,12},{1,13},{2,14},{3,15},{4,8},{5,9},{6,10},{7,11},{8,4},{9,5},... | collective-permute-start | bytes 3244040 | tf_op jit(solution)/shard_map/ppermute | solution.py:41
  33.0 20.2 %collective-permute-start.15 = (bf16[4,528,256]{2,1,0:T(8,128)(2,1)S(1)}, bf16[4,528,256]{2,1,0:T(8,128)(2,1)}, u32[]{:S(2)}, u32[]{:S(2)}) collective-permute-start(bf16[4,528,256]{2,1,0:T(8,128)(2,1)S(1)} %constant_dynamic-update-slice_fusion.2.refs_4_), channel_id=1, source_target_pairs={{0,3},{1,2},{2,1},{3,0},{4,7},{5,6},{6,5},{7,4},{8,11},{9,10},{10,... | collective-permute-start | bytes 3244040 | tf_op jit(solution)/shard_map/ppermute | solution.py:41
  33.9 27.2 %collective-permute-start.18 = (bf16[4,528,256]{2,1,0:T(8,128)(2,1)}, bf16[4,528,256]{2,1,0:T(8,128)(2,1)}, u32[]{:S(2)}, u32[]{:S(2)}) collective-permute-start(bf16[4,528,256]{2,1,0:T(8,128)(2,1)} %constant_dynamic-update-slice_fusion.refs_3_), channel_id=1, source_target_pairs={{0,3},{1,2},{2,1},{3,0},{4,7},{5,6},{6,5},{7,4},{8,11},{9,10},{10,... | collective-permute-start | bytes 3244040 | tf_op jit(solution)/shard_map/ppermute | solution.py:41
  42.0 19.1 %collective-permute-start.19 = (bf16[4,528,256]{2,1,0:T(8,128)(2,1)S(1)}, bf16[4,528,256]{2,1,0:T(8,128)(2,1)S(1)}, u32[]{:S(2)}, u32[]{:S(2)}) collective-permute-start(bf16[4,528,256]{2,1,0:T(8,128)(2,1)S(1)} %constant_dynamic-update-slice_fusion.2.refs_4_), channel_id=1, source_target_pairs={{0,4},{1,5},{2,6},{3,7},{4,0},{5,1},{6,2},{7,3},{8,12},{9,13},{10,... | collective-permute-start | bytes 3244040 | tf_op jit(solution)/shard_map/ppermute | solution.py:41
  53.2 7.9 %collective-permute-start.16 = (bf16[4,528,256]{2,1,0:T(8,128)(2,1)}, bf16[4,528,256]{2,1,0:T(8,128)(2,1)S(1)}, u32[]{:S(2)}, u32[]{:S(2)}) collective-permute-start(bf16[4,528,256]{2,1,0:T(8,128)(2,1)} %collective-permute-done.14.refs_4_), channel_id=1, source_target_pairs={{0,16},{16,0},{32,48},{48,32},{64,80},{80,64},{96,112},{112,96},{1... | collective-permute-start | bytes 3244040 | tf_op jit(solution)/shard_map/ppermute | solution.py:45
  53.3 8.3 %collective-permute-start.17 = (bf16[4,528,256]{2,1,0:T(8,128)(2,1)}, bf16[4,528,256]{2,1,0:T(8,128)(2,1)S(1)}, u32[]{:S(2)}, u32[]{:S(2)}) collective-permute-start(bf16[4,528,256]{2,1,0:T(8,128)(2,1)} %collective-permute-done.15.refs_5_), channel_id=1, source_target_pairs={{0,16},{16,0},{32,48},{48,32},{64,80},{80,64},{96,112},{112,96},{1... | collective-permute-start | bytes 3244040 | tf_op jit(solution)/shard_map/ppermute | solution.py:45
  53.8 20.6 %collective-permute-start.22 = (bf16[4,528,256]{2,1,0:T(8,128)(2,1)}, bf16[4,528,256]{2,1,0:T(8,128)(2,1)S(1)}, u32[]{:S(2)}, u32[]{:S(2)}) collective-permute-start(bf16[4,528,256]{2,1,0:T(8,128)(2,1)} %collective-permute-done.14.refs_4_), channel_id=1, source_target_pairs={{0,3},{1,2},{2,1},{3,0},{4,7},{5,6},{6,5},{7,4},{8,11},{9,10},{10,... | collective-permute-start | bytes 3244040 | tf_op jit(solution)/shard_map/ppermute | solution.py:41
  61.1 15.4 %collective-permute-start.23 = (bf16[4,528,256]{2,1,0:T(8,128)(2,1)}, bf16[4,528,256]{2,1,0:T(8,128)(2,1)S(1)}, u32[]{:S(2)}, u32[]{:S(2)}) collective-permute-start(bf16[4,528,256]{2,1,0:T(8,128)(2,1)} %collective-permute-done.15.refs_5_), channel_id=1, source_target_pairs={{0,4},{1,5},{2,6},{3,7},{4,0},{5,1},{6,2},{7,3},{8,12},{9,13},{10,... | collective-permute-start | bytes 3244040 | tf_op jit(solution)/shard_map/ppermute | solution.py:41
  61.1 15.9 %collective-permute-start.20 = (bf16[4,528,256]{2,1,0:T(8,128)(2,1)}, bf16[4,528,256]{2,1,0:T(8,128)(2,1)S(1)}, u32[]{:S(2)}, u32[]{:S(2)}) collective-permute-start(bf16[4,528,256]{2,1,0:T(8,128)(2,1)} %collective-permute-done.18.refs_14_), channel_id=1, source_target_pairs={{0,16},{16,0},{32,48},{48,32},{64,80},{80,64},{96,112},{112,96},{1... | collective-permute-start | bytes 3244040 | tf_op jit(solution)/shard_map/ppermute | solution.py:45
  61.1 15.9 %collective-permute-start.21 = (bf16[4,528,256]{2,1,0:T(8,128)(2,1)S(1)}, bf16[4,528,256]{2,1,0:T(8,128)(2,1)S(1)}, u32[]{:S(2)}, u32[]{:S(2)}) collective-permute-start(bf16[4,528,256]{2,1,0:T(8,128)(2,1)S(1)} %collective-permute-done.19.refs_15_), channel_id=1, source_target_pairs={{0,16},{16,0},{32,48},{48,32},{64,80},{80,64},{96,112},{112,96},{1... | collective-permute-start | bytes 3244040 | tf_op jit(solution)/shard_map/ppermute | solution.py:45
  76.4 2.7 %collective-permute-start.24 = (bf16[4,528,256]{2,1,0:T(8,128)(2,1)S(1)}, bf16[4,528,256]{2,1,0:T(8,128)(2,1)S(1)}, u32[]{:S(2)}, u32[]{:S(2)}) collective-permute-start(bf16[4,528,256]{2,1,0:T(8,128)(2,1)S(1)} %collective-permute-done.22.refs_18_), channel_id=1, source_target_pairs={{0,16},{16,0},{32,48},{48,32},{64,80},{80,64},{96,112},{112,96},{1... | collective-permute-start | bytes 3244040 | tf_op jit(solution)/shard_map/ppermute | solution.py:45
  76.4 4.3 %collective-permute-start.25 = (bf16[4,528,256]{2,1,0:T(8,128)(2,1)S(1)}, bf16[4,528,256]{2,1,0:T(8,128)(2,1)S(1)}, u32[]{:S(2)}, u32[]{:S(2)}) collective-permute-start(bf16[4,528,256]{2,1,0:T(8,128)(2,1)S(1)} %collective-permute-done.23.refs_19_), channel_id=1, source_target_pairs={{0,16},{16,0},{32,48},{48,32},{64,80},{80,64},{96,112},{112,96},{1... | collective-permute-start | bytes 3244040 | tf_op jit(solution)/shard_map/ppermute | solution.py:45
  (25 other events, 171.5 us)
